TPU v7x, 128 devices: a whole 4x4x4 slice. The times are simulated.
128 devices in a mesh: chan: 8 (over y, x_hi), space: 16 (over z, x_lo, core).
Axes of the slice: x: 4 (x_hi: 2, x_lo: 2; x = x_hi * 2 + x_lo), y: 4, z: 4, core: 2. Of those that a mesh axis runs over, the one named last changes fastest.
Arguments:
- volume: bfloat16 [64, 16, 256, 128], P('space', None, 'chan'), may hold values from -6 to 6
- kernel: bfloat16 [27, 256, 256], P(None, 'chan'), may hold values from -0.078125 to 0.078125
- bias: float32 [256], P('chan'), may hold values from -3 to 3
- cotangent: bfloat16 [64, 16, 256, 128], P('space', None, 'chan'), may hold values from -6 to 6
Outputs:
- output: bfloat16 [64, 16, 256, 128], P('space', None, 'chan')
- input_grad: bfloat16 [64, 16, 256, 128], P('space', None, 'chan')
- weight_grad: float32 [27, 256, 256], P(None, 'chan')
All inputs are finite; a program needn't handle non-finite values.
Results may differ from a plain program's by a relative error of at most 0.0049.
Values may be sent and summed in bfloat16 or wider, within the bound.
No kernel may reach another device: no remote copies, remote signals or barrier semaphores. Data moves between devices by JAX's collectives and lax.ppermute only.
A program may use at most 128 MiB of HBM per device.

v0:
```python
import functools
import math

import jax
import jax.numpy as jnp
from jax import lax
from jax.experimental import pallas as pl
from jax.experimental.pallas import tpu as pltpu
from jax.sharding import PartitionSpec as P

BF16 = jnp.bfloat16
F32 = jnp.float32
VMEM_LIMIT = 44 * 1024 * 1024


def moved(value, step):
    if step == 0:
        return value
    size = value.shape[-1]
    lane = lax.broadcasted_iota(jnp.int32, value.shape, value.ndim - 1)
    rolled = pltpu.roll(value, step % size, value.ndim - 1)
    edge = 0 if step == 1 else size - 1
    return jnp.where(lane == edge, 0.0, rolled)


def pair_of(ref, plane, row):
    return jnp.concatenate([ref[plane, row], ref[plane, row + 1]], axis=1)


def forward_body(at, own, left, right, far_lo, far_hi, kernel, bias, cot_own, cot_other,
                 out_own, out_other, grad, field):
    here_y, half = at[0], at[1]
    planes, rows = own.shape[0], own.shape[1]
    lines = own.shape[2]
    split = far_lo.shape[0]

    def fill(plane, carry):
        field[plane, 9 * half] = jnp.zeros(field.shape[2:], BF16)
        for row in range(rows):
            for shift, ref in ((0, own), (3, left), (1, right)):
                start = pl.multiple_of(lax.rem(here_y + shift, 4) * lines, lines)
                field[plane, row + 1 - half, pl.ds(start, lines), :] = ref[plane, row]
        return carry

    lax.fori_loop(0, planes, fill, 0)
    start = pl.multiple_of(lax.rem(here_y + 2, 4) * lines, lines)

    def fill_far(plane, carry):
        for row in range(rows):
            field[plane, row + 1 - half, pl.ds(start, lines), :] = far_lo[plane, row]
            field[plane + split, row + 1 - half, pl.ds(start, lines), :] = far_hi[plane, row]
        return carry

    lax.fori_loop(0, split, fill_far, 0)
    outs = kernel.shape[1] // 3
    half_outs = outs // 2

    def step(index, carry):
        plane, row = index // 4, 2 * lax.rem(index, 4)
        total = jnp.zeros((3 * outs, 256), F32)
        for a in range(3):
            for b in range(3):
                total = total + jnp.dot(
                    kernel[3 * a + b], pair_of(field, plane + a, row + b),
                    preferred_element_type=F32,
                )
        for r in range(2):
            part = total[:, 128 * r : 128 * r + 128]
            pre = (
                moved(part[:outs], 1) + part[outs : 2 * outs] + moved(part[2 * outs :], -1)
                + bias[...]
            )
            sig = 1.0 / (1.0 + jnp.exp(-pre))
            out = (pre * sig).astype(BF16)
            out_own[plane, row + r] = out[:half_outs]
            out_other[plane, row + r] = out[half_outs:]
            cot = jnp.concatenate(
                [cot_own[plane, row + r], cot_other[plane, row + r]], axis=0
            ).astype(F32)
            grad[plane, row + r] = (cot * sig * (1.0 + pre * (1.0 - sig))).astype(BF16)
        return carry

    lax.fori_loop(0, 16, step, 0)


def spread(line):
    wide = line.astype(F32)
    return [moved(wide, c - 1).astype(BF16) for c in range(3)]


def weight_body(at, field, grad, sums, stacked):
    core = at[2]
    planes, rows, outs = grad.shape[0], grad.shape[1], grad.shape[2]

    def fill(plane, carry):
        for row in range(rows):
            for c, line in enumerate(spread(grad[plane, row])):
                stacked[plane, row, outs * c : outs * (c + 1), :] = line
        return carry

    lax.fori_loop(0, planes, fill, 0)

    def step(tap, carry):
        a, b = tap // 3, lax.rem(tap, 3)
        total = jnp.zeros((3 * outs, 256), F32)
        for plane in range(planes):
            grads = jnp.concatenate([stacked[plane, row] for row in range(rows)], axis=1)
            cells = jnp.concatenate([field[plane + a, row + b] for row in range(rows)], axis=1)
            total = total + lax.dot_general(
                grads, cells, (((1,), (1,)), ((), ())), preferred_element_type=F32
            )
        for c in range(3):
            for side in range(2):
                for part in range(2):
                    low = outs * c + 32 * side + 16 * part
                    sums[part ^ core, side, 3 * tap + c] = total[low : low + 16]
        return carry

    lax.fori_loop(0, 9, step, 0)


def input_body(at, grad, edge, low, high, turned, own, parts, stacked, held):
    here_y, half = at[0], at[1]
    planes, rows, outs = grad.shape[0], grad.shape[1], grad.shape[2]

    def put(plane, row, line):
        for c, value in enumerate(spread(line)):
            stacked[plane, row, outs * c : outs * (c + 1), :] = value

    beside = 9 * (1 - half)

    def fill(plane, carry):
        for row in range(rows):
            put(plane + 1, row + 1, grad[plane, row])
        put(plane + 1, beside, edge[plane])
        return carry

    lax.fori_loop(0, planes, fill, 0)
    for row in range(rows):
        put(0, row + 1, low[row])
        put(planes + 1, row + 1, high[row])
    put(0, beside, low[rows])
    put(planes + 1, beside, high[rows])
    for plane in range(planes + 2):
        stacked[plane, 9 * half] = jnp.zeros(stacked.shape[2:], BF16)

    def step(index, carry):
        plane, row = index // 4, 2 * lax.rem(index, 4)
        terms = jnp.concatenate(
            [
                pair_of(stacked, plane + 2 - a, row + 2 - b)
                for a in range(3)
                for b in range(3)
            ],
            axis=0,
        )
        total = jnp.dot(turned[...], terms, preferred_element_type=F32)
        held[...] = total
        mine = held[pl.ds(pl.multiple_of(64 * here_y, 64), 64), :]
        for r in range(2):
            own[plane, row + r] = mine[:, 128 * r : 128 * r + 128]
            for j in range(4):
                parts[lax.rem(j + 4 - here_y, 4), plane, row + r] = total[
                    64 * j : 64 * j + 64, 128 * r : 128 * r + 128
                ].astype(BF16)
        return carry

    lax.fori_loop(0, 16, step, 0)


def call(body, n_in, outs, scratch, flops):
    vmem = pl.BlockSpec(memory_space=pltpu.VMEM)
    return pl.pallas_call(
        body,
        out_shape=outs,
        in_specs=[pl.BlockSpec(memory_space=pltpu.SMEM)] + [vmem] * (n_in - 1),
        out_specs=[vmem] * len(outs),
        scratch_shapes=scratch,
        compiler_params=pltpu.CompilerParams(vmem_limit_bytes=VMEM_LIMIT),
        cost_estimate=pl.CostEstimate(
            flops=flops, bytes_accessed=8 * 2**20, transcendentals=2**18
        ),
    )


def on_device(volume, kernel, bias, cotangent):
    chan, space = lax.axis_index("chan"), lax.axis_index("space")
    here_y, half, core = chan // 2, chan % 2, space % 2
    at = jnp.stack([here_y, half, core]).astype(jnp.int32)
    swap = functools.partial(
        lax.ppermute, axis_name="chan", perm=[(i, i ^ 1) for i in range(8)]
    )

    def turn(value, step):
        return lax.ppermute(value, "chan", [(i, (i + 2 * step) % 8) for i in range(8)])

    swap_core = functools.partial(
        lax.ppermute, axis_name="space", perm=[(i, i ^ 1) for i in range(16)]
    )

    def up(value):
        return lax.ppermute(value, "space", [(i, i + 1) for i in range(15)])

    def down(value):
        return lax.ppermute(value, "space", [(i + 1, i) for i in range(15)])

    below, above = up(volume[3:]), down(volume[:1])
    rimmed = jnp.concatenate([below, volume, above], axis=0)
    mine = lax.dynamic_slice_in_dim(rimmed, 7 * half, 9, axis=1)
    theirs = lax.dynamic_slice_in_dim(rimmed, 7 * (1 - half), 9, axis=1)
    got = swap(theirs)
    own = jnp.where(
        half == 0,
        jnp.concatenate([mine, got], axis=2),
        jnp.concatenate([got, mine], axis=2),
    )
    left, right = turn(own, 1), turn(own, -1)
    far_lo, far_hi = turn(left[:3], 1), turn(right[3:], -1)

    kernel_all = jnp.concatenate([kernel, swap(kernel)], axis=1)
    bias_all = jnp.concatenate([bias, swap(bias)])
    bias_wide = jnp.broadcast_to(bias_all[:, None], (64, 128))
    turned = kernel_all.reshape(27 * 64, 256).T
    cot_own = lax.dynamic_slice_in_dim(cotangent, 8 * half, 8, axis=1)
    cot_other = swap(lax.dynamic_slice_in_dim(cotangent, 8 * (1 - half), 8, axis=1))

    shape = jax.ShapeDtypeStruct
    flops = 36 * 10**8
    out_own, out_other, grad, field = call(
        forward_body, 10,
        [
            shape((4, 8, 32, 128), BF16),
            shape((4, 8, 32, 128), BF16),
            shape((4, 8, 64, 128), BF16),
            shape((6, 10, 256, 128), BF16),
        ],
        [], flops,
    )(at, own, left, right, far_lo, far_hi, kernel_all.reshape(9, 192, 256), bias_wide,
      cot_own, cot_other)

    def rows_of(first, second):
        return jnp.where(
            half == 0,
            jnp.concatenate([first, second], axis=1),
            jnp.concatenate([second, first], axis=1),
        )

    output = rows_of(out_own, swap(out_other))

    rim = lax.dynamic_index_in_dim(grad, 7 * (1 - half), axis=1, keepdims=False)
    edge = swap(jnp.concatenate([rim[:, 32:], rim[:, :32]], axis=1))
    low = up(jnp.concatenate([grad[3], edge[3:]], axis=0))
    high = down(jnp.concatenate([grad[0], edge[:1]], axis=0))

    (sums,) = call(
        weight_body, 3, [shape((2, 2, 27, 16, 256), F32)],
        [pltpu.VMEM((4, 8, 192, 128), BF16)], flops,
    )(at, field, grad)
    chip = sums[0] + swap_core(sums[1])
    pair = chip[0] + swap(chip[1])
    groups = [[2 * k + c for k in range(8)] for c in range(2)]
    pieces = lax.all_to_all(
        pair.reshape(8, 54, 256), "space", 0, 0, tiled=True, axis_index_groups=groups
    )
    whole = jnp.sum(pieces, axis=0) / math.sqrt(64 * 16 * 128)
    spread_out = lax.all_to_all(
        jnp.broadcast_to(whole[None], (8, 54, 256)), "space", 0, 0, tiled=True,
        axis_index_groups=groups,
    ).reshape(27, 16, 256)
    other = swap_core(spread_out)
    weight_grad = jnp.where(
        core == 0,
        jnp.concatenate([spread_out, other], axis=1),
        jnp.concatenate([other, spread_out], axis=1),
    )

    mine_f, parts = call(
        input_body, 6,
        [shape((4, 8, 64, 128), F32), shape((4, 4, 8, 64, 128), BF16)],
        [pltpu.VMEM((6, 10, 192, 128), BF16), pltpu.VMEM((256, 256), F32)], flops,
    )(at, grad, edge, low, high, turned)
    terms = [turn(parts[1], 1), turn(parts[3], -1), turn(parts[2], 2)]
    back = (mine_f + sum(term.astype(F32) for term in terms)).astype(BF16)
    kept = lax.dynamic_slice_in_dim(back, 32 * half, 32, axis=2)
    sent = lax.dynamic_slice_in_dim(back, 32 * (1 - half), 32, axis=2)
    input_grad = rows_of(kept, swap(sent))
    return output, input_grad, weight_grad


def solution(mesh):
    return jax.shard_map(
        on_device,
        mesh=mesh,
        in_specs=(
            P("space", None, "chan", None),
            P(None, "chan", None),
            P("chan"),
            P("space", None, "chan", None),
        ),
        out_specs=(
            P("space", None, "chan", None),
            P("space", None, "chan", None),
            P(None, "chan", None),
        ),
        check_vma=False,
    )
```

profile of v0, /device:TPU:1, one launch (start us, length us, event | category | flops | bytes accessed | tf_op | source)
XLA Modules:
  0.0 172.1 jit_solution(12913837209364182960)
XLA Ops:
  1.6 4.5 %collective-permute-start = (bf16[1,16,32,128]{3,2,1,0:T(8,128)(2,1)S(1)}, bf16[1,16,32,128]{3,2,1,0:T(8,128)(2,1)S(1)}, u32[]{:S(2)}, u32[]{:S(2)}) collective-permute-start(bf16[1,16,32,128]{3,2,1,0:T(8,128)(2,1)S(1)} %get-tuple-element.27), channel_id=1, source_target_pairs={{0,1},{1,2},{2,3},{3,4},{4,5},{5,6},{6,7},{7,8},{8,9},{9,10},{10,1... | collective-permute-start | bytes 393224 | tf_op jit(solution)/shard_map/ppermute | solution.py:202
  6.1 1.9 %collective-permute-start.1 = (bf16[1,16,32,128]{3,2,1,0:T(8,128)(2,1)S(1)}, bf16[1,16,32,128]{3,2,1,0:T(8,128)(2,1)S(1)}, u32[]{:S(2)}, u32[]{:S(2)}) collective-permute-start(bf16[1,16,32,128]{3,2,1,0:T(8,128)(2,1)S(1)} %get-tuple-element.26), channel_id=1, source_target_pairs={{1,0},{2,1},{3,2},{4,3},{5,4},{6,5},{7,6},{8,7},{9,8},{10,9},{11,1... | collective-permute-start | bytes 393224 | tf_op jit(solution)/shard_map/ppermute | solution.py:205
  9.2 3.2 %collective-permute-done.1 = bf16[1,16,32,128]{3,2,1,0:T(8,128)(2,1)S(1)} collective-permute-done((bf16[1,16,32,128]{3,2,1,0:T(8,128)(2,1)S(1)}, bf16[1,16,32,128]{3,2,1,0:T(8,128)(2,1)S(1)}, u32[]{:S(2)}, u32[]{:S(2)}) %collective-permute-start.1) | collective-permute-done | bytes 131104 | tf_op jit(solution)/shard_map/ppermute | solution.py:205
  12.6 2.5 %collective-permute-start.2 = (bf16[6,9,32,128]{3,2,1,0:T(8,128)(2,1)S(1)}, bf16[6,9,32,128]{3,2,1,0:T(8,128)(2,1)S(1)}, u32[]{:S(2)}, u32[]{:S(2)}) collective-permute-start(bf16[6,9,32,128]{3,2,1,0:T(8,128)(2,1)S(1)} %get-tuple-element.19), channel_id=1, source_target_pairs={{0,16},{16,0},{32,48},{48,32},{64,80},{80,64},{96,112},{112,96},{1... | collective-permute-start | bytes 1327112 | tf_op jit(solution)/shard_map/ppermute | solution.py:211
  15.1 8.4 %collective-permute-done.2 = bf16[6,9,32,128]{3,2,1,0:T(8,128)(2,1)S(1)} collective-permute-done((bf16[6,9,32,128]{3,2,1,0:T(8,128)(2,1)S(1)}, bf16[6,9,32,128]{3,2,1,0:T(8,128)(2,1)S(1)}, u32[]{:S(2)}, u32[]{:S(2)}) %collective-permute-start.2) | collective-permute-done | bytes 442400 | tf_op jit(solution)/shard_map/ppermute | solution.py:211
  23.8 2.8 %collective-permute-start.4 = (bf16[6,9,64,128]{3,2,1,0:T(8,128)(2,1)S(1)}, bf16[6,9,64,128]{3,2,1,0:T(8,128)(2,1)S(1)}, u32[]{:S(2)}, u32[]{:S(2)}) collective-permute-start(bf16[6,9,64,128]{3,2,1,0:T(8,128)(2,1)S(1)} %maximum_select_fusion.own), channel_id=1, source_target_pairs={{0,96},{16,112},{32,0},{48,16},{64,32},{80,48},{96,64},{112,80},{1... | collective-permute-start | bytes 2654216 | tf_op jit(solution)/shard_map/ppermute | solution.py:195
  26.6 2.5 %collective-permute-start.8 = (f32[32]{0:T(128)S(1)}, f32[32]{0:T(128)S(1)}, u32[]{:S(2)}, u32[]{:S(2)}) collective-permute-start(f32[32]{0:T(128)S(1)} %copy-done.17), channel_id=1, source_target_pairs={{0,16},{16,0},{32,48},{48,32},{64,80},{80,64},{96,112},{112,96},{1... | collective-permute-start | bytes 392 | tf_op jit(solution)/shard_map/ppermute | solution.py:221
  30.3 2.5 %collective-permute-start.9 = (bf16[4,8,32,128]{3,2,1,0:T(8,128)(2,1)}, bf16[4,8,32,128]{3,2,1,0:T(8,128)(2,1)}, u32[]{:S(2)}, u32[]{:S(2)}) collective-permute-start(bf16[4,8,32,128]{3,2,1,0:T(8,128)(2,1)} %get-tuple-element.24), channel_id=1, source_target_pairs={{0,16},{16,0},{32,48},{48,32},{64,80},{80,64},{96,112},{112,96},{1... | collective-permute-start | bytes 786440 | tf_op jit(solution)/shard_map/ppermute | solution.py:225
  32.7 11.8 %collective-permute-done.4.right = bf16[6,9,64,128]{3,2,1,0:T(8,128)(2,1)S(1)} collective-permute-done((bf16[6,9,64,128]{3,2,1,0:T(8,128)(2,1)S(1)}, bf16[6,9,64,128]{3,2,1,0:T(8,128)(2,1)S(1)}, u32[]{:S(2)}, u32[]{:S(2)}) %collective-permute-start.4) | collective-permute-done | bytes 884768 | tf_op jit(solution)/shard_map/ppermute | solution.py:195
  45.3 3.5 %collective-permute-start.6 = (bf16[3,9,64,128]{3,2,1,0:T(8,128)(2,1)}, bf16[3,9,64,128]{3,2,1,0:T(8,128)(2,1)S(1)}, u32[]{:S(2)}, u32[]{:S(2)}) collective-permute-start(bf16[3,9,64,128]{3,2,1,0:T(8,128)(2,1)} %slice.69), channel_id=1, source_target_pairs={{0,96},{16,112},{32,0},{48,16},{64,32},{80,48},{96,64},{112,80},{1... | collective-permute-start | bytes 1327112 | tf_op jit(solution)/shard_map/ppermute | solution.py:195
  51.2 7.2 %collective-permute-done.6.far_hi = bf16[3,9,64,128]{3,2,1,0:T(8,128)(2,1)S(1)} collective-permute-done((bf16[3,9,64,128]{3,2,1,0:T(8,128)(2,1)}, bf16[3,9,64,128]{3,2,1,0:T(8,128)(2,1)S(1)}, u32[]{:S(2)}, u32[]{:S(2)}) %collective-permute-start.6) | collective-permute-done | bytes 442400 | tf_op jit(solution)/shard_map/ppermute | solution.py:195
  59.1 3.7 %collective-permute-done.5.far_lo = bf16[3,9,64,128]{3,2,1,0:T(8,128)(2,1)} collective-permute-done((bf16[3,9,64,128]{3,2,1,0:T(8,128)(2,1)}, bf16[3,9,64,128]{3,2,1,0:T(8,128)(2,1)}, u32[]{:S(2)}, u32[]{:S(2)}) %collective-permute-start.5) | collective-permute-done | bytes 442400 | tf_op jit(solution)/shard_map/ppermute | solution.py:195
  65.1 9.7 %shard_map.67 = (bf16[4,8,32,128]{3,2,1,0:T(8,128)(2,1)S(1)}, bf16[4,8,32,128]{3,2,1,0:T(8,128)(2,1)S(1)}, bf16[4,8,64,128]{3,2,1,0:T(8,128)(2,1)S(1)}, bf16[6,10,256,128]{3,2,1,0:T(8,128)(2,1)S(1)}) custom-call(s32[3]{0:T(128)S(1)} %pad_add_fusion.at, bf16[6,9,64,128]{3,2,1,0:T(8,128)(2,1)S(1)} %maximum_select_fusion.own, ...), custom_call_target="tpu_custom_call" | custom-call | flops 3600000000 | bytes 8388608 | tf_op jit(solution)/shard_map/pallas_call | solution.py:229
  75.5 8.7 %shard_map.69 = f32[2,2,27,16,256]{4,3,2,1,0:T(8,128)S(1)} custom-call(s32[3]{0:T(128)S(1)} %pad_add_fusion.at, bf16[6,10,256,128]{3,2,1,0:T(8,128)(2,1)S(1)} %get-tuple-element.14.field, bf16[4,8,64,128]{3,2,1,0:T(8,128)(2,1)S(1)} %get-tuple-element.11.grad), custom_call_target="tpu_custom_call" | custom-call | flops 3600000000 | bytes 8388608 | tf_op jit(solution)/shard_map/pallas_call | solution.py:255
  84.6 2.7 %collective-permute-start.11 = (bf16[4,64,128]{2,1,0:T(8,128)(2,1)S(1)}, bf16[4,64,128]{2,1,0:T(8,128)(2,1)S(1)}, u32[]{:S(2)}, u32[]{:S(2)}) collective-permute-start(bf16[4,64,128]{2,1,0:T(8,128)(2,1)S(1)} %pad_maximum_fusion.2), channel_id=1, source_target_pairs={{0,16},{16,0},{32,48},{48,32},{64,80},{80,64},{96,112},{112,96},{1... | collective-permute-start | bytes 196616 | tf_op jit(solution)/shard_map/ppermute | solution.py:251
  87.4 1.9 %collective-permute-done.11.edge = bf16[4,64,128]{2,1,0:T(8,128)(2,1)S(1)} collective-permute-done((bf16[4,64,128]{2,1,0:T(8,128)(2,1)S(1)}, bf16[4,64,128]{2,1,0:T(8,128)(2,1)S(1)}, u32[]{:S(2)}, u32[]{:S(2)}) %collective-permute-start.11) | collective-permute-done | bytes 65568 | tf_op jit(solution)/shard_map/ppermute | solution.py:251
  89.3 7.6 %collective-permute-start.12 = (bf16[9,64,128]{2,1,0:T(8,128)(2,1)S(1)}, bf16[9,64,128]{2,1,0:T(8,128)(2,1)S(1)}, u32[]{:S(2)}, u32[]{:S(2)}) collective-permute-start(bf16[9,64,128]{2,1,0:T(8,128)(2,1)S(1)} %pad_maximum_fusion), channel_id=1, source_target_pairs={{0,1},{1,2},{2,3},{3,4},{4,5},{5,6},{6,7},{7,8},{8,9},{9,10},{10,1... | collective-permute-start | bytes 442376 | tf_op jit(solution)/shard_map/ppermute | solution.py:202
  97.6 1.9 %collective-permute-start.13 = (bf16[9,64,128]{2,1,0:T(8,128)(2,1)}, bf16[9,64,128]{2,1,0:T(8,128)(2,1)S(1)}, u32[]{:S(2)}, u32[]{:S(2)}) collective-permute-start(bf16[9,64,128]{2,1,0:T(8,128)(2,1)} %pad_maximum_fusion.1), channel_id=1, source_target_pairs={{1,0},{2,1},{3,2},{4,3},{5,4},{6,5},{7,6},{8,7},{9,8},{10,9},{11,1... | collective-permute-start | bytes 442376 | tf_op jit(solution)/shard_map/ppermute | solution.py:205
  100.5 1.8 %collective-permute-start.19 = (f32[27,16,256]{2,1,0:T(8,128)}, f32[27,16,256]{2,1,0:T(8,128)}, u32[]{:S(2)}, u32[]{:S(2)}) collective-permute-start(f32[27,16,256]{2,1,0:T(8,128)} %slice_bitcast_fusion.5), channel_id=1, source_target_pairs={{0,16},{16,0},{32,48},{48,32},{64,80},{80,64},{96,112},{112,96},{1... | collective-permute-start | bytes 1327112 | tf_op jit(solution)/shard_map/ppermute | solution.py:260
  102.3 1.4 copy.8
  109.3 8.1 %shard_map.68 = (f32[4,8,64,128]{3,2,1,0:T(8,128)S(1)}, bf16[4,4,8,64,128]{4,3,2,1,0:T(8,128)(2,1)S(1)}) custom-call(s32[3]{0:T(128)S(1)} %pad_add_fusion.at, bf16[4,8,64,128]{3,2,1,0:T(8,128)(2,1)S(1)} %copy-done.4, bf16[4,64,128]{2,1,0:T(8,128)(2,1)S(1)} %collective-permute-done.11.edge, bf16[9,64,128]{2,1,0:T(8,128)(2,1)S(1)} %copy-done.10, ...), custom_call_target="tpu_custom_call" | custom-call | flops 3600000000 | bytes 8388608 | tf_op jit(solution)/shard_map/pallas_call | solution.py:277
  117.5 1.8 %fusion.1 = f32[27,16,256]{2,1,0:T(8,128)} fusion(f32[27,16,256]{2,1,0:T(8,128)} %collective-permute-done.19, f32[2,27,16,256]{3,2,1,0:T(8,128)S(1)} %copy-done.14), kind=kLoop, calls=%fused_computation.13 | loop fusion | flops 110592 | bytes 1327104 | tf_op jit(solution)/shard_map/add | solution.py:260
  119.3 1.8 %reshape.24 = f32[8,54,256]{2,1,0:T(8,128)} reshape(f32[27,16,256]{2,1,0:T(8,128)} %fusion.1) | data formatting | bytes 884736 | tf_op jit(solution)/shard_map/reshape | solution.py:263
  121.2 9.0 %all-to-all-start = ((f32[8,54,256]{2,1,0:T(8,128)}), f32[8,54,256]{2,1,0:T(8,128)}, u32[]{:S(2)}, u32[]{:S(2)}) async-start(f32[8,54,256]{2,1,0:T(8,128)} %reshape.24), calls=%async_computation | async-start | bytes 917504 | tf_op jit(solution)/shard_map/all_to_all | solution.py:262
  132.1 1.8 %collective-permute-start.15 = (bf16[4,8,64,128]{3,2,1,0:T(8,128)(2,1)}, bf16[4,8,64,128]{3,2,1,0:T(8,128)(2,1)}, u32[]{:S(2)}, u32[]{:S(2)}) collective-permute-start(bf16[4,8,64,128]{3,2,1,0:T(8,128)(2,1)} %get-tuple-element.17), channel_id=1, source_target_pairs={{0,96},{16,112},{32,0},{48,16},{64,32},{80,48},{96,64},{112,80},{1... | collective-permute-start | bytes 1572872 | tf_op jit(solution)/shard_map/ppermute | solution.py:195
  134.0 5.9 %all-to-all-done = f32[8,54,256]{2,1,0:T(8,128)} async-done(((f32[8,54,256]{2,1,0:T(8,128)}), f32[8,54,256]{2,1,0:T(8,128)}, u32[]{:S(2)}, u32[]{:S(2)}) %all-to-all-start) | async-done | bytes 442400 | tf_op jit(solution)/shard_map/all_to_all | solution.py:262
  141.7 3.5 %all-to-all-start.1 = ((f32[8,54,256]{2,1,0:T(8,128)}), f32[8,54,256]{2,1,0:T(8,128)S(1)}, u32[]{:S(2)}, u32[]{:S(2)}) async-start(f32[8,54,256]{2,1,0:T(8,128)} %broadcast_in_dim.5), calls=%async_computation.1 | async-start | bytes 917504 | tf_op jit(solution)/shard_map/all_to_all | solution.py:266
  145.2 1.7 collective-permute-start.10
  147.0 10.6 %collective-permute-done.14 = bf16[4,8,64,128]{3,2,1,0:T(8,128)(2,1)S(1)} collective-permute-done((bf16[4,8,64,128]{3,2,1,0:T(8,128)(2,1)}, bf16[4,8,64,128]{3,2,1,0:T(8,128)(2,1)S(1)}, u32[]{:S(2)}, u32[]{:S(2)}) %collective-permute-start.14) | collective-permute-done | bytes 524320 | tf_op jit(solution)/shard_map/ppermute | solution.py:195
  158.0 1.5 add_convert_fusion
  162.0 1.9 %maximum_select_fusion.2 = bf16[4,16,32,128]{3,2,1,0:T(8,128)(2,1)} fusion(bf16[4,8,32,128]{3,2,1,0:T(8,128)(2,1)} %collective-permute-done.10, bf16[4,8,32,128]{3,2,1,0:T(8,128)(2,1)S(1)} %get-tuple-element.9, pred[]{:T(512)S(6)} %eq.11), kind=kLoop, calls=%fused_computation.6 | loop fusion | flops 786432 | bytes 1048577 | tf_op jit(solution)/shard_map/jit(_where)/select_n | solution.py:242
  163.9 6.3 %collective-permute-done.17 = bf16[4,8,32,128]{3,2,1,0:T(8,128)(2,1)S(1)} collective-permute-done((bf16[4,8,32,128]{3,2,1,0:T(8,128)(2,1)S(1)}, bf16[4,8,32,128]{3,2,1,0:T(8,128)(2,1)S(1)}, u32[]{:S(2)}, u32[]{:S(2)}) %collective-permute-start.17) | collective-permute-done | bytes 262176 | tf_op jit(solution)/shard_map/ppermute | solution.py:286
  (90 shorter events, 27.1 us)
Async XLA Ops:
  1.6 6.5 %collective-permute-start = (bf16[1,16,32,128]{3,2,1,0:T(8,128)(2,1)S(1)}, bf16[1,16,32,128]{3,2,1,0:T(8,128)(2,1)S(1)}, u32[]{:S(2)}, u32[]{:S(2)}) collective-permute-start(bf16[1,16,32,128]{3,2,1,0:T(8,128)(2,1)S(1)} %get-tuple-element.27), channel_id=1, source_target_pairs={{0,1},{1,2},{2,3},{3,4},{4,5},{5,6},{6,7},{7,8},{8,9},{9,10},{10,1... | collective-permute-start | bytes 393224 | tf_op jit(solution)/shard_map/ppermute | solution.py:202
  6.1 6.3 %collective-permute-start.1 = (bf16[1,16,32,128]{3,2,1,0:T(8,128)(2,1)S(1)}, bf16[1,16,32,128]{3,2,1,0:T(8,128)(2,1)S(1)}, u32[]{:S(2)}, u32[]{:S(2)}) collective-permute-start(bf16[1,16,32,128]{3,2,1,0:T(8,128)(2,1)S(1)} %get-tuple-element.26), channel_id=1, source_target_pairs={{1,0},{2,1},{3,2},{4,3},{5,4},{6,5},{7,6},{8,7},{9,8},{10,9},{11,1... | collective-permute-start | bytes 393224 | tf_op jit(solution)/shard_map/ppermute | solution.py:205
  12.4 14.1 %copy-start.17 = (f32[32]{0:T(128)S(1)}, f32[32]{0:T(128)}, u32[]{:S(2)}) copy-start(f32[32]{0:T(128)} %param.6) | copy-start | bytes 388
  12.5 17.1 %copy-start.15 = (bf16[4,16,32,128]{3,2,1,0:T(8,128)(2,1)S(1)}, bf16[4,16,32,128]{3,2,1,0:T(8,128)(2,1)}, u32[]{:S(2)}) copy-start(bf16[4,16,32,128]{3,2,1,0:T(8,128)(2,1)} %param.7) | copy-start | bytes 1572868
  12.6 10.9 %collective-permute-start.2 = (bf16[6,9,32,128]{3,2,1,0:T(8,128)(2,1)S(1)}, bf16[6,9,32,128]{3,2,1,0:T(8,128)(2,1)S(1)}, u32[]{:S(2)}, u32[]{:S(2)}) collective-permute-start(bf16[6,9,32,128]{3,2,1,0:T(8,128)(2,1)S(1)} %get-tuple-element.19), channel_id=1, source_target_pairs={{0,16},{16,0},{32,48},{48,32},{64,80},{80,64},{96,112},{112,96},{1... | collective-permute-start | bytes 1327112 | tf_op jit(solution)/shard_map/ppermute | solution.py:211
  23.8 20.8 %collective-permute-start.4 = (bf16[6,9,64,128]{3,2,1,0:T(8,128)(2,1)S(1)}, bf16[6,9,64,128]{3,2,1,0:T(8,128)(2,1)S(1)}, u32[]{:S(2)}, u32[]{:S(2)}) collective-permute-start(bf16[6,9,64,128]{3,2,1,0:T(8,128)(2,1)S(1)} %maximum_select_fusion.own), channel_id=1, source_target_pairs={{0,96},{16,112},{32,0},{48,16},{64,32},{80,48},{96,64},{112,80},{1... | collective-permute-start | bytes 2654216 | tf_op jit(solution)/shard_map/ppermute | solution.py:195
  26.6 22.3 %collective-permute-start.3 = (bf16[6,9,64,128]{3,2,1,0:T(8,128)(2,1)S(1)}, bf16[6,9,64,128]{3,2,1,0:T(8,128)(2,1)S(1)}, u32[]{:S(2)}, u32[]{:S(2)}) collective-permute-start(bf16[6,9,64,128]{3,2,1,0:T(8,128)(2,1)S(1)} %maximum_select_fusion.own), channel_id=1, source_target_pairs={{0,32},{16,48},{32,64},{48,80},{64,96},{80,112},{96,0},{112,16},{1... | collective-permute-start | bytes 2654216 | tf_op jit(solution)/shard_map/ppermute | solution.py:195
  26.6 23.5 %collective-permute-start.8 = (f32[32]{0:T(128)S(1)}, f32[32]{0:T(128)S(1)}, u32[]{:S(2)}, u32[]{:S(2)}) collective-permute-start(f32[32]{0:T(128)S(1)} %copy-done.17), channel_id=1, source_target_pairs={{0,16},{16,0},{32,48},{48,32},{64,80},{80,64},{96,112},{112,96},{1... | collective-permute-start | bytes 392 | tf_op jit(solution)/shard_map/ppermute | solution.py:221
  29.0 21.1 %collective-permute-start.7 = (bf16[27,32,256]{2,1,0:T(8,128)(2,1)}, bf16[27,32,256]{2,1,0:T(8,128)(2,1)}, u32[]{:S(2)}, u32[]{:S(2)}) collective-permute-start(bf16[27,32,256]{2,1,0:T(8,128)(2,1)} %param.5), channel_id=1, source_target_pairs={{0,16},{16,0},{32,48},{48,32},{64,80},{80,64},{96,112},{112,96},{1... | collective-permute-start | bytes 1327112 | tf_op jit(solution)/shard_map/ppermute | solution.py:220
  30.3 20.9 %collective-permute-start.9 = (bf16[4,8,32,128]{3,2,1,0:T(8,128)(2,1)}, bf16[4,8,32,128]{3,2,1,0:T(8,128)(2,1)}, u32[]{:S(2)}, u32[]{:S(2)}) collective-permute-start(bf16[4,8,32,128]{3,2,1,0:T(8,128)(2,1)} %get-tuple-element.24), channel_id=1, source_target_pairs={{0,16},{16,0},{32,48},{48,32},{64,80},{80,64},{96,112},{112,96},{1... | collective-permute-start | bytes 786440 | tf_op jit(solution)/shard_map/ppermute | solution.py:225
  32.7 17.2 %copy-start.16 = (bf16[27,32,256]{2,1,0:T(8,128)(2,1)S(1)}, bf16[27,32,256]{2,1,0:T(8,128)(2,1)}, u32[]{:S(2)}) copy-start(bf16[27,32,256]{2,1,0:T(8,128)(2,1)} %param.5) | copy-start | bytes 1327108
  45.3 13.0 %collective-permute-start.6 = (bf16[3,9,64,128]{3,2,1,0:T(8,128)(2,1)}, bf16[3,9,64,128]{3,2,1,0:T(8,128)(2,1)S(1)}, u32[]{:S(2)}, u32[]{:S(2)}) collective-permute-start(bf16[3,9,64,128]{3,2,1,0:T(8,128)(2,1)} %slice.69), channel_id=1, source_target_pairs={{0,96},{16,112},{32,0},{48,16},{64,32},{80,48},{96,64},{112,80},{1... | collective-permute-start | bytes 1327112 | tf_op jit(solution)/shard_map/ppermute | solution.py:195
  49.9 12.9 %collective-permute-start.5 = (bf16[3,9,64,128]{3,2,1,0:T(8,128)(2,1)}, bf16[3,9,64,128]{3,2,1,0:T(8,128)(2,1)}, u32[]{:S(2)}, u32[]{:S(2)}) collective-permute-start(bf16[3,9,64,128]{3,2,1,0:T(8,128)(2,1)} %slice.68), channel_id=1, source_target_pairs={{0,32},{16,48},{32,64},{48,80},{64,96},{80,112},{96,0},{112,16},{1... | collective-permute-start | bytes 1327112 | tf_op jit(solution)/shard_map/ppermute | solution.py:195
  62.9 1.2 copy-start.2
  75.5 11.8 %copy-start.3 = (bf16[4,8,64,128]{3,2,1,0:T(8,128)(2,1)}, bf16[4,8,64,128]{3,2,1,0:T(8,128)(2,1)S(1)}, u32[]{:S(2)}) copy-start(bf16[4,8,64,128]{3,2,1,0:T(8,128)(2,1)S(1)} %get-tuple-element.11.grad) | copy-start | bytes 1572868
  84.3 15.2 %collective-permute-start.18 = (f32[2,27,16,256]{3,2,1,0:T(8,128)S(1)}, f32[2,27,16,256]{3,2,1,0:T(8,128)S(1)}, u32[]{:S(2)}, u32[]{:S(2)}) collective-permute-start(f32[2,27,16,256]{3,2,1,0:T(8,128)S(1)} %slice_bitcast_fusion), channel_id=1, source_target_pairs={{0,1},{1,0},{2,3},{3,2},{4,5},{5,4},{6,7},{7,6},{8,9},{9,8},{10,11... | collective-permute-start | bytes 2654216 | tf_op jit(solution)/shard_map/ppermute | solution.py:259
  84.6 4.7 %collective-permute-start.11 = (bf16[4,64,128]{2,1,0:T(8,128)(2,1)S(1)}, bf16[4,64,128]{2,1,0:T(8,128)(2,1)S(1)}, u32[]{:S(2)}, u32[]{:S(2)}) collective-permute-start(bf16[4,64,128]{2,1,0:T(8,128)(2,1)S(1)} %pad_maximum_fusion.2), channel_id=1, source_target_pairs={{0,16},{16,0},{32,48},{48,32},{64,80},{80,64},{96,112},{112,96},{1... | collective-permute-start | bytes 196616 | tf_op jit(solution)/shard_map/ppermute | solution.py:251
  89.3 14.3 %collective-permute-start.12 = (bf16[9,64,128]{2,1,0:T(8,128)(2,1)S(1)}, bf16[9,64,128]{2,1,0:T(8,128)(2,1)S(1)}, u32[]{:S(2)}, u32[]{:S(2)}) collective-permute-start(bf16[9,64,128]{2,1,0:T(8,128)(2,1)S(1)} %pad_maximum_fusion), channel_id=1, source_target_pairs={{0,1},{1,2},{2,3},{3,4},{4,5},{5,6},{6,7},{7,8},{8,9},{9,10},{10,1... | collective-permute-start | bytes 442376 | tf_op jit(solution)/shard_map/ppermute | solution.py:202
  97.6 7.1 %collective-permute-start.13 = (bf16[9,64,128]{2,1,0:T(8,128)(2,1)}, bf16[9,64,128]{2,1,0:T(8,128)(2,1)S(1)}, u32[]{:S(2)}, u32[]{:S(2)}) collective-permute-start(bf16[9,64,128]{2,1,0:T(8,128)(2,1)} %pad_maximum_fusion.1), channel_id=1, source_target_pairs={{1,0},{2,1},{3,2},{4,3},{5,4},{6,5},{7,6},{8,7},{9,8},{10,9},{11,1... | collective-permute-start | bytes 442376 | tf_op jit(solution)/shard_map/ppermute | solution.py:205
  99.7 5.0 %copy-start.13 = (f32[2,27,16,256]{3,2,1,0:T(8,128)}, f32[2,27,16,256]{3,2,1,0:T(8,128)S(1)}, u32[]{:S(2)}) copy-start(f32[2,27,16,256]{3,2,1,0:T(8,128)S(1)} %fusion) | copy-start | bytes 2654212
  100.5 17.0 %collective-permute-start.19 = (f32[27,16,256]{2,1,0:T(8,128)}, f32[27,16,256]{2,1,0:T(8,128)}, u32[]{:S(2)}, u32[]{:S(2)}) collective-permute-start(f32[27,16,256]{2,1,0:T(8,128)} %slice_bitcast_fusion.5), channel_id=1, source_target_pairs={{0,16},{16,0},{32,48},{48,32},{64,80},{80,64},{96,112},{112,96},{1... | collective-permute-start | bytes 1327112 | tf_op jit(solution)/shard_map/ppermute | solution.py:260
  105.3 1.2 copy-start
  109.3 8.2 %copy-start.14 = (f32[2,27,16,256]{3,2,1,0:T(8,128)S(1)}, f32[2,27,16,256]{3,2,1,0:T(8,128)}, u32[]{:S(2)}) copy-start(f32[2,27,16,256]{3,2,1,0:T(8,128)} %copy-done.13) | copy-start | bytes 2654212
  121.2 18.7 %all-to-all-start = ((f32[8,54,256]{2,1,0:T(8,128)}), f32[8,54,256]{2,1,0:T(8,128)}, u32[]{:S(2)}, u32[]{:S(2)}) async-start(f32[8,54,256]{2,1,0:T(8,128)} %reshape.24), calls=%async_computation | async-start | bytes 917504 | tf_op jit(solution)/shard_map/all_to_all | solution.py:262
  131.3 13.9 %copy-start.8 = (bf16[4,8,32,128]{3,2,1,0:T(8,128)(2,1)S(1)}, bf16[4,8,32,128]{3,2,1,0:T(8,128)(2,1)}, u32[]{:S(2)}) copy-start(bf16[4,8,32,128]{3,2,1,0:T(8,128)(2,1)} %copy-done.7) | copy-start | bytes 786436
  131.3 26.3 %collective-permute-start.14 = (bf16[4,8,64,128]{3,2,1,0:T(8,128)(2,1)}, bf16[4,8,64,128]{3,2,1,0:T(8,128)(2,1)S(1)}, u32[]{:S(2)}, u32[]{:S(2)}) collective-permute-start(bf16[4,8,64,128]{3,2,1,0:T(8,128)(2,1)} %get-tuple-element.15), channel_id=1, source_target_pairs={{0,32},{16,48},{32,64},{48,80},{64,96},{80,112},{96,0},{112,16},{1... | collective-permute-start | bytes 1572872 | tf_op jit(solution)/shard_map/ppermute | solution.py:195
  131.3 26.3 %collective-permute-start.16 = (bf16[4,8,64,128]{3,2,1,0:T(8,128)(2,1)}, bf16[4,8,64,128]{3,2,1,0:T(8,128)(2,1)}, u32[]{:S(2)}, u32[]{:S(2)}) collective-permute-start(bf16[4,8,64,128]{3,2,1,0:T(8,128)(2,1)} %get-tuple-element.16), channel_id=1, source_target_pairs={{0,64},{16,80},{32,96},{48,112},{64,0},{80,16},{96,32},{112,48},{1... | collective-permute-start | bytes 1572872 | tf_op jit(solution)/shard_map/ppermute | solution.py:195
  132.1 25.8 %collective-permute-start.15 = (bf16[4,8,64,128]{3,2,1,0:T(8,128)(2,1)}, bf16[4,8,64,128]{3,2,1,0:T(8,128)(2,1)}, u32[]{:S(2)}, u32[]{:S(2)}) collective-permute-start(bf16[4,8,64,128]{3,2,1,0:T(8,128)(2,1)} %get-tuple-element.17), channel_id=1, source_target_pairs={{0,96},{16,112},{32,0},{48,16},{64,32},{80,48},{96,64},{112,80},{1... | collective-permute-start | bytes 1572872 | tf_op jit(solution)/shard_map/ppermute | solution.py:195
  141.7 17.7 %all-to-all-start.1 = ((f32[8,54,256]{2,1,0:T(8,128)}), f32[8,54,256]{2,1,0:T(8,128)S(1)}, u32[]{:S(2)}, u32[]{:S(2)}) async-start(f32[8,54,256]{2,1,0:T(8,128)} %broadcast_in_dim.5), calls=%async_computation.1 | async-start | bytes 917504 | tf_op jit(solution)/shard_map/all_to_all | solution.py:266
  145.2 16.8 %collective-permute-start.10 = (bf16[4,8,32,128]{3,2,1,0:T(8,128)(2,1)S(1)}, bf16[4,8,32,128]{3,2,1,0:T(8,128)(2,1)}, u32[]{:S(2)}, u32[]{:S(2)}) collective-permute-start(bf16[4,8,32,128]{3,2,1,0:T(8,128)(2,1)S(1)} %copy-done.8), channel_id=1, source_target_pairs={{0,16},{16,0},{32,48},{48,32},{64,80},{80,64},{96,112},{112,96},{1... | collective-permute-start | bytes 786440 | tf_op jit(solution)/shard_map/ppermute | solution.py:248
  159.5 11.5 %collective-permute-start.20 = (f32[27,16,256]{2,1,0:T(8,128)S(1)}, f32[27,16,256]{2,1,0:T(8,128)S(1)}, u32[]{:S(2)}, u32[]{:S(2)}) collective-permute-start(f32[27,16,256]{2,1,0:T(8,128)S(1)} %reshape.25), channel_id=1, source_target_pairs={{0,1},{1,0},{2,3},{3,2},{4,5},{5,4},{6,7},{7,6},{8,9},{9,8},{10,11... | collective-permute-start | bytes 1327112 | tf_op jit(solution)/shard_map/ppermute | solution.py:270
  160.7 9.5 %collective-permute-start.17 = (bf16[4,8,32,128]{3,2,1,0:T(8,128)(2,1)S(1)}, bf16[4,8,32,128]{3,2,1,0:T(8,128)(2,1)S(1)}, u32[]{:S(2)}, u32[]{:S(2)}) collective-permute-start(bf16[4,8,32,128]{3,2,1,0:T(8,128)(2,1)S(1)} %get-tuple-element.21), channel_id=1, source_target_pairs={{0,16},{16,0},{32,48},{48,32},{64,80},{80,64},{96,112},{112,96},{1... | collective-permute-start | bytes 786440 | tf_op jit(solution)/shard_map/ppermute | solution.py:286
  (9 other events, 7.7 us)
where the time goes:
time: 173 us; the launch traced here: 172 us
  waiting for transfers between devices  59.7 us (35%)
  starting transfers between devices  54.2 us (31%)
  Pallas kernels  26.6 us (15%)
  local copies, waits for them, and re-layouts  21.2 us (12%)
  other arithmetic  9.45 us (5%)
    ppermute x7, waiting for transfers between devices, turn(): lax.ppermute(value, 'chan', [(i, (i + 2 * step) % 8) for i in range(8)])  33.7 us
    ppermute x2, starting transfers between devices, up(): return lax.ppermute(value, 'space', [(i, i + 1) for i in range(15)])  12.1 us
    unnamed x39, local copies, waits for them, and re-layouts  10.4 us
    pallas_call x1, Pallas kernels, on_device(): call(forward_body, 10, [shape((4, 8, 32, 128), BF16), shape((4, 8, 32, 12...  9.72 us
    ppermute x7, starting transfers between devices, turn(): lax.ppermute(value, 'chan', [(i, (i + 2 * step) % 8) for i in range(8)])  9 us
    all_to_all x1, starting transfers between devices, on_device(): lax.all_to_all(pair.reshape(8, 54, 256), 'space', 0, 0, tiled=True, axis_...  8.95 us
    pallas_call x1, Pallas kernels, on_device(): call(weight_body, 3, [shape((2, 2, 27, 16, 256), F32)], [pltpu.VMEM((4, 8...  8.71 us
    ppermute x1, waiting for transfers between devices, on_device(): got = swap(theirs)  8.37 us
  transfers between devices with their start and end apart: 23, of which 11 were waited for; matrix products, arithmetic and copies ran while one was open for 9% of the time, Pallas kernels for 5%

commit v1 on v0

v1 whole, which is shorter than its diff:
```python
import functools
import math

import jax
import jax.numpy as jnp
from jax import lax
from jax.experimental import pallas as pl
from jax.experimental.pallas import tpu as pltpu
from jax.sharding import Mesh
from jax.sharding import PartitionSpec as P

BF16 = jnp.bfloat16
F32 = jnp.float32
VMEM_LIMIT = 20 * 1024 * 1024
CHAN = ("y", "xh")
SPACE = ("z", "xl", "core")


def moved(value, step):
    if step == 0:
        return value
    size = value.shape[-1]
    lane = lax.broadcasted_iota(jnp.int32, value.shape, value.ndim - 1)
    rolled = pltpu.roll(value, step % size, value.ndim - 1)
    edge = 0 if step == 1 else size - 1
    return jnp.where(lane == edge, 0.0, rolled)


def pair_of(ref, plane, row):
    return jnp.concatenate([ref[plane, row], ref[plane, row + 1]], axis=1)


def starts_of(here_y):
    return [pl.multiple_of(lax.rem(here_y + shift, 4) * 64, 64) for shift in range(4)]


def forward_rows(row, places, kernel, bias, cot_own, cot_other, out_own, out_other, grad,
                 plane_cot, plane_out):
    outs = kernel.shape[1] // 3
    total = jnp.zeros((3 * outs, 256), F32)
    for a, (ref, plane) in enumerate(places):
        for b in range(3):
            total = total + jnp.dot(
                kernel[3 * a + b], pair_of(ref, plane, row + b), preferred_element_type=F32
            )
    for r in range(2):
        part = total[:, 128 * r : 128 * r + 128]
        pre = (
            moved(part[:outs], 1) + part[outs : 2 * outs] + moved(part[2 * outs :], -1)
            + bias[...]
        )
        sig = 1.0 / (1.0 + jnp.exp(-pre))
        out = (pre * sig).astype(BF16)
        out_own[plane_out, row + r] = out[: outs // 2]
        out_other[plane_out, row + r] = out[outs // 2 :]
        cot = jnp.concatenate(
            [cot_own[plane_cot, row + r], cot_other[plane_cot, row + r]], axis=0
        ).astype(F32)
        grad[plane_out, row + r] = (cot * sig * (1.0 + pre * (1.0 - sig))).astype(BF16)


def inner_body(at, own, left, right, far_lo, far_hi, kernel, bias, cot_own, cot_other,
               out_own, out_other, grad, field):
    half, starts = at[1], starts_of(at[0])
    rows = own.shape[1]

    def put(plane, row, shift, value):
        field[plane, row + 1 - half, pl.ds(starts[shift], 64), :] = value

    def fill(plane, carry):
        for row in range(rows):
            for shift, ref in ((0, own), (3, left), (1, right)):
                put(plane, row, shift, ref[plane, row])
        field[plane, 9 * half] = jnp.zeros(field.shape[2:], BF16)
        return carry

    lax.fori_loop(0, 4, fill, 0)

    def fill_far(plane, carry):
        for row in range(rows):
            put(plane, row, 2, far_lo[plane, row])
            put(plane + 2, row, 2, far_hi[plane, row])
        return carry

    lax.fori_loop(0, 2, fill_far, 0)

    def step(index, carry):
        plane, row = index // 4, 2 * lax.rem(index, 4)
        forward_rows(
            row, [(field, plane), (field, plane + 1), (field, plane + 2)], kernel, bias,
            cot_own, cot_other, out_own, out_other, grad, plane + 1, plane,
        )
        return carry

    lax.fori_loop(0, 8, step, 0)


def outer_body(at, field, low, low_far, high, high_far, kernel, bias, cot_own, cot_other,
               in_own, in_other, in_grad, after, out_own, out_other, grad, first, last, rim):
    half, starts = at[1], starts_of(at[0])
    rows = low_far.shape[0]
    for side, near, far in ((0, low, low_far), (1, high, high_far)):
        for row in range(rows):
            for k, shift in enumerate((0, 3, 1)):
                rim[side, row + 1 - half, pl.ds(starts[shift], 64), :] = near[k, row]
            rim[side, row + 1 - half, pl.ds(starts[2], 64), :] = far[row]
        rim[side, 9 * half] = jnp.zeros(rim.shape[2:], BF16)
    for plane in range(2):
        out_own[plane + 1] = in_own[plane]
        out_other[plane + 1] = in_other[plane]
        grad[plane + 1] = in_grad[plane]

    def step(index, carry):
        row = 2 * index
        forward_rows(
            row, [(rim, 0), (field, 0), (field, 1)], kernel, bias,
            cot_own, cot_other, out_own, out_other, grad, 0, 0,
        )
        forward_rows(
            row, [(field, 2), (field, 3), (rim, 1)], kernel, bias,
            cot_own, cot_other, out_own, out_other, grad, 3, 3,
        )
        for r in range(2):
            first[row + r] = grad[0, row + r]
            last[row + r] = grad[3, row + r]
        return carry

    lax.fori_loop(0, 4, step, 0)


def spread(line):
    wide = line.astype(F32)
    return [moved(wide, c - 1).astype(BF16) for c in range(3)]


def weight_body(at, field, rim, grad, keep, give, stacked):
    half, core = at[1], at[2]
    planes, rows, outs = grad.shape[0], grad.shape[1], grad.shape[2]

    def fill(plane, carry):
        for row in range(rows):
            for c, line in enumerate(spread(grad[plane, row])):
                stacked[plane, row, outs * c : outs * (c + 1), :] = line
        return carry

    lax.fori_loop(0, planes, fill, 0)
    for side in range(2):
        for ref in (keep, give):
            ref[side, 432:448, :] = jnp.zeros((16, 256), F32)

    def cells_of(plane, b):
        if plane == 0:
            ref, plane = rim, 0
        elif plane == 5:
            ref, plane = rim, 1
        else:
            ref, plane = field, plane - 1
        return jnp.concatenate([ref[plane, row + b] for row in range(rows)], axis=1)

    for a in range(3):

        def step(b, carry):
            total = jnp.zeros((3 * outs, 256), F32)
            for plane in range(planes):
                grads = jnp.concatenate([stacked[plane, row] for row in range(rows)], axis=1)
                total = total + lax.dot_general(
                    grads, cells_of(plane + a, b), (((1,), (1,)), ((), ())),
                    preferred_element_type=F32,
                )
            for c in range(3):
                line = pl.multiple_of(16 * (9 * a + 3 * b + c), 16)
                for side in range(2):
                    low = outs * c + 32 * side
                    parts = total[low : low + 16], total[low + 16 : low + 32]
                    kept = jnp.where(core == 0, parts[0], parts[1])
                    given = jnp.where(core == 0, parts[1], parts[0])
                    keep[side ^ half, pl.ds(line, 16), :] = kept
                    give[side ^ half, pl.ds(line, 16), :] = given
            return carry

        lax.fori_loop(0, 3, step, 0)


def input_body(chunk, at, grad, rim, turned, turned_edge, after, own, near, far, back,
               stacked, held):
    half, starts = at[1], starts_of(at[0])
    rows, outs = grad.shape[1], grad.shape[2]

    def put(plane, row, line):
        for c, value in enumerate(spread(line)):
            stacked[plane, row, outs * c : outs * (c + 1), :] = value

    first, outer = (1, 0) if chunk == 0 else (0, 3)

    def fill(k, carry):
        for row in range(rows):
            put(k + first, row + 1, grad[k + chunk, row])
        return carry

    lax.fori_loop(0, 3, fill, 0)
    for row in range(rows):
        put(outer, row + 1, rim[row])
    for plane in range(4):
        for row in (0, 9):
            stacked[plane, row] = jnp.zeros(stacked.shape[2:], BF16)

    def store(places):
        for start, ref in zip(starts, (own, near, far, back)):
            block = held[pl.ds(start, 64), :]
            for r, (plane, row) in enumerate(places):
                ref[plane, row] = block[:, 128 * r : 128 * r + 128].astype(ref.dtype)

    def step(index, carry):
        plane, row = index // 4, 2 * lax.rem(index, 4)
        terms = jnp.concatenate(
            [
                pair_of(stacked, plane + 2 - a, row + 2 - b)
                for a in range(3)
                for b in range(3)
            ],
            axis=0,
        )
        held[...] = jnp.dot(turned[...], terms, preferred_element_type=F32)
        store([(plane, row), (plane, row + 1)])
        return carry

    lax.fori_loop(0, 8, step, 0)
    nearest = 8 - 7 * half
    terms = jnp.concatenate(
        [
            jnp.concatenate([stacked[2 - a, nearest], stacked[3 - a, nearest]], axis=1)
            for a in range(3)
        ],
        axis=0,
    )
    held[...] = jnp.dot(turned_edge[...], terms, preferred_element_type=F32)
    store([(0, rows), (1, rows)])


def total_body(at, own, near, far, back, kept, sent):
    half = at[1]
    mine = pl.multiple_of(32 * half, 32)
    others = pl.multiple_of(32 * (1 - half), 32)

    def sums(plane, row, start):
        value = own[plane, row, pl.ds(start, 32), :]
        for ref in (near, far, back):
            value = value + ref[plane, row, pl.ds(start, 32), :].astype(F32)
        return value

    for plane in range(2):
        for row in range(9):
            kept[plane, row] = sums(plane, row, mine)
            sent[plane, row] = sums(plane, row, others).astype(BF16)


def join_body(at, kept_0, kept_1, got_0, got_1, joined):
    half = at[1]
    for k, (kept, got) in enumerate(((kept_0, got_0), (kept_1, got_1))):
        for plane in range(2):
            for row in range(8):
                joined[2 * k + plane, 8 * half + row] = kept[plane, row].astype(BF16)
                joined[2 * k + plane, 8 - 8 * half + row] = got[plane, row]
            beside = 7 * (1 - half)
            joined[2 * k + plane, 8 * half + beside] = (
                kept[plane, beside] + got[plane, 8].astype(F32)
            ).astype(BF16)
            beyond = 7 * half
            joined[2 * k + plane, 8 - 8 * half + beyond] = (
                kept[plane, 8] + got[plane, beyond].astype(F32)
            ).astype(BF16)


def call(body, n_in, outs, scratch, flops, after=0):
    vmem = pl.BlockSpec(memory_space=pltpu.VMEM)
    anywhere = pl.BlockSpec(memory_space=pl.ANY)
    return pl.pallas_call(
        body,
        out_shape=[jax.ShapeDtypeStruct(*out) for out in outs],
        in_specs=[pl.BlockSpec(memory_space=pltpu.SMEM)]
        + [vmem] * (n_in - 1)
        + [anywhere] * after,
        out_specs=[vmem] * len(outs),
        scratch_shapes=scratch,
        compiler_params=pltpu.CompilerParams(vmem_limit_bytes=VMEM_LIMIT),
        cost_estimate=pl.CostEstimate(
            flops=flops, bytes_accessed=8 * 2**20, transcendentals=2**18
        ),
    )


def on_device(volume, kernel, bias, cotangent):
    here_y, half, core = lax.axis_index("y"), lax.axis_index("xh"), lax.axis_index("core")
    at = jnp.stack([here_y, half, core]).astype(jnp.int32)

    def swap(value):
        return lax.ppermute(value, "xh", [(0, 1), (1, 0)])

    def swap_core(value):
        return lax.ppermute(value, "core", [(0, 1), (1, 0)])

    def turn(value, step):
        return lax.ppermute(value, "y", [(i, (i + step) % 4) for i in range(4)])

    def up(value):
        return lax.ppermute(value, SPACE, [(i, i + 1) for i in range(15)])

    def down(value):
        return lax.ppermute(value, SPACE, [(i + 1, i) for i in range(15)])

    mine = lax.dynamic_slice_in_dim(volume, 7 * half, 9, axis=1)
    got = swap(lax.dynamic_slice_in_dim(volume, 7 * (1 - half), 9, axis=1))
    own = jnp.where(
        half == 0,
        jnp.concatenate([mine, got], axis=2),
        jnp.concatenate([got, mine], axis=2),
    )
    left, right = turn(own, 1), turn(own, -1)
    far_lo, far_hi = turn(left[:2], 1), turn(right[2:], -1)
    low = up(jnp.concatenate([own[3:], left[3:], right[3:]], axis=0))
    high = down(jnp.concatenate([own[:1], left[:1], right[:1]], axis=0))
    low_far, high_far = up(far_hi[1]), down(far_lo[0])

    kernel_all = jnp.concatenate([kernel, swap(kernel)], axis=1)
    taps = kernel_all.reshape(9, 192, 256)
    bias_all = jnp.concatenate([bias, swap(bias)])
    bias_wide = jnp.broadcast_to(bias_all[:, None], (64, 128))
    turned = kernel_all.reshape(27 * 64, 256).T
    by_b = taps.reshape(3, 3, 192, 256)
    turned_edge = jnp.where(half == 0, by_b[:, 2], by_b[:, 0]).reshape(576, 256).T
    cot_own = lax.dynamic_slice_in_dim(cotangent, 8 * half, 8, axis=1)
    cot_other = swap(lax.dynamic_slice_in_dim(cotangent, 8 * (1 - half), 8, axis=1))

    flops = 36 * 10**8
    out_own, out_other, grad, field = call(
        inner_body, 10,
        [
            ((2, 8, 32, 128), BF16), ((2, 8, 32, 128), BF16), ((2, 8, 64, 128), BF16),
            ((4, 10, 256, 128), BF16),
        ],
        [], flops // 2,
    )(at, own, left, right, far_lo, far_hi, taps, bias_wide, cot_own, cot_other)
    out_own, out_other, grad, first, last, rim = call(
        outer_body, 13,
        [
            ((4, 8, 32, 128), BF16), ((4, 8, 32, 128), BF16), ((4, 8, 64, 128), BF16),
            ((8, 64, 128), BF16), ((8, 64, 128), BF16), ((2, 10, 256, 128), BF16),
        ],
        [], flops // 2, 1,
    )(at, field, low, low_far, high, high_far, taps, bias_wide, cot_own, cot_other,
      out_own, out_other, grad, turned)

    got_out = swap(out_other)
    output = jnp.where(
        half == 0,
        jnp.concatenate([out_own, got_out], axis=1),
        jnp.concatenate([got_out, out_own], axis=1),
    )
    grad_low, grad_high = up(last), down(first)

    keep, give = call(
        weight_body, 4, [((2, 448, 256), F32)] * 2,
        [pltpu.VMEM((4, 8, 192, 128), BF16)], flops,
    )(at, field, rim, grad)
    chip = (keep + swap_core(give)).reshape(16, 56, 256)
    pieces = lax.all_to_all(chip, ("xh", "z", "xl"), 0, 0, tiled=True)
    whole = jnp.sum(pieces, axis=0) / math.sqrt(64 * 16 * 128)
    everyone = lax.all_to_all(
        jnp.broadcast_to(whole[None], (8, 56, 256)), ("z", "xl"), 0, 0, tiled=True
    ).reshape(448, 256)
    other = swap_core(everyone)
    everyone, other = (v[:432].reshape(27, 16, 256) for v in (everyone, other))
    weight_grad = jnp.where(
        core == 0,
        jnp.concatenate([everyone, other], axis=1),
        jnp.concatenate([other, everyone], axis=1),
    )

    def input_chunk(chunk, rim, after):
        own, near, far, back = call(
            functools.partial(input_body, chunk), 5,
            [((2, 9, 64, 128), F32)] + [((2, 9, 64, 128), BF16)] * 3,
            [pltpu.VMEM((4, 10, 192, 128), BF16), pltpu.VMEM((256, 256), F32)],
            flops // 2, 1,
        )(at, grad, rim, turned, turned_edge, after)
        near, back, far = turn(near, 1), turn(back, -1), turn(far, 2)
        kept, sent = call(
            total_body, 5, [((2, 9, 32, 128), F32), ((2, 9, 32, 128), BF16)], [], 10**6
        )(at, own, near, far, back)
        return kept, swap(sent)

    kept_0, got_0 = input_chunk(0, grad_low, bias_wide)
    kept_1, got_1 = input_chunk(1, grad_high, output)
    (input_grad,) = call(join_body, 5, [((4, 16, 32, 128), BF16)], [], 10**6)(
        at, kept_0, kept_1, got_0, got_1
    )
    return output, input_grad, weight_grad


def solution(mesh):
    split = Mesh(mesh.devices.reshape(4, 2, 4, 2, 2), CHAN + SPACE)
    return jax.shard_map(
        on_device,
        mesh=split,
        in_specs=(
            P(SPACE, None, CHAN, None),
            P(None, CHAN, None),
            P(CHAN),
            P(SPACE, None, CHAN, None),
        ),
        out_specs=(
            P(SPACE, None, CHAN, None),
            P(SPACE, None, CHAN, None),
            P(None, CHAN, None),
        ),
        check_vma=False,
    )
```

time: 173 us -> 153 us (0.88)
  waiting for transfers between devices: 59.7 us -> 38.4 us
  local copies, waits for them, and re-layouts: 21.2 us -> 9.62 us
  starting transfers between devices: 54.2 us -> 65 us
  Pallas kernels: 26.6 us -> 32.8 us
  other arithmetic: 9.45 us -> 4.87 us
    ppermute x21 -> x25, waiting for transfers between devices: 53.8 us -> 29 us  [the longest x7 17.7 us: swap(): return lax.ppermute(value, 'xh', [(0, 1), (1, 0)])]
    ppermute x21 -> x25, starting transfers between devices: 41.8 us -> 51.1 us  [the longest x7 16.2 us: swap(): return lax.ppermute(value, 'xh', [(0, 1), (1, 0)])]
    unnamed x39 -> x21, local copies, waits for them, and re-layouts: 10.4 us -> 1.11 us
    pallas_call x3 -> x8, Pallas kernels: 26.6 us -> 32.8 us  [the longest x2 11.3 us: input_chunk(): call(functools.partial(input_body, chunk), 5, [((2, 9, 64, 128), F32)] +...]
    all_to_all x2, waiting for transfers between devices: 5.88 us -> 9.38 us  [the longest x1 9.38 us: on_device(): pieces = lax.all_to_all(chip, ('xh', 'z', 'xl'), 0, 0, tiled=True)]
    slice x5 -> x7, local copies, waits for them, and re-layouts: 2.64 us -> 4.84 us  [the longest x2 2.08 us: on_device(): everyone, other = (v[:432].reshape(27, 16, 256) for v in (everyone, other))]
    squeeze x5 -> x2, local copies, waits for them, and re-layouts: 2.1 us -> 0.02 us  [on_device(): low_far, high_far = (up(far_hi[1]), down(far_lo[0]))]
    reshape x2 -> x0, local copies, waits for them, and re-layouts: 1.88 us -> none  [the longest x1 1.83 us: on_device(): pair.reshape(8, 54, 256)]
  transfers between devices with their start and end apart: 23 -> 27, of which waited for: 11 -> 9; matrix products, arithmetic and copies ran while one was open for 9% -> 6% of each run, Pallas kernels for 5% -> 13%
where the time goes in v1:
time: 153 us; the launch traced here: 152 us
  starting transfers between devices  65 us (42%)
  waiting for transfers between devices  38.4 us (25%)
  Pallas kernels  32.8 us (21%)
  local copies, waits for them, and re-layouts  9.62 us (6%)
  other arithmetic  4.87 us (3%)
    ppermute x7, waiting for transfers between devices, swap(): return lax.ppermute(value, 'xh', [(0, 1), (1, 0)])  17.7 us
    ppermute x7, starting transfers between devices, swap(): return lax.ppermute(value, 'xh', [(0, 1), (1, 0)])  16.2 us
    ppermute x10, starting transfers between devices, turn(): return lax.ppermute(value, 'y', [(i, (i + step) % 4) for i in range(4)])  15.8 us
    pallas_call x2, Pallas kernels, input_chunk(): call(functools.partial(input_body, chunk), 5, [((2, 9, 64, 128), F32)] +...  11.3 us
    ppermute x3, starting transfers between devices, up(): return lax.ppermute(value, SPACE, [(i, i + 1) for i in range(15)])  9.92 us
    all_to_all x1, waiting for transfers between devices, on_device(): pieces = lax.all_to_all(chip, ('xh', 'z', 'xl'), 0, 0, tiled=True)  9.38 us
    ppermute x10, waiting for transfers between devices, turn(): return lax.ppermute(value, 'y', [(i, (i + step) % 4) for i in range(4)])  8.85 us
    ppermute x3, starting transfers between devices, down(): return lax.ppermute(value, SPACE, [(i + 1, i) for i in range(15)])  8.83 us
  transfers between devices with their start and end apart: 27, of which 9 were waited for; matrix products, arithmetic and copies ran while one was open for 6% of the time, Pallas kernels for 13%

profile of v1, /device:TPU:1, one launch (start us, length us, event | category | flops | bytes accessed | tf_op | source)
XLA Modules:
  0.0 151.8 jit_solution(8595906232670192555)
XLA Ops:
  1.9 3.7 %collective-permute-start = (bf16[4,9,32,128]{3,2,1,0:T(8,128)(2,1)S(1)}, bf16[4,9,32,128]{3,2,1,0:T(8,128)(2,1)S(1)}, u32[]{:S(2)}, u32[]{:S(2)}) collective-permute-start(bf16[4,9,32,128]{3,2,1,0:T(8,128)(2,1)S(1)} %get-tuple-element.60), channel_id=1, source_target_pairs={{0,16},{16,0},{1,17},{17,1},{2,18},{18,2},{3,19},{19,3},{4,20},{20... | collective-permute-start | bytes 884744 | tf_op jit(solution)/shard_map/ppermute | solution.py:297
  6.3 2.9 %collective-permute-start.5 = (bf16[27,32,256]{2,1,0:T(8,128)(2,1)S(1)}, bf16[27,32,256]{2,1,0:T(8,128)(2,1)S(1)}, u32[]{:S(2)}, u32[]{:S(2)}) collective-permute-start(bf16[27,32,256]{2,1,0:T(8,128)(2,1)S(1)} %copy-done.8), channel_id=1, source_target_pairs={{0,16},{16,0},{1,17},{17,1},{2,18},{18,2},{3,19},{19,3},{4,20},{20... | collective-permute-start | bytes 1327112 | tf_op jit(solution)/shard_map/ppermute | solution.py:297
  9.3 2.4 %collective-permute-done = bf16[4,9,32,128]{3,2,1,0:T(8,128)(2,1)S(1)} collective-permute-done((bf16[4,9,32,128]{3,2,1,0:T(8,128)(2,1)S(1)}, bf16[4,9,32,128]{3,2,1,0:T(8,128)(2,1)S(1)}, u32[]{:S(2)}, u32[]{:S(2)}) %collective-permute-start) | collective-permute-done | bytes 294944 | tf_op jit(solution)/shard_map/ppermute | solution.py:297
  12.0 1.7 %collective-permute-start.1 = (bf16[4,9,64,128]{3,2,1,0:T(8,128)(2,1)S(1)}, bf16[4,9,64,128]{3,2,1,0:T(8,128)(2,1)S(1)}, u32[]{:S(2)}, u32[]{:S(2)}) collective-permute-start(bf16[4,9,64,128]{3,2,1,0:T(8,128)(2,1)S(1)} %maximum_select_fusion.1.own), channel_id=1, source_target_pairs={{0,32},{32,64},{64,96},{96,0},{1,33},{33,65},{65,97},{97,1},{2,34}... | collective-permute-start | bytes 1769480 | tf_op jit(solution)/shard_map/ppermute | solution.py:303
  13.7 1.5 %collective-permute-start.2 = (bf16[4,9,64,128]{3,2,1,0:T(8,128)(2,1)S(1)}, bf16[4,9,64,128]{3,2,1,0:T(8,128)(2,1)}, u32[]{:S(2)}, u32[]{:S(2)}) collective-permute-start(bf16[4,9,64,128]{3,2,1,0:T(8,128)(2,1)S(1)} %maximum_select_fusion.1.own), channel_id=1, source_target_pairs={{0,96},{32,0},{64,32},{96,64},{1,97},{33,1},{65,33},{97,65},{2,98}... | collective-permute-start | bytes 1769480 | tf_op jit(solution)/shard_map/ppermute | solution.py:303
  15.3 11.5 %collective-permute-done.6 = f32[32]{0:T(128)S(1)} collective-permute-done((f32[32]{0:T(128)S(1)}, f32[32]{0:T(128)S(1)}, u32[]{:S(2)}, u32[]{:S(2)}) %collective-permute-start.6) | collective-permute-done | bytes 160 | tf_op jit(solution)/shard_map/ppermute | solution.py:297
  28.4 1.7 %collective-permute-start.3 = (bf16[2,9,64,128]{3,2,1,0:T(8,128)(2,1)S(1)}, bf16[2,9,64,128]{3,2,1,0:T(8,128)(2,1)S(1)}, u32[]{:S(2)}, u32[]{:S(2)}) collective-permute-start(bf16[2,9,64,128]{3,2,1,0:T(8,128)(2,1)S(1)} %slice.56), channel_id=1, source_target_pairs={{0,32},{32,64},{64,96},{96,0},{1,33},{33,65},{65,97},{97,1},{2,34}... | collective-permute-start | bytes 884744 | tf_op jit(solution)/shard_map/ppermute | solution.py:303
  31.1 1.5 %collective-permute-start.4 = (bf16[2,9,64,128]{3,2,1,0:T(8,128)(2,1)S(1)}, bf16[2,9,64,128]{3,2,1,0:T(8,128)(2,1)S(1)}, u32[]{:S(2)}, u32[]{:S(2)}) collective-permute-start(bf16[2,9,64,128]{3,2,1,0:T(8,128)(2,1)S(1)} %slice.57), channel_id=1, source_target_pairs={{0,96},{32,0},{64,32},{96,64},{1,97},{33,1},{65,33},{97,65},{2,98}... | collective-permute-start | bytes 884744 | tf_op jit(solution)/shard_map/ppermute | solution.py:303
  33.8 3.8 %collective-permute-start.10 = (bf16[3,9,64,128]{3,2,1,0:T(8,128)(2,1)S(1)}, bf16[3,9,64,128]{3,2,1,0:T(8,128)(2,1)S(1)}, u32[]{:S(2)}, u32[]{:S(2)}) collective-permute-start(bf16[3,9,64,128]{3,2,1,0:T(8,128)(2,1)S(1)} %pad_maximum_fusion.1), channel_id=1, source_target_pairs={{1,0},{2,1},{3,2},{4,3},{5,4},{6,5},{7,6},{8,7},{9,8},{10,9},{11,1... | collective-permute-start | bytes 1327112 | tf_op jit(solution)/shard_map/ppermute | solution.py:309
  37.6 3.2 %collective-permute-start.8 = (bf16[3,9,64,128]{3,2,1,0:T(8,128)(2,1)S(1)}, bf16[3,9,64,128]{3,2,1,0:T(8,128)(2,1)S(1)}, u32[]{:S(2)}, u32[]{:S(2)}) collective-permute-start(bf16[3,9,64,128]{3,2,1,0:T(8,128)(2,1)S(1)} %pad_maximum_fusion), channel_id=1, source_target_pairs={{0,1},{1,2},{2,3},{3,4},{4,5},{5,6},{6,7},{7,8},{8,9},{9,10},{10,1... | collective-permute-start | bytes 1327112 | tf_op jit(solution)/shard_map/ppermute | solution.py:306
  40.9 1.9 %collective-permute-start.11 = (bf16[9,64,128]{2,1,0:T(8,128)(2,1)S(1)}, bf16[9,64,128]{2,1,0:T(8,128)(2,1)S(1)}, u32[]{:S(2)}, u32[]{:S(2)}) collective-permute-start(bf16[9,64,128]{2,1,0:T(8,128)(2,1)S(1)} %slice_bitcast_fusion.2), channel_id=1, source_target_pairs={{1,0},{2,1},{3,2},{4,3},{5,4},{6,5},{7,6},{8,7},{9,8},{10,9},{11,1... | collective-permute-start | bytes 442376 | tf_op jit(solution)/shard_map/ppermute | solution.py:309
  42.8 3.6 %collective-permute-start.9 = (bf16[9,64,128]{2,1,0:T(8,128)(2,1)S(1)}, bf16[9,64,128]{2,1,0:T(8,128)(2,1)S(1)}, u32[]{:S(2)}, u32[]{:S(2)}) collective-permute-start(bf16[9,64,128]{2,1,0:T(8,128)(2,1)S(1)} %slice_bitcast_fusion.3), channel_id=1, source_target_pairs={{0,1},{1,2},{2,3},{3,4},{4,5},{5,6},{6,7},{7,8},{8,9},{9,10},{10,1... | collective-permute-start | bytes 442376 | tf_op jit(solution)/shard_map/ppermute | solution.py:306
  46.6 5.5 %shard_map.67 = (bf16[2,8,32,128]{3,2,1,0:T(8,128)(2,1)S(1)}, bf16[2,8,32,128]{3,2,1,0:T(8,128)(2,1)S(1)}, bf16[2,8,64,128]{3,2,1,0:T(8,128)(2,1)S(1)}, bf16[4,10,256,128]{3,2,1,0:T(8,128)(2,1)S(1)}) custom-call(s32[3]{0:T(128)S(1)} %pad_add_fusion.at, bf16[4,9,64,128]{3,2,1,0:T(8,128)(2,1)S(1)} %maximum_select_fusion.1.own, ...), custom_call_target="tpu_custom_call" | custom-call | flops 1800000000 | bytes 8388608 | tf_op jit(solution)/shard_map/pallas_call | solution.py:335
  52.1 4.6 %shard_map.68 = (bf16[4,8,32,128]{3,2,1,0:T(8,128)(2,1)S(1)}, bf16[4,8,32,128]{3,2,1,0:T(8,128)(2,1)}, bf16[4,8,64,128]{3,2,1,0:T(8,128)(2,1)S(1)}, bf16[8,64,12...) custom-call(s32[3]{0:T(128)S(1)} %pad_add_fusion.at, ...), custom_call_target="tpu_custom_call" | custom-call | flops 1800000000 | bytes 8388608 | tf_op jit(solution)/shard_map/pallas_call | solution.py:343
  56.7 8.6 %shard_map.74 = (f32[2,448,256]{2,1,0:T(8,128)S(1)}, f32[2,448,256]{2,1,0:T(8,128)S(1)}) custom-call(s32[3]{0:T(128)S(1)} %pad_add_fusion.at, bf16[4,10,256,128]{3,2,1,0:T(8,128)(2,1)S(1)} %get-tuple-element.27.field, bf16[2,10,256,128]{3,2,1,0:T(8,128)(2,1)S(1)} %get-tuple-element.48.rim, bf16[4,8,64,128]{3,2,1,0:T(8,128)(2,1)S(1)} %get-tuple-element.33.grad), custom_call_target="tpu_custom_call" | custom-call | flops 3600000000 | bytes 8388608 | tf_op jit(solution)/shard_map/pallas_call | solution.py:361
  65.5 2.5 %collective-permute-done.23 = f32[2,448,256]{2,1,0:T(8,128)S(1)} collective-permute-done((f32[2,448,256]{2,1,0:T(8,128)S(1)}, f32[2,448,256]{2,1,0:T(8,128)S(1)}, u32[]{:S(2)}, u32[]{:S(2)}) %collective-permute-start.23) | collective-permute-done | bytes 917536 | tf_op jit(solution)/shard_map/ppermute | solution.py:300
  69.0 8.5 %all-to-all-start = ((f32[16,56,256]{2,1,0:T(8,128)}), f32[16,56,256]{2,1,0:T(8,128)}, u32[]{:S(2)}, u32[]{:S(2)}) async-start(f32[16,56,256]{2,1,0:T(8,128)} %bitcast.34), calls=%async_computation | async-start | bytes 1835008 | tf_op jit(solution)/shard_map/all_to_all | solution.py:366
  77.5 2.8 %collective-permute-start.12 = (bf16[4,8,32,128]{3,2,1,0:T(8,128)(2,1)}, bf16[4,8,32,128]{3,2,1,0:T(8,128)(2,1)}, u32[]{:S(2)}, u32[]{:S(2)}) collective-permute-start(bf16[4,8,32,128]{3,2,1,0:T(8,128)(2,1)} %get-tuple-element.32), channel_id=1, source_target_pairs={{0,16},{16,0},{1,17},{17,1},{2,18},{18,2},{3,19},{19,3},{4,20},{20... | collective-permute-start | bytes 786440 | tf_op jit(solution)/shard_map/ppermute | solution.py:297
  80.3 3.1 %collective-permute-start.13 = (bf16[8,64,128]{2,1,0:T(8,128)(2,1)S(1)}, bf16[8,64,128]{2,1,0:T(8,128)(2,1)S(1)}, u32[]{:S(2)}, u32[]{:S(2)}) collective-permute-start(bf16[8,64,128]{2,1,0:T(8,128)(2,1)S(1)} %get-tuple-element.34), channel_id=1, source_target_pairs={{0,1},{1,2},{2,3},{3,4},{4,5},{5,6},{6,7},{7,8},{8,9},{9,10},{10,1... | collective-permute-start | bytes 393224 | tf_op jit(solution)/shard_map/ppermute | solution.py:306
  83.4 9.4 %all-to-all-done = f32[16,56,256]{2,1,0:T(8,128)} async-done(((f32[16,56,256]{2,1,0:T(8,128)}), f32[16,56,256]{2,1,0:T(8,128)}, u32[]{:S(2)}, u32[]{:S(2)}) %all-to-all-start) | async-done | bytes 917536 | tf_op jit(solution)/shard_map/all_to_all | solution.py:366
  94.8 5.4 %all-to-all-start.1 = ((f32[8,56,256]{2,1,0:T(8,128)}), f32[8,56,256]{2,1,0:T(8,128)}, u32[]{:S(2)}, u32[]{:S(2)}) async-start(f32[8,56,256]{2,1,0:T(8,128)} %broadcast_in_dim.5), calls=%async_computation.1 | async-start | bytes 917504 | tf_op jit(solution)/shard_map/all_to_all | solution.py:368
  100.5 3.1 %collective-permute-start.17 = (bf16[8,64,128]{2,1,0:T(8,128)(2,1)}, bf16[8,64,128]{2,1,0:T(8,128)(2,1)}, u32[]{:S(2)}, u32[]{:S(2)}) collective-permute-start(bf16[8,64,128]{2,1,0:T(8,128)(2,1)} %get-tuple-element.40), channel_id=1, source_target_pairs={{1,0},{2,1},{3,2},{4,3},{5,4},{6,5},{7,6},{8,7},{9,8},{10,9},{11,1... | collective-permute-start | bytes 393224 | tf_op jit(solution)/shard_map/ppermute | solution.py:309
  103.6 5.9 %shard_map.69 = (f32[2,9,64,128]{3,2,1,0:T(8,128)S(1)}, bf16[2,9,64,128]{3,2,1,0:T(8,128)(2,1)}, bf16[2,9,64,128]{3,2,1,0:T(8,128)(2,1)}, bf16[2,9,64,128]{3,2,1,0:T(8,128)(2,1)}) custom-call(s32[3]{0:T(128)S(1)} %pad_add_fusion.at, bf16[4,8,64,128]{3,2,1,0:T(8,128)(2,1)S(1)} %get-tuple-element.33.grad, bf16[8,64,128]{2,1,0:T(8,128)(2,1)S(1)} %collective-permute-done.13.rim, ...), custom_call_target="tpu_custom_call" | custom-call | flops 1800000000 | bytes 8388608 | tf_op jit(solution)/shard_map/pallas_call | solution.py:380
  109.6 2.6 %collective-permute-start.15 = (bf16[2,9,64,128]{3,2,1,0:T(8,128)(2,1)}, bf16[2,9,64,128]{3,2,1,0:T(8,128)(2,1)S(1)}, u32[]{:S(2)}, u32[]{:S(2)}) collective-permute-start(bf16[2,9,64,128]{3,2,1,0:T(8,128)(2,1)} %get-tuple-element.37), channel_id=1, source_target_pairs={{0,64},{32,96},{64,0},{96,32},{1,65},{33,97},{65,1},{97,33},{2,66}... | collective-permute-start | bytes 884744 | tf_op jit(solution)/shard_map/ppermute | solution.py:303
  115.8 5.4 %shard_map.71 = (f32[2,9,64,128]{3,2,1,0:T(8,128)S(1)}, bf16[2,9,64,128]{3,2,1,0:T(8,128)(2,1)S(1)}, bf16[2,9,64,128]{3,2,1,0:T(8,128)(2,1)S(1)}, bf16[2,9,64,128]{3,2,1,0:T(8,128)(2,1)S(1)}) custom-call(s32[3]{0:T(128)S(1)} %pad_add_fusion.at, bf16[4,8,64,128]{3,2,1,0:T(8,128)(2,1)S(1)} %copy-done.4, bf16[8,64,128]{2,1,0:T(8,128)(2,1)} %collective-permute-done.17.rim, ...), custom_call_target="tpu_custom_call" | custom-call | flops 1800000000 | bytes 8388608 | tf_op jit(solution)/shard_map/pallas_call | solution.py:380
  121.7 5.0 %collective-permute-start.19 = (bf16[2,9,64,128]{3,2,1,0:T(8,128)(2,1)S(1)}, bf16[2,9,64,128]{3,2,1,0:T(8,128)(2,1)S(1)}, u32[]{:S(2)}, u32[]{:S(2)}) collective-permute-start(bf16[2,9,64,128]{3,2,1,0:T(8,128)(2,1)S(1)} %get-tuple-element.43), channel_id=1, source_target_pairs={{0,64},{32,96},{64,0},{96,32},{1,65},{33,97},{65,1},{97,33},{2,66}... | collective-permute-start | bytes 884744 | tf_op jit(solution)/shard_map/ppermute | solution.py:303
  127.5 3.3 %collective-permute-start.21 = (bf16[2,9,32,128]{3,2,1,0:T(8,128)(2,1)S(1)}, bf16[2,9,32,128]{3,2,1,0:T(8,128)(2,1)S(1)}, u32[]{:S(2)}, u32[]{:S(2)}) collective-permute-start(bf16[2,9,32,128]{3,2,1,0:T(8,128)(2,1)S(1)} %get-tuple-element.46), channel_id=1, source_target_pairs={{0,16},{16,0},{1,17},{17,1},{2,18},{18,2},{3,19},{19,3},{4,20},{20... | collective-permute-start | bytes 442376 | tf_op jit(solution)/shard_map/ppermute | solution.py:297
  130.8 1.7 %collective-permute-done.18.near = bf16[2,9,64,128]{3,2,1,0:T(8,128)(2,1)S(1)} collective-permute-done((bf16[2,9,64,128]{3,2,1,0:T(8,128)(2,1)S(1)}, bf16[2,9,64,128]{3,2,1,0:T(8,128)(2,1)S(1)}, u32[]{:S(2)}, u32[]{:S(2)}) %collective-permute-start.18) | collective-permute-done | bytes 294944 | tf_op jit(solution)/shard_map/ppermute | solution.py:303
  132.5 6.1 %collective-permute-done.19.far = bf16[2,9,64,128]{3,2,1,0:T(8,128)(2,1)S(1)} collective-permute-done((bf16[2,9,64,128]{3,2,1,0:T(8,128)(2,1)S(1)}, bf16[2,9,64,128]{3,2,1,0:T(8,128)(2,1)S(1)}, u32[]{:S(2)}, u32[]{:S(2)}) %collective-permute-start.19) | collective-permute-done | bytes 294944 | tf_op jit(solution)/shard_map/ppermute | solution.py:303
  140.2 3.3 %collective-permute-start.22 = (bf16[2,9,32,128]{3,2,1,0:T(8,128)(2,1)S(1)}, bf16[2,9,32,128]{3,2,1,0:T(8,128)(2,1)S(1)}, u32[]{:S(2)}, u32[]{:S(2)}) collective-permute-start(bf16[2,9,32,128]{3,2,1,0:T(8,128)(2,1)S(1)} %get-tuple-element.47), channel_id=1, source_target_pairs={{0,16},{16,0},{1,17},{17,1},{2,18},{18,2},{3,19},{19,3},{4,20},{20... | collective-permute-start | bytes 442376 | tf_op jit(solution)/shard_map/ppermute | solution.py:297
  143.5 3.8 %collective-permute-done.22.got_1 = bf16[2,9,32,128]{3,2,1,0:T(8,128)(2,1)S(1)} collective-permute-done((bf16[2,9,32,128]{3,2,1,0:T(8,128)(2,1)S(1)}, bf16[2,9,32,128]{3,2,1,0:T(8,128)(2,1)S(1)}, u32[]{:S(2)}, u32[]{:S(2)}) %collective-permute-start.22) | collective-permute-done | bytes 147488 | tf_op jit(solution)/shard_map/ppermute | solution.py:297
  147.3 1.4 shard_map.73
  (78 shorter events, 19.0 us)
Async XLA Ops:
  0.7 8.6 %copy-start.9 = (f32[32]{0:T(128)S(1)}, f32[32]{0:T(128)}, u32[]{:S(2)}) copy-start(f32[32]{0:T(128)} %param.6) | copy-start | bytes 388
  1.9 9.9 %collective-permute-start = (bf16[4,9,32,128]{3,2,1,0:T(8,128)(2,1)S(1)}, bf16[4,9,32,128]{3,2,1,0:T(8,128)(2,1)S(1)}, u32[]{:S(2)}, u32[]{:S(2)}) collective-permute-start(bf16[4,9,32,128]{3,2,1,0:T(8,128)(2,1)S(1)} %get-tuple-element.60), channel_id=1, source_target_pairs={{0,16},{16,0},{1,17},{17,1},{2,18},{18,2},{3,19},{19,3},{4,20},{20... | collective-permute-start | bytes 884744 | tf_op jit(solution)/shard_map/ppermute | solution.py:297
  6.3 40.2 %collective-permute-start.7 = (bf16[4,8,32,128]{3,2,1,0:T(8,128)(2,1)}, bf16[4,8,32,128]{3,2,1,0:T(8,128)(2,1)S(1)}, u32[]{:S(2)}, u32[]{:S(2)}) collective-permute-start(bf16[4,8,32,128]{3,2,1,0:T(8,128)(2,1)} %get-tuple-element.57), channel_id=1, source_target_pairs={{0,16},{16,0},{1,17},{17,1},{2,18},{18,2},{3,19},{19,3},{4,20},{20... | collective-permute-start | bytes 786440 | tf_op jit(solution)/shard_map/ppermute | solution.py:297
  6.3 21.4 %collective-permute-start.5 = (bf16[27,32,256]{2,1,0:T(8,128)(2,1)S(1)}, bf16[27,32,256]{2,1,0:T(8,128)(2,1)S(1)}, u32[]{:S(2)}, u32[]{:S(2)}) collective-permute-start(bf16[27,32,256]{2,1,0:T(8,128)(2,1)S(1)} %copy-done.8), channel_id=1, source_target_pairs={{0,16},{16,0},{1,17},{17,1},{2,18},{18,2},{3,19},{19,3},{4,20},{20... | collective-permute-start | bytes 1327112 | tf_op jit(solution)/shard_map/ppermute | solution.py:297
  9.2 17.6 %collective-permute-start.6 = (f32[32]{0:T(128)S(1)}, f32[32]{0:T(128)S(1)}, u32[]{:S(2)}, u32[]{:S(2)}) collective-permute-start(f32[32]{0:T(128)S(1)} %copy-done.9), channel_id=1, source_target_pairs={{0,16},{16,0},{1,17},{17,1},{2,18},{18,2},{3,19},{19,3},{4,20},{20... | collective-permute-start | bytes 392 | tf_op jit(solution)/shard_map/ppermute | solution.py:297
  12.0 16.4 %collective-permute-start.1 = (bf16[4,9,64,128]{3,2,1,0:T(8,128)(2,1)S(1)}, bf16[4,9,64,128]{3,2,1,0:T(8,128)(2,1)S(1)}, u32[]{:S(2)}, u32[]{:S(2)}) collective-permute-start(bf16[4,9,64,128]{3,2,1,0:T(8,128)(2,1)S(1)} %maximum_select_fusion.1.own), channel_id=1, source_target_pairs={{0,32},{32,64},{64,96},{96,0},{1,33},{33,65},{65,97},{97,1},{2,34}... | collective-permute-start | bytes 1769480 | tf_op jit(solution)/shard_map/ppermute | solution.py:303
  13.7 16.4 %collective-permute-start.2 = (bf16[4,9,64,128]{3,2,1,0:T(8,128)(2,1)S(1)}, bf16[4,9,64,128]{3,2,1,0:T(8,128)(2,1)}, u32[]{:S(2)}, u32[]{:S(2)}) collective-permute-start(bf16[4,9,64,128]{3,2,1,0:T(8,128)(2,1)S(1)} %maximum_select_fusion.1.own), channel_id=1, source_target_pairs={{0,96},{32,0},{64,32},{96,64},{1,97},{33,1},{65,33},{97,65},{2,98}... | collective-permute-start | bytes 1769480 | tf_op jit(solution)/shard_map/ppermute | solution.py:303
  28.4 12.5 %collective-permute-start.3 = (bf16[2,9,64,128]{3,2,1,0:T(8,128)(2,1)S(1)}, bf16[2,9,64,128]{3,2,1,0:T(8,128)(2,1)S(1)}, u32[]{:S(2)}, u32[]{:S(2)}) collective-permute-start(bf16[2,9,64,128]{3,2,1,0:T(8,128)(2,1)S(1)} %slice.56), channel_id=1, source_target_pairs={{0,32},{32,64},{64,96},{96,0},{1,33},{33,65},{65,97},{97,1},{2,34}... | collective-permute-start | bytes 884744 | tf_op jit(solution)/shard_map/ppermute | solution.py:303
  31.1 11.7 %collective-permute-start.4 = (bf16[2,9,64,128]{3,2,1,0:T(8,128)(2,1)S(1)}, bf16[2,9,64,128]{3,2,1,0:T(8,128)(2,1)S(1)}, u32[]{:S(2)}, u32[]{:S(2)}) collective-permute-start(bf16[2,9,64,128]{3,2,1,0:T(8,128)(2,1)S(1)} %slice.57), channel_id=1, source_target_pairs={{0,96},{32,0},{64,32},{96,64},{1,97},{33,1},{65,33},{97,65},{2,98}... | collective-permute-start | bytes 884744 | tf_op jit(solution)/shard_map/ppermute | solution.py:303
  33.8 18.3 %collective-permute-start.10 = (bf16[3,9,64,128]{3,2,1,0:T(8,128)(2,1)S(1)}, bf16[3,9,64,128]{3,2,1,0:T(8,128)(2,1)S(1)}, u32[]{:S(2)}, u32[]{:S(2)}) collective-permute-start(bf16[3,9,64,128]{3,2,1,0:T(8,128)(2,1)S(1)} %pad_maximum_fusion.1), channel_id=1, source_target_pairs={{1,0},{2,1},{3,2},{4,3},{5,4},{6,5},{7,6},{8,7},{9,8},{10,9},{11,1... | collective-permute-start | bytes 1327112 | tf_op jit(solution)/shard_map/ppermute | solution.py:309
  37.6 14.5 %collective-permute-start.8 = (bf16[3,9,64,128]{3,2,1,0:T(8,128)(2,1)S(1)}, bf16[3,9,64,128]{3,2,1,0:T(8,128)(2,1)S(1)}, u32[]{:S(2)}, u32[]{:S(2)}) collective-permute-start(bf16[3,9,64,128]{3,2,1,0:T(8,128)(2,1)S(1)} %pad_maximum_fusion), channel_id=1, source_target_pairs={{0,1},{1,2},{2,3},{3,4},{4,5},{5,6},{6,7},{7,8},{8,9},{9,10},{10,1... | collective-permute-start | bytes 1327112 | tf_op jit(solution)/shard_map/ppermute | solution.py:306
  40.9 11.2 %collective-permute-start.11 = (bf16[9,64,128]{2,1,0:T(8,128)(2,1)S(1)}, bf16[9,64,128]{2,1,0:T(8,128)(2,1)S(1)}, u32[]{:S(2)}, u32[]{:S(2)}) collective-permute-start(bf16[9,64,128]{2,1,0:T(8,128)(2,1)S(1)} %slice_bitcast_fusion.2), channel_id=1, source_target_pairs={{1,0},{2,1},{3,2},{4,3},{5,4},{6,5},{7,6},{8,7},{9,8},{10,9},{11,1... | collective-permute-start | bytes 442376 | tf_op jit(solution)/shard_map/ppermute | solution.py:309
  42.8 9.3 %collective-permute-start.9 = (bf16[9,64,128]{2,1,0:T(8,128)(2,1)S(1)}, bf16[9,64,128]{2,1,0:T(8,128)(2,1)S(1)}, u32[]{:S(2)}, u32[]{:S(2)}) collective-permute-start(bf16[9,64,128]{2,1,0:T(8,128)(2,1)S(1)} %slice_bitcast_fusion.3), channel_id=1, source_target_pairs={{0,1},{1,2},{2,3},{3,4},{4,5},{5,6},{6,7},{7,8},{8,9},{9,10},{10,1... | collective-permute-start | bytes 442376 | tf_op jit(solution)/shard_map/ppermute | solution.py:306
  56.7 8.6 %copy-start.1 = (bf16[4,8,32,128]{3,2,1,0:T(8,128)(2,1)}, bf16[4,8,32,128]{3,2,1,0:T(8,128)(2,1)S(1)}, u32[]{:S(2)}) copy-start(bf16[4,8,32,128]{3,2,1,0:T(8,128)(2,1)S(1)} %get-tuple-element.31) | copy-start | bytes 786436
  56.7 46.9 %copy-start.3 = (bf16[4,8,64,128]{3,2,1,0:T(8,128)(2,1)}, bf16[4,8,64,128]{3,2,1,0:T(8,128)(2,1)S(1)}, u32[]{:S(2)}) copy-start(bf16[4,8,64,128]{3,2,1,0:T(8,128)(2,1)S(1)} %get-tuple-element.33.grad) | copy-start | bytes 1572868
  65.4 2.6 %collective-permute-start.23 = (f32[2,448,256]{2,1,0:T(8,128)S(1)}, f32[2,448,256]{2,1,0:T(8,128)S(1)}, u32[]{:S(2)}, u32[]{:S(2)}) collective-permute-start(f32[2,448,256]{2,1,0:T(8,128)S(1)} %get-tuple-element.50), channel_id=1, source_target_pairs={{0,1},{1,0},{2,3},{3,2},{4,5},{5,4},{6,7},{7,6},{8,9},{9,8},{10,11... | collective-permute-start | bytes 2752520 | tf_op jit(solution)/shard_map/ppermute | solution.py:300
  69.0 23.8 %all-to-all-start = ((f32[16,56,256]{2,1,0:T(8,128)}), f32[16,56,256]{2,1,0:T(8,128)}, u32[]{:S(2)}, u32[]{:S(2)}) async-start(f32[16,56,256]{2,1,0:T(8,128)} %bitcast.34), calls=%async_computation | async-start | bytes 1835008 | tf_op jit(solution)/shard_map/all_to_all | solution.py:366
  77.5 35.9 %collective-permute-start.12 = (bf16[4,8,32,128]{3,2,1,0:T(8,128)(2,1)}, bf16[4,8,32,128]{3,2,1,0:T(8,128)(2,1)}, u32[]{:S(2)}, u32[]{:S(2)}) collective-permute-start(bf16[4,8,32,128]{3,2,1,0:T(8,128)(2,1)} %get-tuple-element.32), channel_id=1, source_target_pairs={{0,16},{16,0},{1,17},{17,1},{2,18},{18,2},{3,19},{19,3},{4,20},{20... | collective-permute-start | bytes 786440 | tf_op jit(solution)/shard_map/ppermute | solution.py:297
  80.3 23.3 %collective-permute-start.13 = (bf16[8,64,128]{2,1,0:T(8,128)(2,1)S(1)}, bf16[8,64,128]{2,1,0:T(8,128)(2,1)S(1)}, u32[]{:S(2)}, u32[]{:S(2)}) collective-permute-start(bf16[8,64,128]{2,1,0:T(8,128)(2,1)S(1)} %get-tuple-element.34), channel_id=1, source_target_pairs={{0,1},{1,2},{2,3},{3,4},{4,5},{5,6},{6,7},{7,8},{8,9},{9,10},{10,1... | collective-permute-start | bytes 393224 | tf_op jit(solution)/shard_map/ppermute | solution.py:306
  94.8 19.7 %all-to-all-start.1 = ((f32[8,56,256]{2,1,0:T(8,128)}), f32[8,56,256]{2,1,0:T(8,128)}, u32[]{:S(2)}, u32[]{:S(2)}) async-start(f32[8,56,256]{2,1,0:T(8,128)} %broadcast_in_dim.5), calls=%async_computation.1 | async-start | bytes 917504 | tf_op jit(solution)/shard_map/all_to_all | solution.py:368
  100.5 14.3 %collective-permute-start.17 = (bf16[8,64,128]{2,1,0:T(8,128)(2,1)}, bf16[8,64,128]{2,1,0:T(8,128)(2,1)}, u32[]{:S(2)}, u32[]{:S(2)}) collective-permute-start(bf16[8,64,128]{2,1,0:T(8,128)(2,1)} %get-tuple-element.40), channel_id=1, source_target_pairs={{1,0},{2,1},{3,2},{4,3},{5,4},{6,5},{7,6},{8,7},{9,8},{10,9},{11,1... | collective-permute-start | bytes 393224 | tf_op jit(solution)/shard_map/ppermute | solution.py:309
  103.6 9.7 %copy-start.2 = (bf16[4,8,32,128]{3,2,1,0:T(8,128)(2,1)S(1)}, bf16[4,8,32,128]{3,2,1,0:T(8,128)(2,1)}, u32[]{:S(2)}) copy-start(bf16[4,8,32,128]{3,2,1,0:T(8,128)(2,1)} %copy-done.1) | copy-start | bytes 786436
  109.6 12.1 %collective-permute-start.14 = (bf16[2,9,64,128]{3,2,1,0:T(8,128)(2,1)}, bf16[2,9,64,128]{3,2,1,0:T(8,128)(2,1)S(1)}, u32[]{:S(2)}, u32[]{:S(2)}) collective-permute-start(bf16[2,9,64,128]{3,2,1,0:T(8,128)(2,1)} %get-tuple-element.36), channel_id=1, source_target_pairs={{0,32},{32,64},{64,96},{96,0},{1,33},{33,65},{65,97},{97,1},{2,34}... | collective-permute-start | bytes 884744 | tf_op jit(solution)/shard_map/ppermute | solution.py:303
  109.6 17.0 %collective-permute-start.15 = (bf16[2,9,64,128]{3,2,1,0:T(8,128)(2,1)}, bf16[2,9,64,128]{3,2,1,0:T(8,128)(2,1)S(1)}, u32[]{:S(2)}, u32[]{:S(2)}) collective-permute-start(bf16[2,9,64,128]{3,2,1,0:T(8,128)(2,1)} %get-tuple-element.37), channel_id=1, source_target_pairs={{0,64},{32,96},{64,0},{96,32},{1,65},{33,97},{65,1},{97,33},{2,66}... | collective-permute-start | bytes 884744 | tf_op jit(solution)/shard_map/ppermute | solution.py:303
  112.3 14.6 %collective-permute-start.16 = (bf16[2,9,64,128]{3,2,1,0:T(8,128)(2,1)}, bf16[2,9,64,128]{3,2,1,0:T(8,128)(2,1)S(1)}, u32[]{:S(2)}, u32[]{:S(2)}) collective-permute-start(bf16[2,9,64,128]{3,2,1,0:T(8,128)(2,1)} %get-tuple-element.38), channel_id=1, source_target_pairs={{0,96},{32,0},{64,32},{96,64},{1,97},{33,1},{65,33},{97,65},{2,98}... | collective-permute-start | bytes 884744 | tf_op jit(solution)/shard_map/ppermute | solution.py:303
  114.4 6.8 %copy-start = (bf16[4,16,32,128]{3,2,1,0:T(8,128)(2,1)}, bf16[4,16,32,128]{3,2,1,0:T(8,128)(2,1)S(1)}, u32[]{:S(2)}) copy-start(bf16[4,16,32,128]{3,2,1,0:T(8,128)(2,1)S(1)} %maximum_select_fusion.2.after) | copy-start | bytes 1572868
  114.5 35.3 %collective-permute-start.24 = (f32[448,256]{1,0:T(8,128)}, f32[448,256]{1,0:T(8,128)}, u32[]{:S(2)}, u32[]{:S(2)}) collective-permute-start(f32[448,256]{1,0:T(8,128)} %bitcast.12), channel_id=1, source_target_pairs={{0,1},{1,0},{2,3},{3,2},{4,5},{5,4},{6,7},{7,6},{8,9},{9,8},{10,11... | collective-permute-start | bytes 1376264 | tf_op jit(solution)/shard_map/ppermute | solution.py:300
  121.2 11.3 %collective-permute-start.18 = (bf16[2,9,64,128]{3,2,1,0:T(8,128)(2,1)S(1)}, bf16[2,9,64,128]{3,2,1,0:T(8,128)(2,1)S(1)}, u32[]{:S(2)}, u32[]{:S(2)}) collective-permute-start(bf16[2,9,64,128]{3,2,1,0:T(8,128)(2,1)S(1)} %get-tuple-element.42), channel_id=1, source_target_pairs={{0,32},{32,64},{64,96},{96,0},{1,33},{33,65},{65,97},{97,1},{2,34}... | collective-permute-start | bytes 884744 | tf_op jit(solution)/shard_map/ppermute | solution.py:303
  121.7 17.0 %collective-permute-start.19 = (bf16[2,9,64,128]{3,2,1,0:T(8,128)(2,1)S(1)}, bf16[2,9,64,128]{3,2,1,0:T(8,128)(2,1)S(1)}, u32[]{:S(2)}, u32[]{:S(2)}) collective-permute-start(bf16[2,9,64,128]{3,2,1,0:T(8,128)(2,1)S(1)} %get-tuple-element.43), channel_id=1, source_target_pairs={{0,64},{32,96},{64,0},{96,32},{1,65},{33,97},{65,1},{97,33},{2,66}... | collective-permute-start | bytes 884744 | tf_op jit(solution)/shard_map/ppermute | solution.py:303
  126.7 12.9 %collective-permute-start.20 = (bf16[2,9,64,128]{3,2,1,0:T(8,128)(2,1)S(1)}, bf16[2,9,64,128]{3,2,1,0:T(8,128)(2,1)S(1)}, u32[]{:S(2)}, u32[]{:S(2)}) collective-permute-start(bf16[2,9,64,128]{3,2,1,0:T(8,128)(2,1)S(1)} %get-tuple-element.44), channel_id=1, source_target_pairs={{0,96},{32,0},{64,32},{96,64},{1,97},{33,1},{65,33},{97,65},{2,98}... | collective-permute-start | bytes 884744 | tf_op jit(solution)/shard_map/ppermute | solution.py:303
  127.5 16.0 %collective-permute-start.21 = (bf16[2,9,32,128]{3,2,1,0:T(8,128)(2,1)S(1)}, bf16[2,9,32,128]{3,2,1,0:T(8,128)(2,1)S(1)}, u32[]{:S(2)}, u32[]{:S(2)}) collective-permute-start(bf16[2,9,32,128]{3,2,1,0:T(8,128)(2,1)S(1)} %get-tuple-element.46), channel_id=1, source_target_pairs={{0,16},{16,0},{1,17},{17,1},{2,18},{18,2},{3,19},{19,3},{4,20},{20... | collective-permute-start | bytes 442376 | tf_op jit(solution)/shard_map/ppermute | solution.py:297
  140.2 7.1 %collective-permute-start.22 = (bf16[2,9,32,128]{3,2,1,0:T(8,128)(2,1)S(1)}, bf16[2,9,32,128]{3,2,1,0:T(8,128)(2,1)S(1)}, u32[]{:S(2)}, u32[]{:S(2)}) collective-permute-start(bf16[2,9,32,128]{3,2,1,0:T(8,128)(2,1)S(1)} %get-tuple-element.47), channel_id=1, source_target_pairs={{0,16},{16,0},{1,17},{17,1},{2,18},{18,2},{3,19},{19,3},{4,20},{20... | collective-permute-start | bytes 442376 | tf_op jit(solution)/shard_map/ppermute | solution.py:297
  (5 other events, 23.4 us)

commit v2 on v1

v2 whole, which is shorter than its diff:
```python
import functools
import math

import jax
import jax.numpy as jnp
from jax import lax
from jax.experimental import pallas as pl
from jax.experimental.pallas import tpu as pltpu
from jax.sharding import Mesh
from jax.sharding import PartitionSpec as P

BF16 = jnp.bfloat16
F32 = jnp.float32
VMEM_LIMIT = 20 * 1024 * 1024
CHAN = ("y", "xh")
SPACE = ("z", "xl", "core")


def moved(value, step):
    if step == 0:
        return value
    size = value.shape[-1]
    lane = lax.broadcasted_iota(jnp.int32, value.shape, value.ndim - 1)
    rolled = pltpu.roll(value, step % size, value.ndim - 1)
    edge = 0 if step == 1 else size - 1
    return jnp.where(lane == edge, 0.0, rolled)


def pair_of(ref, plane, row):
    return jnp.concatenate([ref[plane, row], ref[plane, row + 1]], axis=1)


def starts_of(here_y):
    return [pl.multiple_of(lax.rem(here_y + shift, 4) * 64, 64) for shift in range(4)]


def forward_rows(row, places, kernel, bias, cot_own, cot_other, out_own, out_other, grad,
                 plane_cot, plane_out):
    outs = kernel.shape[1] // 3
    total = jnp.zeros((3 * outs, 256), F32)
    for a, (ref, plane) in enumerate(places):
        for b in range(3):
            total = total + jnp.dot(
                kernel[3 * a + b], pair_of(ref, plane, row + b), preferred_element_type=F32
            )
    for r in range(2):
        part = total[:, 128 * r : 128 * r + 128]
        pre = (
            moved(part[:outs], 1) + part[outs : 2 * outs] + moved(part[2 * outs :], -1)
            + bias[...]
        )
        sig = 1.0 / (1.0 + jnp.exp(-pre))
        out = (pre * sig).astype(BF16)
        out_own[plane_out, row + r] = out[: outs // 2]
        out_other[plane_out, row + r] = out[outs // 2 :]
        cot = jnp.concatenate(
            [cot_own[plane_cot, row + r], cot_other[plane_cot, row + r]], axis=0
        ).astype(F32)
        grad[plane_out, row + r] = (cot * sig * (1.0 + pre * (1.0 - sig))).astype(BF16)


def ready_body(at, kernel, bias, cotangent, after, kernel_out, cot_own, cot_sent):
    half = at[1]
    kernel_out[:27] = kernel[...]
    rest = bias[...]
    for k in range(3):
        part = rest.astype(BF16)
        kernel_out[27 + k // 2, :, 128 * (k % 2) : 128 * (k % 2) + 128] = part
        rest = rest - part.astype(F32)
    kernel_out[28, :, 128:] = jnp.zeros((32, 128), BF16)
    for plane in range(4):
        for row in range(8):
            cot_own[plane, row] = cotangent[plane, 8 * half + row]
            cot_sent[plane, row] = cotangent[plane, 8 - 8 * half + row]


def rims_body(at, own_lo, own_hi, left_lo, left_hi, right_lo, right_hi, far_lo, far_hi,
              kernel, cot, up_rim, down_rim):
    for k, (lower, upper) in enumerate(
        ((own_lo, own_hi), (right_lo, right_hi), (far_lo, far_hi), (left_lo, left_hi))
    ):
        up_rim[k] = upper[1]
        down_rim[k] = lower[0]


def inner_body(at, own_lo, own_hi, left_lo, left_hi, right_lo, right_hi, far_lo, far_hi,
               kernel_own, kernel_other, cot_own, cot_other, out_own, out_other, grad,
               field, kernel, bias):
    half, starts = at[1], starts_of(at[0])
    rows = own_lo.shape[1]

    def fill_kernel(ab, carry):
        for c in range(3):
            kernel[ab, 64 * c : 64 * c + 32] = kernel_own[3 * ab + c]
            kernel[ab, 64 * c + 32 : 64 * c + 64] = kernel_other[3 * ab + c]
        return carry

    lax.fori_loop(0, 9, fill_kernel, 0)
    for k, ref in enumerate((kernel_own, kernel_other)):
        bias[32 * k : 32 * k + 32] = (
            ref[27, :, :128].astype(F32) + ref[27, :, 128:].astype(F32)
        ) + ref[28, :, :128].astype(F32)
    sources = (own_lo, own_hi), (right_lo, right_hi), (far_lo, far_hi), (left_lo, left_hi)

    def fill(k, carry):
        for upper in range(2):
            plane = k + 2 * upper
            for row in range(rows):
                for start, pair in zip(starts, sources):
                    field[plane, row + 1 - half, pl.ds(start, 64), :] = pair[upper][k, row]
            field[plane, 9 * half] = jnp.zeros(field.shape[2:], BF16)
        return carry

    lax.fori_loop(0, 2, fill, 0)

    def step(index, carry):
        plane, row = index // 4, 2 * lax.rem(index, 4)
        forward_rows(
            row, [(field, plane), (field, plane + 1), (field, plane + 2)], kernel, bias,
            cot_own, cot_other, out_own, out_other, grad, plane + 1, plane,
        )
        return carry

    lax.fori_loop(0, 8, step, 0)


def outer_body(at, field, low, high, kernel, bias, cot_own, cot_other,
               in_own, in_other, in_grad, after, out_own, out_other, grad, first, last, rim):
    half, starts = at[1], starts_of(at[0])
    for side, ref in ((0, low), (1, high)):
        for row in range(ref.shape[1]):
            for k, start in enumerate(starts):
                rim[side, row + 1 - half, pl.ds(start, 64), :] = ref[k, row]
        rim[side, 9 * half] = jnp.zeros(rim.shape[2:], BF16)
    for plane in range(2):
        out_own[plane + 1] = in_own[plane]
        out_other[plane + 1] = in_other[plane]
        grad[plane + 1] = in_grad[plane]

    def step(index, carry):
        row = 2 * index
        forward_rows(
            row, [(rim, 0), (field, 0), (field, 1)], kernel, bias,
            cot_own, cot_other, out_own, out_other, grad, 0, 0,
        )
        forward_rows(
            row, [(field, 2), (field, 3), (rim, 1)], kernel, bias,
            cot_own, cot_other, out_own, out_other, grad, 3, 3,
        )
        for r in range(2):
            first[row + r] = grad[0, row + r]
            last[row + r] = grad[3, row + r]
        return carry

    lax.fori_loop(0, 4, step, 0)


def spread(line):
    wide = line.astype(F32)
    return [moved(wide, c - 1).astype(BF16) for c in range(3)]


def weight_sums(at, planes, grad_of, cells_of, store, stacked):
    rows, outs = stacked.shape[1], stacked.shape[2] // 3
    for k in range(planes):
        for row in range(rows):
            for c, line in enumerate(spread(grad_of(k, row))):
                stacked[k, row, outs * c : outs * (c + 1), :] = line
    for a in range(3):

        def step(b, carry):
            total = jnp.zeros((3 * outs, 256), F32)
            for k in range(planes):
                grads = jnp.concatenate([stacked[k, row] for row in range(rows)], axis=1)
                ref, plane = cells_of(k, a)
                cells = jnp.concatenate([ref[plane, row + b] for row in range(rows)], axis=1)
                total = total + lax.dot_general(
                    grads, cells, (((1,), (1,)), ((), ())), preferred_element_type=F32
                )
            for c in range(3):
                line = pl.multiple_of(16 * (9 * a + 3 * b + c), 16)
                for side in range(2):
                    low = outs * c + 32 * side
                    parts = total[low : low + 16], total[low + 16 : low + 32]
                    kept = jnp.where(at[2] == 0, parts[0], parts[1])
                    given = jnp.where(at[2] == 0, parts[1], parts[0])
                    store(side ^ at[1], pl.ds(line, 16), kept, given)
            return carry

        lax.fori_loop(0, 3, step, 0)


def inner_weight_body(at, field, grad, kernel, keep, give, turned, turned_edge, stacked):
    width = kernel.shape[1]
    wide = [kernel[ab] for ab in range(9)]
    for k in range(0, 8, 2):
        turned[:, width * k : width * (k + 2)] = jnp.concatenate(wide[k : k + 2], axis=0).T
    turned[:, 8 * width :] = wide[8].T
    beside = [
        jnp.where(at[1] == 0, kernel[3 * a + 2], kernel[3 * a]) for a in range(3)
    ]
    turned_edge[...] = jnp.concatenate(beside, axis=0).T

    def store(side, lines, kept, given):
        keep[side, lines, :] = kept
        give[side, lines, :] = given

    weight_sums(
        at, 2, lambda k, row: grad[k, row], lambda k, a: (field, k + a), store, stacked
    )


def outer_weight_body(at, field, rim, grad, in_keep, in_give, after, keep, give, stacked):
    for side in range(2):
        for ref in (keep, give):
            ref[side, 432:448, :] = jnp.zeros((16, 256), F32)

    def store(side, lines, kept, given):
        keep[side, lines, :] = kept + in_keep[side, lines, :]
        give[side, lines, :] = given + in_give[side, lines, :]

    places = [[(rim, 0), (field, 0), (field, 1)], [(field, 2), (field, 3), (rim, 1)]]
    weight_sums(
        at, 2, lambda k, row: grad[3 * k, row], lambda k, a: places[k][a], store, stacked
    )


def input_terms(at, lines, planes, turned, turned_edge, outs, stacked, held):
    half, starts = at[1], starts_of(at[0])
    rows, width = 8, stacked.shape[2] // 3
    for plane, line_of in enumerate(lines):
        for row in range(rows):
            for c, value in enumerate(spread(line_of(row))):
                stacked[plane, row + 1, width * c : width * (c + 1), :] = value
        for row in (0, 9):
            stacked[plane, row] = jnp.zeros(stacked.shape[2:], BF16)

    def store(places):
        for start, ref in zip(starts, outs):
            block = held[pl.ds(start, 64), :]
            for r, (plane, row) in enumerate(places):
                ref[plane, row] = block[:, 128 * r : 128 * r + 128].astype(ref.dtype)

    def step(index, carry):
        row = 2 * index
        for first, plane in planes:
            terms = jnp.concatenate(
                [
                    pair_of(stacked, first + 2 - a, row + 2 - b)
                    for a in range(3)
                    for b in range(3)
                ],
                axis=0,
            )
            held[...] = jnp.dot(turned[...], terms, preferred_element_type=F32)
            store([(plane, row), (plane, row + 1)])
        return carry

    lax.fori_loop(0, rows // 2, step, 0)
    nearest = 8 - 7 * half
    terms = jnp.concatenate(
        [
            jnp.concatenate([stacked[first + 2 - a, nearest] for first, _ in planes], axis=1)
            for a in range(3)
        ],
        axis=0,
    )
    held[...] = jnp.dot(turned_edge[...], terms, preferred_element_type=F32)
    store([(plane, rows) for _, plane in planes])


def inner_input_body(at, grad, turned, turned_edge, own, near, far, back, stacked, held):
    lines = [lambda row, k=k: grad[k, row] for k in range(4)]
    input_terms(
        at, lines, [(0, 0), (1, 1)], turned, turned_edge, (own, near, far, back), stacked, held
    )


def outer_input_body(at, grad, low, high, turned, turned_edge, *refs):
    given, outs, (stacked, held) = refs[:4], refs[4:8], refs[8:]
    for source, ref in zip(given, outs):
        for plane in range(2):
            ref[plane + 1] = source[plane]
    lines = [lambda row, k=k: grad[k, row] for k in range(4)]
    lines = [lambda row: low[row]] + lines + [lambda row: high[row]]
    input_terms(at, lines, [(0, 0), (3, 3)], turned, turned_edge, outs, stacked, held)


def total_body(at, own, near, far, back, kept, sent):
    half = at[1]
    mine = pl.multiple_of(32 * half, 32)
    others = pl.multiple_of(32 * (1 - half), 32)

    def sums(plane, row, start):
        value = own[plane, row, pl.ds(start, 32), :]
        for ref in (near, far, back):
            value = value + ref[plane, row, pl.ds(start, 32), :].astype(F32)
        return value

    for plane in range(4):
        for row in range(9):
            kept[plane, row] = sums(plane, row, mine)
            sent[plane, row] = sums(plane, row, others).astype(BF16)


def join_body(at, kept, got, joined):
    half = at[1]
    for plane in range(4):
        for row in range(8):
            joined[plane, 8 * half + row] = kept[plane, row].astype(BF16)
            joined[plane, 8 - 8 * half + row] = got[plane, row]
        beside = 7 * (1 - half)
        joined[plane, 8 * half + beside] = (
            kept[plane, beside] + got[plane, 8].astype(F32)
        ).astype(BF16)
        beyond = 7 * half
        joined[plane, 8 - 8 * half + beyond] = (
            kept[plane, 8] + got[plane, beyond].astype(F32)
        ).astype(BF16)


def add_body(at, keep, got, chip):
    chip[...] = keep[...] + got[...]


def mean_body(at, pieces, copies):
    total = pieces[0]
    for k in range(1, pieces.shape[0]):
        total = total + pieces[k]
    total = total * (1.0 / math.sqrt(64 * 16 * 128))
    for k in range(copies.shape[0]):
        copies[k] = total


def weave_body(at, mine, other, joined):
    core = at[2]
    for tap in range(27):
        first, second = (ref[16 * tap : 16 * tap + 16] for ref in (mine, other))
        joined[tap, :16] = jnp.where(core == 0, first, second)
        joined[tap, 16:] = jnp.where(core == 0, second, first)


def call(body, n_in, outs, scratch, flops, after=0):
    vmem = pl.BlockSpec(memory_space=pltpu.VMEM)
    anywhere = pl.BlockSpec(memory_space=pl.ANY)
    return pl.pallas_call(
        body,
        out_shape=[jax.ShapeDtypeStruct(*out) for out in outs],
        in_specs=[pl.BlockSpec(memory_space=pltpu.SMEM)]
        + [vmem] * (n_in - 1)
        + [anywhere] * after,
        out_specs=[vmem] * len(outs),
        scratch_shapes=scratch,
        compiler_params=pltpu.CompilerParams(vmem_limit_bytes=VMEM_LIMIT),
        cost_estimate=pl.CostEstimate(
            flops=flops, bytes_accessed=8 * 2**20, transcendentals=2**18
        ),
    )


def on_device(volume, kernel, bias, cotangent):
    here_y, half, core = lax.axis_index("y"), lax.axis_index("xh"), lax.axis_index("core")
    at = jnp.stack([here_y, half, core]).astype(jnp.int32)

    def swap(value):
        return lax.ppermute(value, "xh", [(0, 1), (1, 0)])

    def swap_core(value):
        return lax.ppermute(value, "core", [(0, 1), (1, 0)])

    def turn(value, step):
        return lax.ppermute(value, "y", [(i, (i + step) % 4) for i in range(4)])

    def up(value):
        return lax.ppermute(value, SPACE, [(i, i + 1) for i in range(15)])

    def down(value):
        return lax.ppermute(value, SPACE, [(i + 1, i) for i in range(15)])

    mine = lax.dynamic_slice_in_dim(volume, 7 * half, 9, axis=1)
    got = swap(lax.dynamic_slice_in_dim(volume, 7 * (1 - half), 9, axis=1))
    own_lo, own_hi = (
        jnp.where(
            half == 0,
            jnp.concatenate([mine[k : k + 2], got[k : k + 2]], axis=2),
            jnp.concatenate([got[k : k + 2], mine[k : k + 2]], axis=2),
        )
        for k in (0, 2)
    )
    left_lo, right_hi = turn(own_lo, 1), turn(own_hi, -1)
    left_hi, right_lo = turn(own_hi, 1), turn(own_lo, -1)
    far_lo, far_hi = turn(left_lo, 1), turn(right_hi, -1)
    kernel_sent, cot_own, cot_sent = call(
        ready_body, 4,
        [((29, 32, 256), BF16), ((4, 8, 32, 128), BF16), ((4, 8, 32, 128), BF16)],
        [], 10**6, 1,
    )(at, kernel, jnp.broadcast_to(bias[:, None], (32, 128)), cotangent, own_lo)
    kernel_other, cot_other = swap(kernel_sent), swap(cot_sent)
    up_rim, down_rim = call(rims_body, 9, [((4, 9, 64, 128), BF16)] * 2, [], 10**6, 2)(
        at, own_lo, own_hi, left_lo, left_hi, right_lo, right_hi, far_lo, far_hi,
        kernel_other, cot_other,
    )
    low, high = up(up_rim), down(down_rim)

    flops = 36 * 10**8
    out_own, out_other, grad, field, taps, bias_wide = call(
        inner_body, 13,
        [
            ((2, 8, 32, 128), BF16), ((2, 8, 32, 128), BF16), ((2, 8, 64, 128), BF16),
            ((4, 10, 256, 128), BF16), ((9, 192, 256), BF16),
            ((64, 128), F32),
        ],
        [], flops // 2,
    )(at, own_lo, own_hi, left_lo, left_hi, right_lo, right_hi, far_lo, far_hi,
      kernel_sent, kernel_other, cot_own, cot_other)
    keep, give, turned, turned_edge = call(
        inner_weight_body, 4,
        [((2, 448, 256), F32)] * 2 + [((256, 1728), BF16), ((256, 576), BF16)],
        [pltpu.VMEM((2, 8, 192, 128), BF16)], flops // 2,
    )(at, field, grad, taps)
    out_own, out_other, grad, first, last, rim = call(
        outer_body, 11,
        [
            ((4, 8, 32, 128), BF16), ((4, 8, 32, 128), BF16), ((4, 8, 64, 128), BF16),
            ((8, 64, 128), BF16), ((8, 64, 128), BF16), ((2, 10, 256, 128), BF16),
        ],
        [], flops // 2, 1,
    )(at, field, low, high, taps, bias_wide, cot_own, cot_other,
      out_own, out_other, grad, keep)

    got_out = swap(out_other)
    output = jnp.where(
        half == 0,
        jnp.concatenate([out_own, got_out], axis=1),
        jnp.concatenate([got_out, out_own], axis=1),
    )
    grad_low, grad_high = up(last), down(first)

    def input_chunk(chunk, rim):
        return call(
            functools.partial(input_body, chunk), 5,
            [((2, 9, 64, 128), F32)] + [((2, 9, 64, 128), BF16)] * 3,
            [pltpu.VMEM((4, 10, 192, 128), BF16), pltpu.VMEM((256, 256), F32)],
            flops // 2,
        )(at, grad, rim, turned, turned_edge)

    def total_chunk(own, near, far, back):
        near, back, far = turn(near, 1), turn(back, -1), turn(far, 2)
        kept, sent = call(
            total_body, 5, [((2, 9, 32, 128), F32), ((2, 9, 32, 128), BF16)], [], 10**6
        )(at, own, near, far, back)
        return kept, sent, swap(sent)

    def input_shapes(planes):
        return [((planes, 9, 64, 128), F32)] + [((planes, 9, 64, 128), BF16)] * 3

    def input_scratch(planes):
        return [pltpu.VMEM((planes, 10, 192, 128), BF16), pltpu.VMEM((256, 256), F32)]

    parts = call(
        inner_input_body, 4, input_shapes(2), input_scratch(4), flops // 2
    )(at, grad, turned, turned_edge)
    own, near, far, back = call(
        outer_input_body, 10, input_shapes(4), input_scratch(6), flops // 2
    )(at, grad, grad_low, grad_high, turned, turned_edge, *parts)
    keep, give = call(
        outer_weight_body, 6, [((2, 448, 256), F32)] * 2,
        [pltpu.VMEM((2, 8, 192, 128), BF16)], flops // 2, 1,
    )(at, field, rim, grad, keep, give, near)
    near, back, far = turn(near, 1), turn(back, -1), turn(far, 2)
    kept, sent = call(
        total_body, 5, [((4, 9, 32, 128), F32), ((4, 9, 32, 128), BF16)], [], 10**6
    )(at, own, near, far, back)
    got = swap(sent)
    (chip,) = call(add_body, 3, [((2, 448, 256), F32)], [], 10**6)(
        at, keep, swap_core(give)
    )
    pieces = lax.all_to_all(
        chip.reshape(16, 56, 256), ("xh", "z", "xl"), 0, 0, tiled=True
    )
    (copies,) = call(mean_body, 2, [((8, 56, 256), F32)], [], 10**6)(at, pieces)
    everyone = lax.all_to_all(copies, ("z", "xl"), 0, 0, tiled=True).reshape(448, 256)
    (weight_grad,) = call(weave_body, 3, [((27, 32, 256), F32)], [], 10**6)(
        at, everyone, swap_core(everyone)
    )
    (input_grad,) = call(join_body, 3, [((4, 16, 32, 128), BF16)], [], 10**6)(at, kept, got)
    return output, input_grad, weight_grad


def solution(mesh):
    split = Mesh(mesh.devices.reshape(4, 2, 4, 2, 2), CHAN + SPACE)
    return jax.shard_map(
        on_device,
        mesh=split,
        in_specs=(
            P(SPACE, None, CHAN, None),
            P(None, CHAN, None),
            P(CHAN),
            P(SPACE, None, CHAN, None),
        ),
        out_specs=(
            P(SPACE, None, CHAN, None),
            P(SPACE, None, CHAN, None),
            P(None, CHAN, None),
        ),
        check_vma=False,
    )
```

time: 153 us -> 143 us (0.935)
  starting transfers between devices: 65 us -> 45.5 us
  blocking collectives: 0 us -> 11.1 us
  waiting for transfers between devices: 38.4 us -> 44.6 us
  local copies, waits for them, and re-layouts: 9.62 us -> 3.61 us
  other arithmetic: 4.87 us -> 1.15 us
  Pallas kernels: 32.8 us -> 35.8 us
    all_to_all x0 -> x1, blocking collectives: none -> 11.1 us  [on_device(): lax.all_to_all(copies, ('z', 'xl'), 0, 0, tiled=True).reshape(448, 256)]
    ppermute x10 -> x9, starting transfers between devices: 15.8 us -> 9.39 us  [turn(): return lax.ppermute(value, 'y', [(i, (i + step) % 4) for i in range(4)])]
    ppermute x7 -> x5, starting transfers between devices: 16.2 us -> 10.1 us  [swap(): return lax.ppermute(value, 'xh', [(0, 1), (1, 0)])]
    all_to_all x2 -> x1, starting transfers between devices: 13.9 us -> 8.28 us  [on_device(): lax.all_to_all(chip.reshape(16, 56, 256), ('xh', 'z', 'xl'), 0, 0, tiled=...]
    ppermute x3 -> x2, starting transfers between devices: 8.83 us -> 4.33 us  [down(): return lax.ppermute(value, SPACE, [(i + 1, i) for i in range(15)])]
    slice x7 -> x2, local copies, waits for them, and re-layouts: 4.84 us -> 1.02 us  [the longest x1 1 us: on_device(): mine[k:k + 2]]
    ppermute x10 -> x9, waiting for transfers between devices: 8.85 us -> 5.09 us  [turn(): return lax.ppermute(value, 'y', [(i, (i + step) % 4) for i in range(4)])]
    ppermute x7 -> x5, waiting for transfers between devices: 17.7 us -> 21.4 us  [swap(): return lax.ppermute(value, 'xh', [(0, 1), (1, 0)])]
  transfers between devices with their start and end apart: 27 -> 21, of which waited for: 9 -> 11; matrix products, arithmetic and copies ran while one was open for 6% -> 1% of each run, Pallas kernels for 13% -> 13%
where the time goes in v2:
time: 143 us
  starting transfers between devices  45.5 us (32%)
  waiting for transfers between devices  44.6 us (31%)
  Pallas kernels  35.8 us (25%)
  blocking collectives  11.1 us (8%)
  local copies, waits for them, and re-layouts  3.61 us (3%)
    ppermute x5, waiting for transfers between devices, swap(): return lax.ppermute(value, 'xh', [(0, 1), (1, 0)])  21.4 us
    all_to_all x1, waiting for transfers between devices, on_device(): lax.all_to_all(chip.reshape(16, 56, 256), ('xh', 'z', 'xl'), 0, 0, tiled=...  13 us
    all_to_all x1, blocking collectives, on_device(): lax.all_to_all(copies, ('z', 'xl'), 0, 0, tiled=True).reshape(448, 256)  11.1 us
    ppermute x2, starting transfers between devices, up(): return lax.ppermute(value, SPACE, [(i, i + 1) for i in range(15)])  10.7 us
    ppermute x5, starting transfers between devices, swap(): return lax.ppermute(value, 'xh', [(0, 1), (1, 0)])  10.1 us
    ppermute x9, starting transfers between devices, turn(): return lax.ppermute(value, 'y', [(i, (i + step) % 4) for i in range(4)])  9.39 us
    all_to_all x1, starting transfers between devices, on_device(): lax.all_to_all(chip.reshape(16, 56, 256), ('xh', 'z', 'xl'), 0, 0, tiled=...  8.28 us
    pallas_call x1, Pallas kernels, on_device(): call(inner_weight_body, 4, [((2, 448, 256), F32)] * 2 + [((256, 1728), BF...  5.54 us
  transfers between devices with their start and end apart: 21, of which 11 were waited for; matrix products, arithmetic and copies ran while one was open for 1% of the time, Pallas kernels for 13%

profile of v2, /device:TPU:1, one launch (start us, length us, event | category | flops | bytes accessed | tf_op | source)
XLA Modules:
  0.0 142.7 jit_solution(11267895343838521738)
XLA Ops:
  1.7 3.7 %collective-permute-start = (bf16[4,9,32,128]{3,2,1,0:T(8,128)(2,1)S(1)}, bf16[4,9,32,128]{3,2,1,0:T(8,128)(2,1)S(1)}, u32[]{:S(2)}, u32[]{:S(2)}) collective-permute-start(bf16[4,9,32,128]{3,2,1,0:T(8,128)(2,1)S(1)} %constant_dynamic-slice_fusion.1), channel_id=1, source_target_pairs={{0,16},{16,0},{1,17},{17,1},{2,18},{18,2},{3,19},{19,3},{4,20},{20... | collective-permute-start | bytes 884744 | tf_op jit(solution)/shard_map/ppermute | solution.py:366
  6.3 5.3 %collective-permute-done = bf16[4,9,32,128]{3,2,1,0:T(8,128)(2,1)S(1)} collective-permute-done((bf16[4,9,32,128]{3,2,1,0:T(8,128)(2,1)S(1)}, bf16[4,9,32,128]{3,2,1,0:T(8,128)(2,1)S(1)}, u32[]{:S(2)}, u32[]{:S(2)}) %collective-permute-start) | collective-permute-done | bytes 294944 | tf_op jit(solution)/shard_map/ppermute | solution.py:366
  11.7 1.7 %collective-permute-start.1 = (bf16[2,9,64,128]{3,2,1,0:T(8,128)(2,1)S(1)}, bf16[2,9,64,128]{3,2,1,0:T(8,128)(2,1)S(1)}, u32[]{:S(2)}, u32[]{:S(2)}) collective-permute-start(bf16[2,9,64,128]{3,2,1,0:T(8,128)(2,1)S(1)} %maximum_select_fusion.1.after.own_lo), channel_id=1, source_target_pairs={{0,32},{32,64},{64,96},{96,0},{1,33},{33,65},{65,97},{97,1},{2,34}... | collective-permute-start | bytes 884744 | tf_op jit(solution)/shard_map/ppermute | solution.py:372
  13.6 1.5 %collective-permute-start.4 = (bf16[2,9,64,128]{3,2,1,0:T(8,128)(2,1)S(1)}, bf16[2,9,64,128]{3,2,1,0:T(8,128)(2,1)S(1)}, u32[]{:S(2)}, u32[]{:S(2)}) collective-permute-start(bf16[2,9,64,128]{3,2,1,0:T(8,128)(2,1)S(1)} %maximum_select_fusion.2.own_hi), channel_id=1, source_target_pairs={{0,96},{32,0},{64,32},{96,64},{1,97},{33,1},{65,33},{97,65},{2,98}... | collective-permute-start | bytes 884744 | tf_op jit(solution)/shard_map/ppermute | solution.py:372
  15.9 2.8 %collective-permute-start.8 = (bf16[4,8,32,128]{3,2,1,0:T(8,128)(2,1)S(1)}, bf16[4,8,32,128]{3,2,1,0:T(8,128)(2,1)S(1)}, u32[]{:S(2)}, u32[]{:S(2)}) collective-permute-start(bf16[4,8,32,128]{3,2,1,0:T(8,128)(2,1)S(1)} %get-tuple-element.38), channel_id=1, source_target_pairs={{0,16},{16,0},{1,17},{17,1},{2,18},{18,2},{3,19},{19,3},{4,20},{20... | collective-permute-start | bytes 786440 | tf_op jit(solution)/shard_map/ppermute | solution.py:366
  18.9 1.5 %collective-permute-start.3 = (bf16[2,9,64,128]{3,2,1,0:T(8,128)(2,1)S(1)}, bf16[2,9,64,128]{3,2,1,0:T(8,128)(2,1)S(1)}, u32[]{:S(2)}, u32[]{:S(2)}) collective-permute-start(bf16[2,9,64,128]{3,2,1,0:T(8,128)(2,1)S(1)} %maximum_select_fusion.1.after.own_lo), channel_id=1, source_target_pairs={{0,96},{32,0},{64,32},{96,64},{1,97},{33,1},{65,33},{97,65},{2,98}... | collective-permute-start | bytes 884744 | tf_op jit(solution)/shard_map/ppermute | solution.py:372
  20.4 3.1 %collective-permute-done.8.cot_other.cot = bf16[4,8,32,128]{3,2,1,0:T(8,128)(2,1)S(1)} collective-permute-done((bf16[4,8,32,128]{3,2,1,0:T(8,128)(2,1)S(1)}, bf16[4,8,32,128]{3,2,1,0:T(8,128)(2,1)S(1)}, u32[]{:S(2)}, u32[]{:S(2)}) %collective-permute-start.8) | collective-permute-done | bytes 262176 | tf_op jit(solution)/shard_map/ppermute | solution.py:366
  24.5 1.7 %collective-permute-start.6 = (bf16[2,9,64,128]{3,2,1,0:T(8,128)(2,1)S(1)}, bf16[2,9,64,128]{3,2,1,0:T(8,128)(2,1)S(1)}, u32[]{:S(2)}, u32[]{:S(2)}) collective-permute-start(bf16[2,9,64,128]{3,2,1,0:T(8,128)(2,1)S(1)} %collective-permute-done.4.right_hi), channel_id=1, source_target_pairs={{0,96},{32,0},{64,32},{96,64},{1,97},{33,1},{65,33},{97,65},{2,98}... | collective-permute-start | bytes 884744 | tf_op jit(solution)/shard_map/ppermute | solution.py:372
  27.1 3.4 %collective-permute-done.2.left_hi = bf16[2,9,64,128]{3,2,1,0:T(8,128)(2,1)S(1)} collective-permute-done((bf16[2,9,64,128]{3,2,1,0:T(8,128)(2,1)S(1)}, bf16[2,9,64,128]{3,2,1,0:T(8,128)(2,1)S(1)}, u32[]{:S(2)}, u32[]{:S(2)}) %collective-permute-start.2) | collective-permute-done | bytes 294944 | tf_op jit(solution)/shard_map/ppermute | solution.py:372
  30.5 3.1 %collective-permute-done.7.kernel_other.kernel = bf16[29,32,256]{2,1,0:T(8,128)(2,1)S(1)} collective-permute-done((bf16[29,32,256]{2,1,0:T(8,128)(2,1)S(1)}, bf16[29,32,256]{2,1,0:T(8,128)(2,1)S(1)}, u32[]{:S(2)}, u32[]{:S(2)}) %collective-permute-start.7) | collective-permute-done | bytes 475168 | tf_op jit(solution)/shard_map/ppermute | solution.py:366
  35.0 8.8 %collective-permute-start.9 = (bf16[4,9,64,128]{3,2,1,0:T(8,128)(2,1)S(1)}, bf16[4,9,64,128]{3,2,1,0:T(8,128)(2,1)S(1)}, u32[]{:S(2)}, u32[]{:S(2)}) collective-permute-start(bf16[4,9,64,128]{3,2,1,0:T(8,128)(2,1)S(1)} %get-tuple-element.40), channel_id=1, source_target_pairs={{0,1},{1,2},{2,3},{3,4},{4,5},{5,6},{6,7},{7,8},{8,9},{9,10},{10,1... | collective-permute-start | bytes 1769480 | tf_op jit(solution)/shard_map/ppermute | solution.py:375
  43.8 1.9 %collective-permute-start.10 = (bf16[4,9,64,128]{3,2,1,0:T(8,128)(2,1)S(1)}, bf16[4,9,64,128]{3,2,1,0:T(8,128)(2,1)S(1)}, u32[]{:S(2)}, u32[]{:S(2)}) collective-permute-start(bf16[4,9,64,128]{3,2,1,0:T(8,128)(2,1)S(1)} %get-tuple-element.41), channel_id=1, source_target_pairs={{1,0},{2,1},{3,2},{4,3},{5,4},{6,5},{7,6},{8,7},{9,8},{10,9},{11,1... | collective-permute-start | bytes 1769480 | tf_op jit(solution)/shard_map/ppermute | solution.py:378
  45.8 5.0 %shard_map.68 = (bf16[2,8,32,128]{3,2,1,0:T(8,128)(2,1)S(1)}, bf16[2,8,32,128]{3,2,1,0:T(8,128)(2,1)S(1)}, bf16[2,8,64,128]{3,2,1,0:T(8,128)(2,1)S(1)}, bf16[4,1...) custom-call(s32[3]{0:T(128)S(1)} %pad_add_fusion.at, ...), custom_call_target="tpu_custom_call" | custom-call | flops 1800000000 | bytes 8388608 | tf_op jit(solution)/shard_map/pallas_call | solution.py:406
  50.8 5.5 %shard_map.70 = (f32[2,448,256]{2,1,0:T(8,128)S(1)}, f32[2,448,256]{2,1,0:T(8,128)S(1)}, bf16[256,1728]{1,0:T(8,128)(2,1)S(1)}, bf16[256,576]{1,0:T(8,128)(2,1)S(1)}) custom-call(s32[3]{0:T(128)S(1)} %pad_add_fusion.at, bf16[4,10,256,128]{3,2,1,0:T(8,128)(2,1)S(1)} %get-tuple-element.39.field, bf16[2,8,64,128]{3,2,1,0:T(8,128)(2,1)S(1)} %get-tuple-element.46.grad.in_grad, ...), custom_call_target="tpu_custom_call" | custom-call | flops 1800000000 | bytes 8388608 | tf_op jit(solution)/shard_map/pallas_call | solution.py:416
  56.4 2.6 %collective-permute-done.10.high = bf16[4,9,64,128]{3,2,1,0:T(8,128)(2,1)S(1)} collective-permute-done((bf16[4,9,64,128]{3,2,1,0:T(8,128)(2,1)S(1)}, bf16[4,9,64,128]{3,2,1,0:T(8,128)(2,1)S(1)}, u32[]{:S(2)}, u32[]{:S(2)}) %collective-permute-start.10) | collective-permute-done | bytes 589856 | tf_op jit(solution)/shard_map/ppermute | solution.py:378
  59.0 3.8 %shard_map.71 = (bf16[4,8,32,128]{3,2,1,0:T(8,128)(2,1)S(1)}, bf16[4,8,32,128]{3,2,1,0:T(8,128)(2,1)S(1)}, bf16[4,8,64,128]{3,2,1,0:T(8,128)(2,1)S(1)}, bf16[8,6...) custom-call(s32[3]{0:T(128)S(1)} %pad_add_fusion.at, ...), custom_call_target="tpu_custom_call" | custom-call | flops 1800000000 | bytes 8388608 | tf_op jit(solution)/shard_map/pallas_call | solution.py:421
  63.6 1.9 %collective-permute-start.12 = (bf16[8,64,128]{2,1,0:T(8,128)(2,1)S(1)}, bf16[8,64,128]{2,1,0:T(8,128)(2,1)S(1)}, u32[]{:S(2)}, u32[]{:S(2)}) collective-permute-start(bf16[8,64,128]{2,1,0:T(8,128)(2,1)S(1)} %get-tuple-element.51), channel_id=1, source_target_pairs={{0,1},{1,2},{2,3},{3,4},{4,5},{5,6},{6,7},{7,8},{8,9},{9,10},{10,1... | collective-permute-start | bytes 393224 | tf_op jit(solution)/shard_map/ppermute | solution.py:375
  65.5 2.4 %collective-permute-start.13 = (bf16[8,64,128]{2,1,0:T(8,128)(2,1)S(1)}, bf16[8,64,128]{2,1,0:T(8,128)(2,1)S(1)}, u32[]{:S(2)}, u32[]{:S(2)}) collective-permute-start(bf16[8,64,128]{2,1,0:T(8,128)(2,1)S(1)} %get-tuple-element.52), channel_id=1, source_target_pairs={{1,0},{2,1},{3,2},{4,3},{5,4},{6,5},{7,6},{8,7},{9,8},{10,9},{11,1... | collective-permute-start | bytes 393224 | tf_op jit(solution)/shard_map/ppermute | solution.py:378
  67.9 4.1 %shard_map.72 = (f32[2,9,64,128]{3,2,1,0:T(8,128)S(1)}, bf16[2,9,64,128]{3,2,1,0:T(8,128)(2,1)S(1)}, bf16[2,9,64,128]{3,2,1,0:T(8,128)(2,1)S(1)}, bf16[2,9,64,128]{3,2,1,0:T(8,128)(2,1)S(1)}) custom-call(s32[3]{0:T(128)S(1)} %pad_add_fusion.at, bf16[4,8,64,128]{3,2,1,0:T(8,128)(2,1)S(1)} %get-tuple-element.50.grad, ...), custom_call_target="tpu_custom_call" | custom-call | flops 1800000000 | bytes 8388608 | tf_op jit(solution)/shard_map/pallas_call | solution.py:460
  72.0 4.3 %shard_map.73 = (f32[4,9,64,128]{3,2,1,0:T(8,128)S(1)}, bf16[4,9,64,128]{3,2,1,0:T(8,128)(2,1)S(1)}, bf16[4,9,64,128]{3,2,1,0:T(8,128)(2,1)S(1)}, bf16[4,9,64,128]{3,2,1,0:T(8,128)(2,1)S(1)}) custom-call(s32[3]{0:T(128)S(1)} %pad_add_fusion.at, bf16[4,8,64,128]{3,2,1,0:T(8,128)(2,1)S(1)} %get-tuple-element.50.grad, ...), custom_call_target="tpu_custom_call" | custom-call | flops 1800000000 | bytes 8388608 | tf_op jit(solution)/shard_map/pallas_call | solution.py:463
  77.1 5.3 %shard_map.76 = (f32[2,448,256]{2,1,0:T(8,128)S(1)}, f32[2,448,256]{2,1,0:T(8,128)S(1)}) custom-call(s32[3]{0:T(128)S(1)} %pad_add_fusion.at, bf16[4,10,256,128]{3,2,1,0:T(8,128)(2,1)S(1)} %get-tuple-element.39.field, bf16[2,10,256,128]{3,2,1,0:T(8,128)(2,1)S(1)} %get-tuple-element.65.rim, bf16[4,8,64,128]{3,2,1,0:T(8,128)(2,1)S(1)} %get-tuple-element.50.grad, ...), custom_call_target="tpu_custom_call" | custom-call | flops 1800000000 | bytes 8388608 | tf_op jit(solution)/shard_map/pallas_call | solution.py:466
  82.4 2.5 %collective-permute-done.18.got = f32[2,448,256]{2,1,0:T(8,128)S(1)} collective-permute-done((f32[2,448,256]{2,1,0:T(8,128)S(1)}, f32[2,448,256]{2,1,0:T(8,128)S(1)}, u32[]{:S(2)}, u32[]{:S(2)}) %collective-permute-start.18) | collective-permute-done | bytes 917536 | tf_op jit(solution)/shard_map/ppermute | solution.py:369
  84.9 1.6 %shard_map.77 = f32[2,448,256]{2,1,0:T(8,128)} custom-call(s32[3]{0:T(128)S(1)} %pad_add_fusion.at, f32[2,448,256]{2,1,0:T(8,128)S(1)} %get-tuple-element.67.keep, f32[2,448,256]{2,1,0:T(8,128)S(1)} %collective-permute-done.18.got), custom_call_target="tpu_custom_call" | custom-call | flops 1000000 | bytes 8388608 | tf_op jit(solution)/shard_map/pallas_call | solution.py:475
  86.5 8.3 %all-to-all-start = ((f32[16,56,256]{2,1,0:T(8,128)}), f32[16,56,256]{2,1,0:T(8,128)S(1)}, u32[]{:S(2)}, u32[]{:S(2)}) async-start(f32[16,56,256]{2,1,0:T(8,128)} %bitcast.3), calls=%async_computation | async-start | bytes 1835008 | tf_op jit(solution)/shard_map/all_to_all | solution.py:478
  96.7 13.0 %all-to-all-done.pieces = f32[16,56,256]{2,1,0:T(8,128)S(1)} async-done(((f32[16,56,256]{2,1,0:T(8,128)}), f32[16,56,256]{2,1,0:T(8,128)S(1)}, u32[]{:S(2)}, u32[]{:S(2)}) %all-to-all-start) | async-done | bytes 917536 | tf_op jit(solution)/shard_map/all_to_all | solution.py:478
  110.3 11.1 %all_to_all.10 = f32[8,56,256]{2,1,0:T(8,128)S(1)} all-to-all(f32[8,56,256]{2,1,0:T(8,128)S(1)} %shard_map.78), channel_id=1, replica_groups=mesh['y'=4,'xh'=2,'z'=4,'xl'=2,'core'=2] {'z','xl'}, dimensions={0} | all-to-all | bytes 917504 | tf_op jit(solution)/shard_map/all_to_all | solution.py:482
  121.4 2.6 %collective-permute-start.19 = (f32[448,256]{1,0:T(8,128)S(1)}, f32[448,256]{1,0:T(8,128)S(1)}, u32[]{:S(2)}, u32[]{:S(2)}) collective-permute-start(f32[448,256]{1,0:T(8,128)S(1)} %bitcast.5), channel_id=1, source_target_pairs={{0,1},{1,0},{2,3},{3,2},{4,5},{5,4},{6,7},{7,6},{8,9},{9,8},{10,11... | collective-permute-start | bytes 1376264 | tf_op jit(solution)/shard_map/ppermute | solution.py:369
  124.0 2.0 %collective-permute-start.11 = (bf16[4,8,32,128]{3,2,1,0:T(8,128)(2,1)S(1)}, bf16[4,8,32,128]{3,2,1,0:T(8,128)(2,1)S(1)}, u32[]{:S(2)}, u32[]{:S(2)}) collective-permute-start(bf16[4,8,32,128]{3,2,1,0:T(8,128)(2,1)S(1)} %copy-done.5), channel_id=1, source_target_pairs={{0,16},{16,0},{1,17},{17,1},{2,18},{18,2},{3,19},{19,3},{4,20},{20... | collective-permute-start | bytes 786440 | tf_op jit(solution)/shard_map/ppermute | solution.py:366
  126.0 1.5 %shard_map.74 = (f32[4,9,32,128]{3,2,1,0:T(8,128)S(1)}, bf16[4,9,32,128]{3,2,1,0:T(8,128)(2,1)S(1)}) custom-call(s32[3]{0:T(128)S(1)} %pad_add_fusion.at, f32[4,9,64,128]{3,2,1,0:T(8,128)S(1)} %get-tuple-element.59.own, bf16[4,9,64,128]{3,2,1,0:T(8,128)(2,1)} %collective-permute-done.14.near, bf16[4,9,64,128]{3,2,1,0:T(8,128)(2,1)S(1)} %collective-permute-done.15.far, ...), custom_call_target="tpu_custom_call" | custom-call | flops 1000000 | bytes 8388608 | tf_op jit(solution)/shard_map/pallas_call | solution.py:471
  129.0 4.5 %collective-permute-done.11 = bf16[4,8,32,128]{3,2,1,0:T(8,128)(2,1)S(1)} collective-permute-done((bf16[4,8,32,128]{3,2,1,0:T(8,128)(2,1)S(1)}, bf16[4,8,32,128]{3,2,1,0:T(8,128)(2,1)S(1)}, u32[]{:S(2)}, u32[]{:S(2)}) %collective-permute-start.11) | collective-permute-done | bytes 262176 | tf_op jit(solution)/shard_map/ppermute | solution.py:366
  134.3 5.5 %collective-permute-done.17.got = bf16[4,9,32,128]{3,2,1,0:T(8,128)(2,1)S(1)} collective-permute-done((bf16[4,9,32,128]{3,2,1,0:T(8,128)(2,1)S(1)}, bf16[4,9,32,128]{3,2,1,0:T(8,128)(2,1)S(1)}, u32[]{:S(2)}, u32[]{:S(2)}) %collective-permute-start.17) | collective-permute-done | bytes 294944 | tf_op jit(solution)/shard_map/ppermute | solution.py:366
  141.2 1.5 %shard_map.79 = f32[27,32,256]{2,1,0:T(8,128)} custom-call(s32[3]{0:T(128)S(1)} %pad_add_fusion.at, f32[448,256]{1,0:T(8,128)S(1)} %bitcast.6, f32[448,256]{1,0:T(8,128)S(1)} %collective-permute-done.19.other), custom_call_target="tpu_custom_call" | custom-call | flops 1000000 | bytes 8388608 | tf_op jit(solution)/shard_map/pallas_call | solution.py:483
  (46 shorter events, 14.4 us)
Async XLA Ops:
  1.6 13.6 %copy-start.6 = (f32[32]{0:T(128)S(1)}, f32[32]{0:T(128)}, u32[]{:S(2)}) copy-start(f32[32]{0:T(128)} %param.6) | copy-start | bytes 388
  1.6 13.6 %copy-start = (bf16[4,16,32,128]{3,2,1,0:T(8,128)(2,1)S(1)}, bf16[4,16,32,128]{3,2,1,0:T(8,128)(2,1)}, u32[]{:S(2)}) copy-start(bf16[4,16,32,128]{3,2,1,0:T(8,128)(2,1)} %cotangent.1) | copy-start | bytes 1572868
  1.7 13.6 %copy-start.1 = (bf16[27,32,256]{2,1,0:T(8,128)(2,1)S(1)}, bf16[27,32,256]{2,1,0:T(8,128)(2,1)}, u32[]{:S(2)}) copy-start(bf16[27,32,256]{2,1,0:T(8,128)(2,1)} %kernel.1) | copy-start | bytes 1327108
  1.7 9.9 %collective-permute-start = (bf16[4,9,32,128]{3,2,1,0:T(8,128)(2,1)S(1)}, bf16[4,9,32,128]{3,2,1,0:T(8,128)(2,1)S(1)}, u32[]{:S(2)}, u32[]{:S(2)}) collective-permute-start(bf16[4,9,32,128]{3,2,1,0:T(8,128)(2,1)S(1)} %constant_dynamic-slice_fusion.1), channel_id=1, source_target_pairs={{0,16},{16,0},{1,17},{17,1},{2,18},{18,2},{3,19},{19,3},{4,20},{20... | collective-permute-start | bytes 884744 | tf_op jit(solution)/shard_map/ppermute | solution.py:366
  11.7 11.7 %collective-permute-start.1 = (bf16[2,9,64,128]{3,2,1,0:T(8,128)(2,1)S(1)}, bf16[2,9,64,128]{3,2,1,0:T(8,128)(2,1)S(1)}, u32[]{:S(2)}, u32[]{:S(2)}) collective-permute-start(bf16[2,9,64,128]{3,2,1,0:T(8,128)(2,1)S(1)} %maximum_select_fusion.1.after.own_lo), channel_id=1, source_target_pairs={{0,32},{32,64},{64,96},{96,0},{1,33},{33,65},{65,97},{97,1},{2,34}... | collective-permute-start | bytes 884744 | tf_op jit(solution)/shard_map/ppermute | solution.py:372
  13.6 10.9 %collective-permute-start.4 = (bf16[2,9,64,128]{3,2,1,0:T(8,128)(2,1)S(1)}, bf16[2,9,64,128]{3,2,1,0:T(8,128)(2,1)S(1)}, u32[]{:S(2)}, u32[]{:S(2)}) collective-permute-start(bf16[2,9,64,128]{3,2,1,0:T(8,128)(2,1)S(1)} %maximum_select_fusion.2.own_hi), channel_id=1, source_target_pairs={{0,96},{32,0},{64,32},{96,64},{1,97},{33,1},{65,33},{97,65},{2,98}... | collective-permute-start | bytes 884744 | tf_op jit(solution)/shard_map/ppermute | solution.py:372
  15.9 7.6 %collective-permute-start.8 = (bf16[4,8,32,128]{3,2,1,0:T(8,128)(2,1)S(1)}, bf16[4,8,32,128]{3,2,1,0:T(8,128)(2,1)S(1)}, u32[]{:S(2)}, u32[]{:S(2)}) collective-permute-start(bf16[4,8,32,128]{3,2,1,0:T(8,128)(2,1)S(1)} %get-tuple-element.38), channel_id=1, source_target_pairs={{0,16},{16,0},{1,17},{17,1},{2,18},{18,2},{3,19},{19,3},{4,20},{20... | collective-permute-start | bytes 786440 | tf_op jit(solution)/shard_map/ppermute | solution.py:366
  18.7 14.9 %collective-permute-start.7 = (bf16[29,32,256]{2,1,0:T(8,128)(2,1)S(1)}, bf16[29,32,256]{2,1,0:T(8,128)(2,1)S(1)}, u32[]{:S(2)}, u32[]{:S(2)}) collective-permute-start(bf16[29,32,256]{2,1,0:T(8,128)(2,1)S(1)} %get-tuple-element.36.kernel_own), channel_id=1, source_target_pairs={{0,16},{16,0},{1,17},{17,1},{2,18},{18,2},{3,19},{19,3},{4,20},{20... | collective-permute-start | bytes 1425416 | tf_op jit(solution)/shard_map/ppermute | solution.py:366
  18.9 8.2 %collective-permute-start.3 = (bf16[2,9,64,128]{3,2,1,0:T(8,128)(2,1)S(1)}, bf16[2,9,64,128]{3,2,1,0:T(8,128)(2,1)S(1)}, u32[]{:S(2)}, u32[]{:S(2)}) collective-permute-start(bf16[2,9,64,128]{3,2,1,0:T(8,128)(2,1)S(1)} %maximum_select_fusion.1.after.own_lo), channel_id=1, source_target_pairs={{0,96},{32,0},{64,32},{96,64},{1,97},{33,1},{65,33},{97,65},{2,98}... | collective-permute-start | bytes 884744 | tf_op jit(solution)/shard_map/ppermute | solution.py:372
  23.4 7.1 %collective-permute-start.2 = (bf16[2,9,64,128]{3,2,1,0:T(8,128)(2,1)S(1)}, bf16[2,9,64,128]{3,2,1,0:T(8,128)(2,1)S(1)}, u32[]{:S(2)}, u32[]{:S(2)}) collective-permute-start(bf16[2,9,64,128]{3,2,1,0:T(8,128)(2,1)S(1)} %maximum_select_fusion.2.own_hi), channel_id=1, source_target_pairs={{0,32},{32,64},{64,96},{96,0},{1,33},{33,65},{65,97},{97,1},{2,34}... | collective-permute-start | bytes 884744 | tf_op jit(solution)/shard_map/ppermute | solution.py:372
  23.5 10.9 %collective-permute-start.5 = (bf16[2,9,64,128]{3,2,1,0:T(8,128)(2,1)S(1)}, bf16[2,9,64,128]{3,2,1,0:T(8,128)(2,1)S(1)}, u32[]{:S(2)}, u32[]{:S(2)}) collective-permute-start(bf16[2,9,64,128]{3,2,1,0:T(8,128)(2,1)S(1)} %collective-permute-done.1.left_lo), channel_id=1, source_target_pairs={{0,32},{32,64},{64,96},{96,0},{1,33},{33,65},{65,97},{97,1},{2,34}... | collective-permute-start | bytes 884744 | tf_op jit(solution)/shard_map/ppermute | solution.py:372
  24.5 9.9 %collective-permute-start.6 = (bf16[2,9,64,128]{3,2,1,0:T(8,128)(2,1)S(1)}, bf16[2,9,64,128]{3,2,1,0:T(8,128)(2,1)S(1)}, u32[]{:S(2)}, u32[]{:S(2)}) collective-permute-start(bf16[2,9,64,128]{3,2,1,0:T(8,128)(2,1)S(1)} %collective-permute-done.4.right_hi), channel_id=1, source_target_pairs={{0,96},{32,0},{64,32},{96,64},{1,97},{33,1},{65,33},{97,65},{2,98}... | collective-permute-start | bytes 884744 | tf_op jit(solution)/shard_map/ppermute | solution.py:372
  35.0 21.3 %collective-permute-start.9 = (bf16[4,9,64,128]{3,2,1,0:T(8,128)(2,1)S(1)}, bf16[4,9,64,128]{3,2,1,0:T(8,128)(2,1)S(1)}, u32[]{:S(2)}, u32[]{:S(2)}) collective-permute-start(bf16[4,9,64,128]{3,2,1,0:T(8,128)(2,1)S(1)} %get-tuple-element.40), channel_id=1, source_target_pairs={{0,1},{1,2},{2,3},{3,4},{4,5},{5,6},{6,7},{7,8},{8,9},{9,10},{10,1... | collective-permute-start | bytes 1769480 | tf_op jit(solution)/shard_map/ppermute | solution.py:375
  43.8 15.2 %collective-permute-start.10 = (bf16[4,9,64,128]{3,2,1,0:T(8,128)(2,1)S(1)}, bf16[4,9,64,128]{3,2,1,0:T(8,128)(2,1)S(1)}, u32[]{:S(2)}, u32[]{:S(2)}) collective-permute-start(bf16[4,9,64,128]{3,2,1,0:T(8,128)(2,1)S(1)} %get-tuple-element.41), channel_id=1, source_target_pairs={{1,0},{2,1},{3,2},{4,3},{5,4},{6,5},{7,6},{8,7},{9,8},{10,9},{11,1... | collective-permute-start | bytes 1769480 | tf_op jit(solution)/shard_map/ppermute | solution.py:378
  62.9 0.7 copy-start.4
  63.6 8.4 %collective-permute-start.12 = (bf16[8,64,128]{2,1,0:T(8,128)(2,1)S(1)}, bf16[8,64,128]{2,1,0:T(8,128)(2,1)S(1)}, u32[]{:S(2)}, u32[]{:S(2)}) collective-permute-start(bf16[8,64,128]{2,1,0:T(8,128)(2,1)S(1)} %get-tuple-element.51), channel_id=1, source_target_pairs={{0,1},{1,2},{2,3},{3,4},{4,5},{5,6},{6,7},{7,8},{8,9},{9,10},{10,1... | collective-permute-start | bytes 393224 | tf_op jit(solution)/shard_map/ppermute | solution.py:375
  65.5 6.5 %collective-permute-start.13 = (bf16[8,64,128]{2,1,0:T(8,128)(2,1)S(1)}, bf16[8,64,128]{2,1,0:T(8,128)(2,1)S(1)}, u32[]{:S(2)}, u32[]{:S(2)}) collective-permute-start(bf16[8,64,128]{2,1,0:T(8,128)(2,1)S(1)} %get-tuple-element.52), channel_id=1, source_target_pairs={{1,0},{2,1},{3,2},{4,3},{5,4},{6,5},{7,6},{8,7},{9,8},{10,9},{11,1... | collective-permute-start | bytes 393224 | tf_op jit(solution)/shard_map/ppermute | solution.py:378
  76.3 0.8 copy-start.3
  77.1 5.3 %copy-start.2 = (bf16[4,9,64,128]{3,2,1,0:T(8,128)(2,1)}, bf16[4,9,64,128]{3,2,1,0:T(8,128)(2,1)S(1)}, u32[]{:S(2)}) copy-start(bf16[4,9,64,128]{3,2,1,0:T(8,128)(2,1)S(1)} %get-tuple-element.62) | copy-start | bytes 1769476
  82.4 2.6 %collective-permute-start.18 = (f32[2,448,256]{2,1,0:T(8,128)S(1)}, f32[2,448,256]{2,1,0:T(8,128)S(1)}, u32[]{:S(2)}, u32[]{:S(2)}) collective-permute-start(f32[2,448,256]{2,1,0:T(8,128)S(1)} %get-tuple-element.68), channel_id=1, source_target_pairs={{0,1},{1,0},{2,3},{3,2},{4,5},{5,4},{6,7},{7,6},{8,9},{9,8},{10,11... | collective-permute-start | bytes 2752520 | tf_op jit(solution)/shard_map/ppermute | solution.py:369
  86.5 23.2 %all-to-all-start = ((f32[16,56,256]{2,1,0:T(8,128)}), f32[16,56,256]{2,1,0:T(8,128)S(1)}, u32[]{:S(2)}, u32[]{:S(2)}) async-start(f32[16,56,256]{2,1,0:T(8,128)} %bitcast.3), calls=%async_computation | async-start | bytes 1835008 | tf_op jit(solution)/shard_map/all_to_all | solution.py:478
  94.8 31.2 %collective-permute-start.15 = (bf16[4,9,64,128]{3,2,1,0:T(8,128)(2,1)}, bf16[4,9,64,128]{3,2,1,0:T(8,128)(2,1)S(1)}, u32[]{:S(2)}, u32[]{:S(2)}) collective-permute-start(bf16[4,9,64,128]{3,2,1,0:T(8,128)(2,1)} %copy-done.3), channel_id=1, source_target_pairs={{0,64},{32,96},{64,0},{96,32},{1,65},{33,97},{65,1},{97,33},{2,66}... | collective-permute-start | bytes 1769480 | tf_op jit(solution)/shard_map/ppermute | solution.py:372
  95.2 30.8 %collective-permute-start.16 = (bf16[4,9,64,128]{3,2,1,0:T(8,128)(2,1)}, bf16[4,9,64,128]{3,2,1,0:T(8,128)(2,1)}, u32[]{:S(2)}, u32[]{:S(2)}) collective-permute-start(bf16[4,9,64,128]{3,2,1,0:T(8,128)(2,1)} %copy-done.2), channel_id=1, source_target_pairs={{0,96},{32,0},{64,32},{96,64},{1,97},{33,1},{65,33},{97,65},{2,98}... | collective-permute-start | bytes 1769480 | tf_op jit(solution)/shard_map/ppermute | solution.py:372
  96.0 30.0 %collective-permute-start.14 = (bf16[4,9,64,128]{3,2,1,0:T(8,128)(2,1)S(1)}, bf16[4,9,64,128]{3,2,1,0:T(8,128)(2,1)}, u32[]{:S(2)}, u32[]{:S(2)}) collective-permute-start(bf16[4,9,64,128]{3,2,1,0:T(8,128)(2,1)S(1)} %get-tuple-element.60.after), channel_id=1, source_target_pairs={{0,32},{32,64},{64,96},{96,0},{1,33},{33,65},{65,97},{97,1},{2,34}... | collective-permute-start | bytes 1769480 | tf_op jit(solution)/shard_map/ppermute | solution.py:372
  109.7 14.3 %copy-start.5 = (bf16[4,8,32,128]{3,2,1,0:T(8,128)(2,1)S(1)}, bf16[4,8,32,128]{3,2,1,0:T(8,128)(2,1)}, u32[]{:S(2)}) copy-start(bf16[4,8,32,128]{3,2,1,0:T(8,128)(2,1)} %copy-done.4) | copy-start | bytes 786436
  121.4 19.7 %collective-permute-start.19 = (f32[448,256]{1,0:T(8,128)S(1)}, f32[448,256]{1,0:T(8,128)S(1)}, u32[]{:S(2)}, u32[]{:S(2)}) collective-permute-start(f32[448,256]{1,0:T(8,128)S(1)} %bitcast.5), channel_id=1, source_target_pairs={{0,1},{1,0},{2,3},{3,2},{4,5},{5,4},{6,7},{7,6},{8,9},{9,8},{10,11... | collective-permute-start | bytes 1376264 | tf_op jit(solution)/shard_map/ppermute | solution.py:369
  124.0 9.4 %collective-permute-start.11 = (bf16[4,8,32,128]{3,2,1,0:T(8,128)(2,1)S(1)}, bf16[4,8,32,128]{3,2,1,0:T(8,128)(2,1)S(1)}, u32[]{:S(2)}, u32[]{:S(2)}) collective-permute-start(bf16[4,8,32,128]{3,2,1,0:T(8,128)(2,1)S(1)} %copy-done.5), channel_id=1, source_target_pairs={{0,16},{16,0},{1,17},{17,1},{2,18},{18,2},{3,19},{19,3},{4,20},{20... | collective-permute-start | bytes 786440 | tf_op jit(solution)/shard_map/ppermute | solution.py:366
  127.6 12.2 %collective-permute-start.17 = (bf16[4,9,32,128]{3,2,1,0:T(8,128)(2,1)S(1)}, bf16[4,9,32,128]{3,2,1,0:T(8,128)(2,1)S(1)}, u32[]{:S(2)}, u32[]{:S(2)}) collective-permute-start(bf16[4,9,32,128]{3,2,1,0:T(8,128)(2,1)S(1)} %get-tuple-element.64), channel_id=1, source_target_pairs={{0,16},{16,0},{1,17},{17,1},{2,18},{18,2},{3,19},{19,3},{4,20},{20... | collective-permute-start | bytes 884744 | tf_op jit(solution)/shard_map/ppermute | solution.py:366

commit v3 on v2

--- a/solution.py
+++ b/solution.py
@@ -269,7 +269,7 @@
     store([(plane, rows) for _, plane in planes])
 
 
-def inner_input_body(at, grad, turned, turned_edge, own, near, far, back, stacked, held):
+def inner_input_body(at, grad, turned, turned_edge, after, own, near, far, back, stacked, held):
     lines = [lambda row, k=k: grad[k, row] for k in range(4)]
     input_terms(
         at, lines, [(0, 0), (1, 1)], turned, turned_edge, (own, near, far, back), stacked, held
@@ -277,7 +277,7 @@
 
 
 def outer_input_body(at, grad, low, high, turned, turned_edge, *refs):
-    given, outs, (stacked, held) = refs[:4], refs[4:8], refs[8:]
+    given, outs, (stacked, held) = refs[:4], refs[5:9], refs[9:]
     for source, ref in zip(given, outs):
         for plane in range(2):
             ref[plane + 1] = source[plane]
@@ -319,14 +319,14 @@
         ).astype(BF16)
 
 
-def add_body(at, keep, got, chip):
-    chip[...] = keep[...] + got[...]
+def add_body(at, keep, got, first, second, third, chip):
+    chip[...] = (keep[...] + got[...]).astype(BF16)
 
 
 def mean_body(at, pieces, copies):
-    total = pieces[0]
+    total = pieces[0].astype(F32)
     for k in range(1, pieces.shape[0]):
-        total = total + pieces[k]
+        total = total + pieces[k].astype(F32)
     total = total * (1.0 / math.sqrt(64 * 16 * 128))
     for k in range(copies.shape[0]):
         copies[k] = total
@@ -444,40 +444,33 @@
             flops // 2,
         )(at, grad, rim, turned, turned_edge)
 
-    def total_chunk(own, near, far, back):
-        near, back, far = turn(near, 1), turn(back, -1), turn(far, 2)
-        kept, sent = call(
-            total_body, 5, [((2, 9, 32, 128), F32), ((2, 9, 32, 128), BF16)], [], 10**6
-        )(at, own, near, far, back)
-        return kept, sent, swap(sent)
-
     def input_shapes(planes):
         return [((planes, 9, 64, 128), F32)] + [((planes, 9, 64, 128), BF16)] * 3
 
     def input_scratch(planes):
         return [pltpu.VMEM((planes, 10, 192, 128), BF16), pltpu.VMEM((256, 256), F32)]
 
-    parts = call(
-        inner_input_body, 4, input_shapes(2), input_scratch(4), flops // 2
-    )(at, grad, turned, turned_edge)
-    own, near, far, back = call(
-        outer_input_body, 10, input_shapes(4), input_scratch(6), flops // 2
-    )(at, grad, grad_low, grad_high, turned, turned_edge, *parts)
     keep, give = call(
         outer_weight_body, 6, [((2, 448, 256), F32)] * 2,
         [pltpu.VMEM((2, 8, 192, 128), BF16)], flops // 2, 1,
-    )(at, field, rim, grad, keep, give, near)
+    )(at, field, rim, grad, keep, give, grad)
+    parts = call(
+        inner_input_body, 4, input_shapes(2), input_scratch(4), flops // 2, 1
+    )(at, grad, turned, turned_edge, keep)
+    own, near, far, back = call(
+        outer_input_body, 10, input_shapes(4), input_scratch(6), flops // 2, 1
+    )(at, grad, grad_low, grad_high, turned, turned_edge, *parts, keep)
+    (chip,) = call(add_body, 3, [((2, 448, 256), BF16)], [], 10**6, 3)(
+        at, keep, swap_core(give), near, near, near
+    )
+    pieces = lax.all_to_all(
+        chip.reshape(16, 56, 256), ("xh", "z", "xl"), 0, 0, tiled=True
+    )
     near, back, far = turn(near, 1), turn(back, -1), turn(far, 2)
     kept, sent = call(
         total_body, 5, [((4, 9, 32, 128), F32), ((4, 9, 32, 128), BF16)], [], 10**6
     )(at, own, near, far, back)
     got = swap(sent)
-    (chip,) = call(add_body, 3, [((2, 448, 256), F32)], [], 10**6)(
-        at, keep, swap_core(give)
-    )
-    pieces = lax.all_to_all(
-        chip.reshape(16, 56, 256), ("xh", "z", "xl"), 0, 0, tiled=True
-    )
     (copies,) = call(mean_body, 2, [((8, 56, 256), F32)], [], 10**6)(at, pieces)
     everyone = lax.all_to_all(copies, ("z", "xl"), 0, 0, tiled=True).reshape(448, 256)
     (weight_grad,) = call(weave_body, 3, [((27, 32, 256), F32)], [], 10**6)(

time: 143 us -> 136 us (0.951)
  waiting for transfers between devices: 44.6 us -> 37.9 us
  starting transfers between devices: 45.5 us -> 47.1 us
    all_to_all x1, waiting for transfers between devices: 13 us -> 7.22 us  [on_device(): lax.all_to_all(chip.reshape(16, 56, 256), ('xh', 'z', 'xl'), 0, 0, tiled=...]
    ppermute x9, waiting for transfers between devices: 5.09 us -> 10.4 us  [turn(): return lax.ppermute(value, 'y', [(i, (i + step) % 4) for i in range(4)])]
    ppermute x5, waiting for transfers between devices: 21.4 us -> 17.4 us  [swap(): return lax.ppermute(value, 'xh', [(0, 1), (1, 0)])]
    ppermute x2, waiting for transfers between devices: 2.46 us -> 0.01 us  [swap_core(): return lax.ppermute(value, 'core', [(0, 1), (1, 0)])]
    ppermute x2, starting transfers between devices: 10.7 us -> 12.3 us  [up(): return lax.ppermute(value, SPACE, [(i, i + 1) for i in range(15)])]
  transfers between devices with their start and end apart: 21 -> 21, of which waited for: 11 -> 12; matrix products, arithmetic and copies ran while one was open for 1% -> 2% of each run, Pallas kernels for 13% -> 17%
where the time goes in v3:
time: 136 us
  starting transfers between devices  47.1 us (35%)
  waiting for transfers between devices  37.9 us (28%)
  Pallas kernels  36.4 us (27%)
  blocking collectives  9.73 us (7%)
  local copies, waits for them, and re-layouts  2.81 us (2%)
    ppermute x5, waiting for transfers between devices, swap(): return lax.ppermute(value, 'xh', [(0, 1), (1, 0)])  17.4 us
    ppermute x2, starting transfers between devices, up(): return lax.ppermute(value, SPACE, [(i, i + 1) for i in range(15)])  12.3 us
    ppermute x5, starting transfers between devices, swap(): return lax.ppermute(value, 'xh', [(0, 1), (1, 0)])  10.9 us
    ppermute x9, waiting for transfers between devices, turn(): return lax.ppermute(value, 'y', [(i, (i + step) % 4) for i in range(4)])  10.4 us
    all_to_all x1, blocking collectives, on_device(): lax.all_to_all(copies, ('z', 'xl'), 0, 0, tiled=True).reshape(448, 256)  9.73 us
    ppermute x9, starting transfers between devices, turn(): return lax.ppermute(value, 'y', [(i, (i + step) % 4) for i in range(4)])  9.38 us
    all_to_all x1, waiting for transfers between devices, on_device(): lax.all_to_all(chip.reshape(16, 56, 256), ('xh', 'z', 'xl'), 0, 0, tiled=...  7.22 us
    all_to_all x1, starting transfers between devices, on_device(): lax.all_to_all(chip.reshape(16, 56, 256), ('xh', 'z', 'xl'), 0, 0, tiled=...  6.91 us
  transfers between devices with their start and end apart: 21, of which 12 were waited for; matrix products, arithmetic and copies ran while one was open for 2% of the time, Pallas kernels for 17%

profile of v3, /device:TPU:1, one launch (start us, length us, event | category | flops | bytes accessed | tf_op | source)
XLA Modules:
  0.0 135.9 jit_solution(12785678829108269690)
XLA Ops:
  1.7 3.7 %collective-permute-start = (bf16[4,9,32,128]{3,2,1,0:T(8,128)(2,1)S(1)}, bf16[4,9,32,128]{3,2,1,0:T(8,128)(2,1)S(1)}, u32[]{:S(2)}, u32[]{:S(2)}) collective-permute-start(bf16[4,9,32,128]{3,2,1,0:T(8,128)(2,1)S(1)} %constant_dynamic-slice_fusion.1), channel_id=1, source_target_pairs={{0,16},{16,0},{1,17},{17,1},{2,18},{18,2},{3,19},{19,3},{4,20},{20... | collective-permute-start | bytes 884744 | tf_op jit(solution)/shard_map/ppermute | solution.py:366
  6.3 5.3 %collective-permute-done = bf16[4,9,32,128]{3,2,1,0:T(8,128)(2,1)S(1)} collective-permute-done((bf16[4,9,32,128]{3,2,1,0:T(8,128)(2,1)S(1)}, bf16[4,9,32,128]{3,2,1,0:T(8,128)(2,1)S(1)}, u32[]{:S(2)}, u32[]{:S(2)}) %collective-permute-start) | collective-permute-done | bytes 294944 | tf_op jit(solution)/shard_map/ppermute | solution.py:366
  11.7 1.7 %collective-permute-start.1 = (bf16[2,9,64,128]{3,2,1,0:T(8,128)(2,1)S(1)}, bf16[2,9,64,128]{3,2,1,0:T(8,128)(2,1)S(1)}, u32[]{:S(2)}, u32[]{:S(2)}) collective-permute-start(bf16[2,9,64,128]{3,2,1,0:T(8,128)(2,1)S(1)} %maximum_select_fusion.1.after.own_lo), channel_id=1, source_target_pairs={{0,32},{32,64},{64,96},{96,0},{1,33},{33,65},{65,97},{97,1},{2,34}... | collective-permute-start | bytes 884744 | tf_op jit(solution)/shard_map/ppermute | solution.py:372
  13.6 1.5 %collective-permute-start.4 = (bf16[2,9,64,128]{3,2,1,0:T(8,128)(2,1)S(1)}, bf16[2,9,64,128]{3,2,1,0:T(8,128)(2,1)S(1)}, u32[]{:S(2)}, u32[]{:S(2)}) collective-permute-start(bf16[2,9,64,128]{3,2,1,0:T(8,128)(2,1)S(1)} %maximum_select_fusion.2.own_hi), channel_id=1, source_target_pairs={{0,96},{32,0},{64,32},{96,64},{1,97},{33,1},{65,33},{97,65},{2,98}... | collective-permute-start | bytes 884744 | tf_op jit(solution)/shard_map/ppermute | solution.py:372
  15.9 2.8 %collective-permute-start.8 = (bf16[4,8,32,128]{3,2,1,0:T(8,128)(2,1)S(1)}, bf16[4,8,32,128]{3,2,1,0:T(8,128)(2,1)S(1)}, u32[]{:S(2)}, u32[]{:S(2)}) collective-permute-start(bf16[4,8,32,128]{3,2,1,0:T(8,128)(2,1)S(1)} %get-tuple-element.38), channel_id=1, source_target_pairs={{0,16},{16,0},{1,17},{17,1},{2,18},{18,2},{3,19},{19,3},{4,20},{20... | collective-permute-start | bytes 786440 | tf_op jit(solution)/shard_map/ppermute | solution.py:366
  18.9 1.5 %collective-permute-start.3 = (bf16[2,9,64,128]{3,2,1,0:T(8,128)(2,1)S(1)}, bf16[2,9,64,128]{3,2,1,0:T(8,128)(2,1)S(1)}, u32[]{:S(2)}, u32[]{:S(2)}) collective-permute-start(bf16[2,9,64,128]{3,2,1,0:T(8,128)(2,1)S(1)} %maximum_select_fusion.1.after.own_lo), channel_id=1, source_target_pairs={{0,96},{32,0},{64,32},{96,64},{1,97},{33,1},{65,33},{97,65},{2,98}... | collective-permute-start | bytes 884744 | tf_op jit(solution)/shard_map/ppermute | solution.py:372
  20.4 3.1 %collective-permute-done.8.cot_other.cot = bf16[4,8,32,128]{3,2,1,0:T(8,128)(2,1)S(1)} collective-permute-done((bf16[4,8,32,128]{3,2,1,0:T(8,128)(2,1)S(1)}, bf16[4,8,32,128]{3,2,1,0:T(8,128)(2,1)S(1)}, u32[]{:S(2)}, u32[]{:S(2)}) %collective-permute-start.8) | collective-permute-done | bytes 262176 | tf_op jit(solution)/shard_map/ppermute | solution.py:366
  24.5 1.7 %collective-permute-start.6 = (bf16[2,9,64,128]{3,2,1,0:T(8,128)(2,1)S(1)}, bf16[2,9,64,128]{3,2,1,0:T(8,128)(2,1)S(1)}, u32[]{:S(2)}, u32[]{:S(2)}) collective-permute-start(bf16[2,9,64,128]{3,2,1,0:T(8,128)(2,1)S(1)} %collective-permute-done.4.right_hi), channel_id=1, source_target_pairs={{0,96},{32,0},{64,32},{96,64},{1,97},{33,1},{65,33},{97,65},{2,98}... | collective-permute-start | bytes 884744 | tf_op jit(solution)/shard_map/ppermute | solution.py:372
  27.1 3.4 %collective-permute-done.2.left_hi = bf16[2,9,64,128]{3,2,1,0:T(8,128)(2,1)S(1)} collective-permute-done((bf16[2,9,64,128]{3,2,1,0:T(8,128)(2,1)S(1)}, bf16[2,9,64,128]{3,2,1,0:T(8,128)(2,1)S(1)}, u32[]{:S(2)}, u32[]{:S(2)}) %collective-permute-start.2) | collective-permute-done | bytes 294944 | tf_op jit(solution)/shard_map/ppermute | solution.py:372
  30.5 3.1 %collective-permute-done.7.kernel_other.kernel = bf16[29,32,256]{2,1,0:T(8,128)(2,1)S(1)} collective-permute-done((bf16[29,32,256]{2,1,0:T(8,128)(2,1)S(1)}, bf16[29,32,256]{2,1,0:T(8,128)(2,1)S(1)}, u32[]{:S(2)}, u32[]{:S(2)}) %collective-permute-start.7) | collective-permute-done | bytes 475168 | tf_op jit(solution)/shard_map/ppermute | solution.py:366
  35.0 8.8 %collective-permute-start.9 = (bf16[4,9,64,128]{3,2,1,0:T(8,128)(2,1)S(1)}, bf16[4,9,64,128]{3,2,1,0:T(8,128)(2,1)S(1)}, u32[]{:S(2)}, u32[]{:S(2)}) collective-permute-start(bf16[4,9,64,128]{3,2,1,0:T(8,128)(2,1)S(1)} %get-tuple-element.40), channel_id=1, source_target_pairs={{0,1},{1,2},{2,3},{3,4},{4,5},{5,6},{6,7},{7,8},{8,9},{9,10},{10,1... | collective-permute-start | bytes 1769480 | tf_op jit(solution)/shard_map/ppermute | solution.py:375
  43.8 1.9 %collective-permute-start.10 = (bf16[4,9,64,128]{3,2,1,0:T(8,128)(2,1)S(1)}, bf16[4,9,64,128]{3,2,1,0:T(8,128)(2,1)S(1)}, u32[]{:S(2)}, u32[]{:S(2)}) collective-permute-start(bf16[4,9,64,128]{3,2,1,0:T(8,128)(2,1)S(1)} %get-tuple-element.41), channel_id=1, source_target_pairs={{1,0},{2,1},{3,2},{4,3},{5,4},{6,5},{7,6},{8,7},{9,8},{10,9},{11,1... | collective-permute-start | bytes 1769480 | tf_op jit(solution)/shard_map/ppermute | solution.py:378
  45.8 5.0 %shard_map.68 = (bf16[2,8,32,128]{3,2,1,0:T(8,128)(2,1)S(1)}, bf16[2,8,32,128]{3,2,1,0:T(8,128)(2,1)S(1)}, bf16[2,8,64,128]{3,2,1,0:T(8,128)(2,1)S(1)}, bf16[4,1...) custom-call(s32[3]{0:T(128)S(1)} %pad_add_fusion.at, ...), custom_call_target="tpu_custom_call" | custom-call | flops 1800000000 | bytes 8388608 | tf_op jit(solution)/shard_map/pallas_call | solution.py:406
  50.8 5.5 %shard_map.70 = (f32[2,448,256]{2,1,0:T(8,128)S(1)}, f32[2,448,256]{2,1,0:T(8,128)S(1)}, bf16[256,1728]{1,0:T(8,128)(2,1)S(1)}, bf16[256,576]{1,0:T(8,128)(2,1)S(1)}) custom-call(s32[3]{0:T(128)S(1)} %pad_add_fusion.at, bf16[4,10,256,128]{3,2,1,0:T(8,128)(2,1)S(1)} %get-tuple-element.39.field, bf16[2,8,64,128]{3,2,1,0:T(8,128)(2,1)S(1)} %get-tuple-element.46.grad.in_grad, ...), custom_call_target="tpu_custom_call" | custom-call | flops 1800000000 | bytes 8388608 | tf_op jit(solution)/shard_map/pallas_call | solution.py:416
  56.4 2.6 %collective-permute-done.10.high = bf16[4,9,64,128]{3,2,1,0:T(8,128)(2,1)S(1)} collective-permute-done((bf16[4,9,64,128]{3,2,1,0:T(8,128)(2,1)S(1)}, bf16[4,9,64,128]{3,2,1,0:T(8,128)(2,1)S(1)}, u32[]{:S(2)}, u32[]{:S(2)}) %collective-permute-start.10) | collective-permute-done | bytes 589856 | tf_op jit(solution)/shard_map/ppermute | solution.py:378
  59.0 3.8 %shard_map.71 = (bf16[4,8,32,128]{3,2,1,0:T(8,128)(2,1)S(1)}, bf16[4,8,32,128]{3,2,1,0:T(8,128)(2,1)S(1)}, bf16[4,8,64,128]{3,2,1,0:T(8,128)(2,1)S(1)}, bf16[8,6...) custom-call(s32[3]{0:T(128)S(1)} %pad_add_fusion.at, ...), custom_call_target="tpu_custom_call" | custom-call | flops 1800000000 | bytes 8388608 | tf_op jit(solution)/shard_map/pallas_call | solution.py:421
  63.6 5.3 %shard_map.72 = (f32[2,448,256]{2,1,0:T(8,128)S(1)}, f32[2,448,256]{2,1,0:T(8,128)S(1)}) custom-call(s32[3]{0:T(128)S(1)} %pad_add_fusion.at, bf16[4,10,256,128]{3,2,1,0:T(8,128)(2,1)S(1)} %get-tuple-element.39.field, bf16[2,10,256,128]{3,2,1,0:T(8,128)(2,1)S(1)} %get-tuple-element.55.rim, bf16[4,8,64,128]{3,2,1,0:T(8,128)(2,1)S(1)} %get-tuple-element.50.grad.after, ...), custom_call_target="tpu_custom_call" | custom-call | flops 1800000000 | bytes 8388608 | tf_op jit(solution)/shard_map/pallas_call | solution.py:453
  68.9 3.5 %collective-permute-start.12 = (bf16[8,64,128]{2,1,0:T(8,128)(2,1)S(1)}, bf16[8,64,128]{2,1,0:T(8,128)(2,1)S(1)}, u32[]{:S(2)}, u32[]{:S(2)}) collective-permute-start(bf16[8,64,128]{2,1,0:T(8,128)(2,1)S(1)} %get-tuple-element.51), channel_id=1, source_target_pairs={{0,1},{1,2},{2,3},{3,4},{4,5},{5,6},{6,7},{7,8},{8,9},{9,10},{10,1... | collective-permute-start | bytes 393224 | tf_op jit(solution)/shard_map/ppermute | solution.py:375
  72.4 1.9 %collective-permute-start.13 = (bf16[8,64,128]{2,1,0:T(8,128)(2,1)S(1)}, bf16[8,64,128]{2,1,0:T(8,128)(2,1)S(1)}, u32[]{:S(2)}, u32[]{:S(2)}) collective-permute-start(bf16[8,64,128]{2,1,0:T(8,128)(2,1)S(1)} %get-tuple-element.52), channel_id=1, source_target_pairs={{1,0},{2,1},{3,2},{4,3},{5,4},{6,5},{7,6},{8,7},{9,8},{10,9},{11,1... | collective-permute-start | bytes 393224 | tf_op jit(solution)/shard_map/ppermute | solution.py:378
  74.3 4.1 %shard_map.73 = (f32[2,9,64,128]{3,2,1,0:T(8,128)S(1)}, bf16[2,9,64,128]{3,2,1,0:T(8,128)(2,1)S(1)}, bf16[2,9,64,128]{3,2,1,0:T(8,128)(2,1)S(1)}, bf16[2,9,64,128]{3,2,1,0:T(8,128)(2,1)S(1)}) custom-call(s32[3]{0:T(128)S(1)} %pad_add_fusion.at, bf16[4,8,64,128]{3,2,1,0:T(8,128)(2,1)S(1)} %get-tuple-element.50.grad.after, ...), custom_call_target="tpu_custom_call" | custom-call | flops 1800000000 | bytes 8388608 | tf_op jit(solution)/shard_map/pallas_call | solution.py:457
  78.7 5.1 %shard_map.74 = (f32[4,9,64,128]{3,2,1,0:T(8,128)S(1)}, bf16[4,9,64,128]{3,2,1,0:T(8,128)(2,1)S(1)}, bf16[4,9,64,128]{3,2,1,0:T(8,128)(2,1)}, bf16[4,9,64,128]{3,2,1,0:T(8,128)(2,1)S(1)}) custom-call(s32[3]{0:T(128)S(1)} %pad_add_fusion.at, bf16[4,8,64,128]{3,2,1,0:T(8,128)(2,1)S(1)} %get-tuple-element.50.grad.after, ...), custom_call_target="tpu_custom_call" | custom-call | flops 1800000000 | bytes 8388608 | tf_op jit(solution)/shard_map/pallas_call | solution.py:460
  83.8 1.4 %shard_map.77 = bf16[2,448,256]{2,1,0:T(8,128)(2,1)} custom-call(s32[3]{0:T(128)S(1)} %pad_add_fusion.at, f32[2,448,256]{2,1,0:T(8,128)S(1)} %get-tuple-element.57.after.refs_4_.keep, f32[2,448,256]{2,1,0:T(8,128)S(1)} %collective-permute-done.18.got, bf16[4,9,64,128]{3,2,1,0:T(8,128)(2,1)S(1)} %get-tuple-element.63.first.second.third, ...), custom_call_target="tpu_custom_call" | custom-call | flops 1000000 | bytes 8388608 | tf_op jit(solution)/shard_map/pallas_call | solution.py:463
  85.2 6.9 %all-to-all-start = ((bf16[16,56,256]{2,1,0:T(8,128)(2,1)}), bf16[16,56,256]{2,1,0:T(8,128)(2,1)S(1)}, u32[]{:S(2)}, u32[]{:S(2)}) async-start(bf16[16,56,256]{2,1,0:T(8,128)(2,1)} %bitcast.3), calls=%async_computation | async-start | bytes 917504 | tf_op jit(solution)/shard_map/all_to_all | solution.py:466
  94.0 7.2 %all-to-all-done.pieces = bf16[16,56,256]{2,1,0:T(8,128)(2,1)S(1)} async-done(((bf16[16,56,256]{2,1,0:T(8,128)(2,1)}), bf16[16,56,256]{2,1,0:T(8,128)(2,1)S(1)}, u32[]{:S(2)}, u32[]{:S(2)}) %all-to-all-start) | async-done | bytes 458784 | tf_op jit(solution)/shard_map/all_to_all | solution.py:466
  101.9 9.7 %all_to_all.10 = f32[8,56,256]{2,1,0:T(8,128)S(1)} all-to-all(f32[8,56,256]{2,1,0:T(8,128)S(1)} %shard_map.78), channel_id=1, replica_groups=mesh['y'=4,'xh'=2,'z'=4,'xl'=2,'core'=2] {'z','xl'}, dimensions={0} | all-to-all | bytes 917504 | tf_op jit(solution)/shard_map/all_to_all | solution.py:475
  111.6 3.7 %collective-permute-start.19 = (f32[448,256]{1,0:T(8,128)S(1)}, f32[448,256]{1,0:T(8,128)S(1)}, u32[]{:S(2)}, u32[]{:S(2)}) collective-permute-start(f32[448,256]{1,0:T(8,128)S(1)} %bitcast.5), channel_id=1, source_target_pairs={{0,1},{1,0},{2,3},{3,2},{4,5},{5,4},{6,7},{7,6},{8,9},{9,8},{10,11... | collective-permute-start | bytes 1376264 | tf_op jit(solution)/shard_map/ppermute | solution.py:369
  116.6 2.1 %collective-permute-done.16.back = bf16[4,9,64,128]{3,2,1,0:T(8,128)(2,1)S(1)} collective-permute-done((bf16[4,9,64,128]{3,2,1,0:T(8,128)(2,1)}, bf16[4,9,64,128]{3,2,1,0:T(8,128)(2,1)S(1)}, u32[]{:S(2)}, u32[]{:S(2)}) %collective-permute-start.16) | collective-permute-done | bytes 589856 | tf_op jit(solution)/shard_map/ppermute | solution.py:372
  118.7 3.2 %collective-permute-done.14.near = bf16[4,9,64,128]{3,2,1,0:T(8,128)(2,1)} collective-permute-done((bf16[4,9,64,128]{3,2,1,0:T(8,128)(2,1)S(1)}, bf16[4,9,64,128]{3,2,1,0:T(8,128)(2,1)}, u32[]{:S(2)}, u32[]{:S(2)}) %collective-permute-start.14) | collective-permute-done | bytes 589856 | tf_op jit(solution)/shard_map/ppermute | solution.py:372
  121.9 1.4 %shard_map.75 = (f32[4,9,32,128]{3,2,1,0:T(8,128)S(1)}, bf16[4,9,32,128]{3,2,1,0:T(8,128)(2,1)S(1)}) custom-call(s32[3]{0:T(128)S(1)} %pad_add_fusion.at, f32[4,9,64,128]{3,2,1,0:T(8,128)S(1)} %get-tuple-element.62.own, bf16[4,9,64,128]{3,2,1,0:T(8,128)(2,1)} %collective-permute-done.14.near, bf16[4,9,64,128]{3,2,1,0:T(8,128)(2,1)S(1)} %collective-permute-done.15.far, ...), custom_call_target="tpu_custom_call" | custom-call | flops 1000000 | bytes 8388608 | tf_op jit(solution)/shard_map/pallas_call | solution.py:470
  123.3 2.9 %collective-permute-start.17 = (bf16[4,9,32,128]{3,2,1,0:T(8,128)(2,1)S(1)}, bf16[4,9,32,128]{3,2,1,0:T(8,128)(2,1)S(1)}, u32[]{:S(2)}, u32[]{:S(2)}) collective-permute-start(bf16[4,9,32,128]{3,2,1,0:T(8,128)(2,1)S(1)} %get-tuple-element.67), channel_id=1, source_target_pairs={{0,16},{16,0},{1,17},{17,1},{2,18},{18,2},{3,19},{19,3},{4,20},{20... | collective-permute-start | bytes 884744 | tf_op jit(solution)/shard_map/ppermute | solution.py:366
  127.0 6.0 %collective-permute-done.17.got = bf16[4,9,32,128]{3,2,1,0:T(8,128)(2,1)S(1)} collective-permute-done((bf16[4,9,32,128]{3,2,1,0:T(8,128)(2,1)S(1)}, bf16[4,9,32,128]{3,2,1,0:T(8,128)(2,1)S(1)}, u32[]{:S(2)}, u32[]{:S(2)}) %collective-permute-start.17) | collective-permute-done | bytes 294944 | tf_op jit(solution)/shard_map/ppermute | solution.py:366
  134.4 1.5 %shard_map.79 = f32[27,32,256]{2,1,0:T(8,128)} custom-call(s32[3]{0:T(128)S(1)} %pad_add_fusion.at, f32[448,256]{1,0:T(8,128)S(1)} %bitcast.6, f32[448,256]{1,0:T(8,128)S(1)} %collective-permute-done.19.other), custom_call_target="tpu_custom_call" | custom-call | flops 1000000 | bytes 8388608 | tf_op jit(solution)/shard_map/pallas_call | solution.py:476
  (48 shorter events, 13.8 us)
Async XLA Ops:
  1.6 13.6 %copy-start.7 = (f32[32]{0:T(128)S(1)}, f32[32]{0:T(128)}, u32[]{:S(2)}) copy-start(f32[32]{0:T(128)} %param.6) | copy-start | bytes 388
  1.6 13.6 %copy-start = (bf16[4,16,32,128]{3,2,1,0:T(8,128)(2,1)S(1)}, bf16[4,16,32,128]{3,2,1,0:T(8,128)(2,1)}, u32[]{:S(2)}) copy-start(bf16[4,16,32,128]{3,2,1,0:T(8,128)(2,1)} %cotangent.1) | copy-start | bytes 1572868
  1.7 13.6 %copy-start.1 = (bf16[27,32,256]{2,1,0:T(8,128)(2,1)S(1)}, bf16[27,32,256]{2,1,0:T(8,128)(2,1)}, u32[]{:S(2)}) copy-start(bf16[27,32,256]{2,1,0:T(8,128)(2,1)} %kernel.1) | copy-start | bytes 1327108
  1.7 9.9 %collective-permute-start = (bf16[4,9,32,128]{3,2,1,0:T(8,128)(2,1)S(1)}, bf16[4,9,32,128]{3,2,1,0:T(8,128)(2,1)S(1)}, u32[]{:S(2)}, u32[]{:S(2)}) collective-permute-start(bf16[4,9,32,128]{3,2,1,0:T(8,128)(2,1)S(1)} %constant_dynamic-slice_fusion.1), channel_id=1, source_target_pairs={{0,16},{16,0},{1,17},{17,1},{2,18},{18,2},{3,19},{19,3},{4,20},{20... | collective-permute-start | bytes 884744 | tf_op jit(solution)/shard_map/ppermute | solution.py:366
  11.7 11.7 %collective-permute-start.1 = (bf16[2,9,64,128]{3,2,1,0:T(8,128)(2,1)S(1)}, bf16[2,9,64,128]{3,2,1,0:T(8,128)(2,1)S(1)}, u32[]{:S(2)}, u32[]{:S(2)}) collective-permute-start(bf16[2,9,64,128]{3,2,1,0:T(8,128)(2,1)S(1)} %maximum_select_fusion.1.after.own_lo), channel_id=1, source_target_pairs={{0,32},{32,64},{64,96},{96,0},{1,33},{33,65},{65,97},{97,1},{2,34}... | collective-permute-start | bytes 884744 | tf_op jit(solution)/shard_map/ppermute | solution.py:372
  13.6 10.9 %collective-permute-start.4 = (bf16[2,9,64,128]{3,2,1,0:T(8,128)(2,1)S(1)}, bf16[2,9,64,128]{3,2,1,0:T(8,128)(2,1)S(1)}, u32[]{:S(2)}, u32[]{:S(2)}) collective-permute-start(bf16[2,9,64,128]{3,2,1,0:T(8,128)(2,1)S(1)} %maximum_select_fusion.2.own_hi), channel_id=1, source_target_pairs={{0,96},{32,0},{64,32},{96,64},{1,97},{33,1},{65,33},{97,65},{2,98}... | collective-permute-start | bytes 884744 | tf_op jit(solution)/shard_map/ppermute | solution.py:372
  15.9 7.6 %collective-permute-start.8 = (bf16[4,8,32,128]{3,2,1,0:T(8,128)(2,1)S(1)}, bf16[4,8,32,128]{3,2,1,0:T(8,128)(2,1)S(1)}, u32[]{:S(2)}, u32[]{:S(2)}) collective-permute-start(bf16[4,8,32,128]{3,2,1,0:T(8,128)(2,1)S(1)} %get-tuple-element.38), channel_id=1, source_target_pairs={{0,16},{16,0},{1,17},{17,1},{2,18},{18,2},{3,19},{19,3},{4,20},{20... | collective-permute-start | bytes 786440 | tf_op jit(solution)/shard_map/ppermute | solution.py:366
  18.7 14.9 %collective-permute-start.7 = (bf16[29,32,256]{2,1,0:T(8,128)(2,1)S(1)}, bf16[29,32,256]{2,1,0:T(8,128)(2,1)S(1)}, u32[]{:S(2)}, u32[]{:S(2)}) collective-permute-start(bf16[29,32,256]{2,1,0:T(8,128)(2,1)S(1)} %get-tuple-element.36.kernel_own), channel_id=1, source_target_pairs={{0,16},{16,0},{1,17},{17,1},{2,18},{18,2},{3,19},{19,3},{4,20},{20... | collective-permute-start | bytes 1425416 | tf_op jit(solution)/shard_map/ppermute | solution.py:366
  18.9 8.2 %collective-permute-start.3 = (bf16[2,9,64,128]{3,2,1,0:T(8,128)(2,1)S(1)}, bf16[2,9,64,128]{3,2,1,0:T(8,128)(2,1)S(1)}, u32[]{:S(2)}, u32[]{:S(2)}) collective-permute-start(bf16[2,9,64,128]{3,2,1,0:T(8,128)(2,1)S(1)} %maximum_select_fusion.1.after.own_lo), channel_id=1, source_target_pairs={{0,96},{32,0},{64,32},{96,64},{1,97},{33,1},{65,33},{97,65},{2,98}... | collective-permute-start | bytes 884744 | tf_op jit(solution)/shard_map/ppermute | solution.py:372
  23.4 7.1 %collective-permute-start.2 = (bf16[2,9,64,128]{3,2,1,0:T(8,128)(2,1)S(1)}, bf16[2,9,64,128]{3,2,1,0:T(8,128)(2,1)S(1)}, u32[]{:S(2)}, u32[]{:S(2)}) collective-permute-start(bf16[2,9,64,128]{3,2,1,0:T(8,128)(2,1)S(1)} %maximum_select_fusion.2.own_hi), channel_id=1, source_target_pairs={{0,32},{32,64},{64,96},{96,0},{1,33},{33,65},{65,97},{97,1},{2,34}... | collective-permute-start | bytes 884744 | tf_op jit(solution)/shard_map/ppermute | solution.py:372
  23.5 10.9 %collective-permute-start.5 = (bf16[2,9,64,128]{3,2,1,0:T(8,128)(2,1)S(1)}, bf16[2,9,64,128]{3,2,1,0:T(8,128)(2,1)S(1)}, u32[]{:S(2)}, u32[]{:S(2)}) collective-permute-start(bf16[2,9,64,128]{3,2,1,0:T(8,128)(2,1)S(1)} %collective-permute-done.1.left_lo), channel_id=1, source_target_pairs={{0,32},{32,64},{64,96},{96,0},{1,33},{33,65},{65,97},{97,1},{2,34}... | collective-permute-start | bytes 884744 | tf_op jit(solution)/shard_map/ppermute | solution.py:372
  24.5 9.9 %collective-permute-start.6 = (bf16[2,9,64,128]{3,2,1,0:T(8,128)(2,1)S(1)}, bf16[2,9,64,128]{3,2,1,0:T(8,128)(2,1)S(1)}, u32[]{:S(2)}, u32[]{:S(2)}) collective-permute-start(bf16[2,9,64,128]{3,2,1,0:T(8,128)(2,1)S(1)} %collective-permute-done.4.right_hi), channel_id=1, source_target_pairs={{0,96},{32,0},{64,32},{96,64},{1,97},{33,1},{65,33},{97,65},{2,98}... | collective-permute-start | bytes 884744 | tf_op jit(solution)/shard_map/ppermute | solution.py:372
  35.0 21.3 %collective-permute-start.9 = (bf16[4,9,64,128]{3,2,1,0:T(8,128)(2,1)S(1)}, bf16[4,9,64,128]{3,2,1,0:T(8,128)(2,1)S(1)}, u32[]{:S(2)}, u32[]{:S(2)}) collective-permute-start(bf16[4,9,64,128]{3,2,1,0:T(8,128)(2,1)S(1)} %get-tuple-element.40), channel_id=1, source_target_pairs={{0,1},{1,2},{2,3},{3,4},{4,5},{5,6},{6,7},{7,8},{8,9},{9,10},{10,1... | collective-permute-start | bytes 1769480 | tf_op jit(solution)/shard_map/ppermute | solution.py:375
  43.8 15.2 %collective-permute-start.10 = (bf16[4,9,64,128]{3,2,1,0:T(8,128)(2,1)S(1)}, bf16[4,9,64,128]{3,2,1,0:T(8,128)(2,1)S(1)}, u32[]{:S(2)}, u32[]{:S(2)}) collective-permute-start(bf16[4,9,64,128]{3,2,1,0:T(8,128)(2,1)S(1)} %get-tuple-element.41), channel_id=1, source_target_pairs={{1,0},{2,1},{3,2},{4,3},{5,4},{6,5},{7,6},{8,7},{9,8},{10,9},{11,1... | collective-permute-start | bytes 1769480 | tf_op jit(solution)/shard_map/ppermute | solution.py:378
  62.9 0.7 copy-start.5
  63.6 5.3 %copy-start.2 = (bf16[4,8,32,128]{3,2,1,0:T(8,128)(2,1)}, bf16[4,8,32,128]{3,2,1,0:T(8,128)(2,1)S(1)}, u32[]{:S(2)}) copy-start(bf16[4,8,32,128]{3,2,1,0:T(8,128)(2,1)S(1)} %get-tuple-element.48) | copy-start | bytes 786436
  68.8 15.0 %collective-permute-start.18 = (f32[2,448,256]{2,1,0:T(8,128)S(1)}, f32[2,448,256]{2,1,0:T(8,128)S(1)}, u32[]{:S(2)}, u32[]{:S(2)}) collective-permute-start(f32[2,448,256]{2,1,0:T(8,128)S(1)} %get-tuple-element.68), channel_id=1, source_target_pairs={{0,1},{1,0},{2,3},{3,2},{4,5},{5,4},{6,7},{7,6},{8,9},{9,8},{10,11... | collective-permute-start | bytes 2752520 | tf_op jit(solution)/shard_map/ppermute | solution.py:369
  68.9 9.5 %collective-permute-start.12 = (bf16[8,64,128]{2,1,0:T(8,128)(2,1)S(1)}, bf16[8,64,128]{2,1,0:T(8,128)(2,1)S(1)}, u32[]{:S(2)}, u32[]{:S(2)}) collective-permute-start(bf16[8,64,128]{2,1,0:T(8,128)(2,1)S(1)} %get-tuple-element.51), channel_id=1, source_target_pairs={{0,1},{1,2},{2,3},{3,4},{4,5},{5,6},{6,7},{7,8},{8,9},{9,10},{10,1... | collective-permute-start | bytes 393224 | tf_op jit(solution)/shard_map/ppermute | solution.py:375
  72.4 6.3 %collective-permute-start.13 = (bf16[8,64,128]{2,1,0:T(8,128)(2,1)S(1)}, bf16[8,64,128]{2,1,0:T(8,128)(2,1)S(1)}, u32[]{:S(2)}, u32[]{:S(2)}) collective-permute-start(bf16[8,64,128]{2,1,0:T(8,128)(2,1)S(1)} %get-tuple-element.52), channel_id=1, source_target_pairs={{1,0},{2,1},{3,2},{4,3},{5,4},{6,5},{7,6},{8,7},{9,8},{10,9},{11,1... | collective-permute-start | bytes 393224 | tf_op jit(solution)/shard_map/ppermute | solution.py:378
  83.8 1.4 %copy-start.4 = (bf16[4,9,64,128]{3,2,1,0:T(8,128)(2,1)}, bf16[4,9,64,128]{3,2,1,0:T(8,128)(2,1)S(1)}, u32[]{:S(2)}) copy-start(bf16[4,9,64,128]{3,2,1,0:T(8,128)(2,1)S(1)} %get-tuple-element.65) | copy-start | bytes 1769476
  85.2 16.1 %all-to-all-start = ((bf16[16,56,256]{2,1,0:T(8,128)(2,1)}), bf16[16,56,256]{2,1,0:T(8,128)(2,1)S(1)}, u32[]{:S(2)}, u32[]{:S(2)}) async-start(bf16[16,56,256]{2,1,0:T(8,128)(2,1)} %bitcast.3), calls=%async_computation | async-start | bytes 917504 | tf_op jit(solution)/shard_map/all_to_all | solution.py:466
  92.1 24.5 %collective-permute-start.15 = (bf16[4,9,64,128]{3,2,1,0:T(8,128)(2,1)}, bf16[4,9,64,128]{3,2,1,0:T(8,128)(2,1)S(1)}, u32[]{:S(2)}, u32[]{:S(2)}) collective-permute-start(bf16[4,9,64,128]{3,2,1,0:T(8,128)(2,1)} %get-tuple-element.64), channel_id=1, source_target_pairs={{0,64},{32,96},{64,0},{96,32},{1,65},{33,97},{65,1},{97,33},{2,66}... | collective-permute-start | bytes 1769480 | tf_op jit(solution)/shard_map/ppermute | solution.py:372
  92.6 26.1 %collective-permute-start.16 = (bf16[4,9,64,128]{3,2,1,0:T(8,128)(2,1)}, bf16[4,9,64,128]{3,2,1,0:T(8,128)(2,1)S(1)}, u32[]{:S(2)}, u32[]{:S(2)}) collective-permute-start(bf16[4,9,64,128]{3,2,1,0:T(8,128)(2,1)} %copy-done.4), channel_id=1, source_target_pairs={{0,96},{32,0},{64,32},{96,64},{1,97},{33,1},{65,33},{97,65},{2,98}... | collective-permute-start | bytes 1769480 | tf_op jit(solution)/shard_map/ppermute | solution.py:372
  93.4 28.5 %collective-permute-start.14 = (bf16[4,9,64,128]{3,2,1,0:T(8,128)(2,1)S(1)}, bf16[4,9,64,128]{3,2,1,0:T(8,128)(2,1)}, u32[]{:S(2)}, u32[]{:S(2)}) collective-permute-start(bf16[4,9,64,128]{3,2,1,0:T(8,128)(2,1)S(1)} %get-tuple-element.63.first.second.third), channel_id=1, source_target_pairs={{0,32},{32,64},{64,96},{96,0},{1,33},{33,65},{65,97},{97,1},{2,34}... | collective-permute-start | bytes 1769480 | tf_op jit(solution)/shard_map/ppermute | solution.py:372
  101.2 14.0 %copy-start.6 = (bf16[4,8,32,128]{3,2,1,0:T(8,128)(2,1)S(1)}, bf16[4,8,32,128]{3,2,1,0:T(8,128)(2,1)}, u32[]{:S(2)}) copy-start(bf16[4,8,32,128]{3,2,1,0:T(8,128)(2,1)} %copy-done.5) | copy-start | bytes 786436
  111.6 22.8 %collective-permute-start.19 = (f32[448,256]{1,0:T(8,128)S(1)}, f32[448,256]{1,0:T(8,128)S(1)}, u32[]{:S(2)}, u32[]{:S(2)}) collective-permute-start(f32[448,256]{1,0:T(8,128)S(1)} %bitcast.5), channel_id=1, source_target_pairs={{0,1},{1,0},{2,3},{3,2},{4,5},{5,4},{6,7},{7,6},{8,9},{9,8},{10,11... | collective-permute-start | bytes 1376264 | tf_op jit(solution)/shard_map/ppermute | solution.py:369
  115.3 10.9 %collective-permute-start.11 = (bf16[4,8,32,128]{3,2,1,0:T(8,128)(2,1)S(1)}, bf16[4,8,32,128]{3,2,1,0:T(8,128)(2,1)S(1)}, u32[]{:S(2)}, u32[]{:S(2)}) collective-permute-start(bf16[4,8,32,128]{3,2,1,0:T(8,128)(2,1)S(1)} %copy-done.6), channel_id=1, source_target_pairs={{0,16},{16,0},{1,17},{17,1},{2,18},{18,2},{3,19},{19,3},{4,20},{20... | collective-permute-start | bytes 786440 | tf_op jit(solution)/shard_map/ppermute | solution.py:366
  121.9 4.3 %copy-start.3 = (bf16[4,8,32,128]{3,2,1,0:T(8,128)(2,1)S(1)}, bf16[4,8,32,128]{3,2,1,0:T(8,128)(2,1)}, u32[]{:S(2)}) copy-start(bf16[4,8,32,128]{3,2,1,0:T(8,128)(2,1)} %copy-done.2) | copy-start | bytes 786436
  123.3 9.7 %collective-permute-start.17 = (bf16[4,9,32,128]{3,2,1,0:T(8,128)(2,1)S(1)}, bf16[4,9,32,128]{3,2,1,0:T(8,128)(2,1)S(1)}, u32[]{:S(2)}, u32[]{:S(2)}) collective-permute-start(bf16[4,9,32,128]{3,2,1,0:T(8,128)(2,1)S(1)} %get-tuple-element.67), channel_id=1, source_target_pairs={{0,16},{16,0},{1,17},{17,1},{2,18},{18,2},{3,19},{19,3},{4,20},{20... | collective-permute-start | bytes 884744 | tf_op jit(solution)/shard_map/ppermute | solution.py:366

commit v4 on v3

--- a/solution.py
+++ b/solution.py
@@ -43,6 +43,7 @@
             total = total + jnp.dot(
                 kernel[3 * a + b], pair_of(ref, plane, row + b), preferred_element_type=F32
             )
+    others = cot_other[29 + 4 * plane_cot + row // 2]
     for r in range(2):
         part = total[:, 128 * r : 128 * r + 128]
         pre = (
@@ -54,12 +55,12 @@
         out_own[plane_out, row + r] = out[: outs // 2]
         out_other[plane_out, row + r] = out[outs // 2 :]
         cot = jnp.concatenate(
-            [cot_own[plane_cot, row + r], cot_other[plane_cot, row + r]], axis=0
+            [cot_own[plane_cot, row + r], others[:, 128 * r : 128 * r + 128]], axis=0
         ).astype(F32)
         grad[plane_out, row + r] = (cot * sig * (1.0 + pre * (1.0 - sig))).astype(BF16)
 
 
-def ready_body(at, kernel, bias, cotangent, after, kernel_out, cot_own, cot_sent):
+def ready_body(at, kernel, bias, cotangent, after, kernel_out, cot_own):
     half = at[1]
     kernel_out[:27] = kernel[...]
     rest = bias[...]
@@ -71,11 +72,12 @@
     for plane in range(4):
         for row in range(8):
             cot_own[plane, row] = cotangent[plane, 8 * half + row]
-            cot_sent[plane, row] = cotangent[plane, 8 - 8 * half + row]
+            place, low = 29 + 4 * plane + row // 2, 128 * (row % 2)
+            kernel_out[place, :, low : low + 128] = cotangent[plane, 8 - 8 * half + row]
 
 
 def rims_body(at, own_lo, own_hi, left_lo, left_hi, right_lo, right_hi, far_lo, far_hi,
-              kernel, cot, up_rim, down_rim):
+              kernel, up_rim, down_rim):
     for k, (lower, upper) in enumerate(
         ((own_lo, own_hi), (right_lo, right_hi), (far_lo, far_hi), (left_lo, left_hi))
     ):
@@ -84,7 +86,7 @@
 
 
 def inner_body(at, own_lo, own_hi, left_lo, left_hi, right_lo, right_hi, far_lo, far_hi,
-               kernel_own, kernel_other, cot_own, cot_other, out_own, out_other, grad,
+               kernel_own, kernel_other, cot_own, out_own, out_other, grad,
                field, kernel, bias):
     half, starts = at[1], starts_of(at[0])
     rows = own_lo.shape[1]
@@ -117,7 +119,7 @@
         plane, row = index // 4, 2 * lax.rem(index, 4)
         forward_rows(
             row, [(field, plane), (field, plane + 1), (field, plane + 2)], kernel, bias,
-            cot_own, cot_other, out_own, out_other, grad, plane + 1, plane,
+            cot_own, kernel_other, out_own, out_other, grad, plane + 1, plane,
         )
         return carry
 
@@ -390,21 +392,20 @@
     left_lo, right_hi = turn(own_lo, 1), turn(own_hi, -1)
     left_hi, right_lo = turn(own_hi, 1), turn(own_lo, -1)
     far_lo, far_hi = turn(left_lo, 1), turn(right_hi, -1)
-    kernel_sent, cot_own, cot_sent = call(
-        ready_body, 4,
-        [((29, 32, 256), BF16), ((4, 8, 32, 128), BF16), ((4, 8, 32, 128), BF16)],
+    kernel_sent, cot_own = call(
+        ready_body, 4, [((45, 32, 256), BF16), ((4, 8, 32, 128), BF16)],
         [], 10**6, 1,
     )(at, kernel, jnp.broadcast_to(bias[:, None], (32, 128)), cotangent, own_lo)
-    kernel_other, cot_other = swap(kernel_sent), swap(cot_sent)
-    up_rim, down_rim = call(rims_body, 9, [((4, 9, 64, 128), BF16)] * 2, [], 10**6, 2)(
+    kernel_other = swap(kernel_sent)
+    up_rim, down_rim = call(rims_body, 9, [((4, 9, 64, 128), BF16)] * 2, [], 10**6, 1)(
         at, own_lo, own_hi, left_lo, left_hi, right_lo, right_hi, far_lo, far_hi,
-        kernel_other, cot_other,
+        kernel_other,
     )
     low, high = up(up_rim), down(down_rim)
 
     flops = 36 * 10**8
     out_own, out_other, grad, field, taps, bias_wide = call(
-        inner_body, 13,
+        inner_body, 12,
         [
             ((2, 8, 32, 128), BF16), ((2, 8, 32, 128), BF16), ((2, 8, 64, 128), BF16),
             ((4, 10, 256, 128), BF16), ((9, 192, 256), BF16),
@@ -412,7 +413,7 @@
         ],
         [], flops // 2,
     )(at, own_lo, own_hi, left_lo, left_hi, right_lo, right_hi, far_lo, far_hi,
-      kernel_sent, kernel_other, cot_own, cot_other)
+      kernel_sent, kernel_other, cot_own)
     keep, give, turned, turned_edge = call(
         inner_weight_body, 4,
         [((2, 448, 256), F32)] * 2 + [((256, 1728), BF16), ((256, 576), BF16)],
@@ -425,7 +426,7 @@
             ((8, 64, 128), BF16), ((8, 64, 128), BF16), ((2, 10, 256, 128), BF16),
         ],
         [], flops // 2, 1,
-    )(at, field, low, high, taps, bias_wide, cot_own, cot_other,
+    )(at, field, low, high, taps, bias_wide, cot_own, kernel_other,
       out_own, out_other, grad, keep)
 
     got_out = swap(out_other)

time: 136 us -> 134 us (0.985)
  starting transfers between devices: 47.1 us -> 42.1 us
    ppermute x9, waiting for transfers between devices: 10.4 us -> 19 us  [turn(): return lax.ppermute(value, 'y', [(i, (i + step) % 4) for i in range(4)])]
    ppermute x5 -> x4, waiting for transfers between devices: 17.4 us -> 10.9 us  [swap(): return lax.ppermute(value, 'xh', [(0, 1), (1, 0)])]
    ppermute x2, starting transfers between devices: 12.3 us -> 7.23 us  [up(): return lax.ppermute(value, SPACE, [(i, i + 1) for i in range(15)])]
    ppermute x9, starting transfers between devices: 9.38 us -> 11.1 us  [turn(): return lax.ppermute(value, 'y', [(i, (i + step) % 4) for i in range(4)])]
    all_to_all x1, waiting for transfers between devices: 7.22 us -> 5.59 us  [on_device(): lax.all_to_all(chip.reshape(16, 56, 256), ('xh', 'z', 'xl'), 0, 0, tiled=...]
    ppermute x5 -> x4, starting transfers between devices: 10.9 us -> 10.9 us  [swap(): return lax.ppermute(value, 'xh', [(0, 1), (1, 0)])]
  transfers between devices with their start and end apart: 21 -> 20, of which waited for: 12 -> 11; matrix products, arithmetic and copies ran while one was open for 2% -> 2% of each run, Pallas kernels for 17% -> 17%
where the time goes in v4:
time: 134 us; the launch traced here: 133 us
  starting transfers between devices  42.1 us (31%)
  waiting for transfers between devices  39.2 us (29%)
  Pallas kernels  36.5 us (27%)
  blocking collectives  10.6 us (8%)
  local copies, waits for them, and re-layouts  2.88 us (2%)
    ppermute x9, waiting for transfers between devices, turn(): return lax.ppermute(value, 'y', [(i, (i + step) % 4) for i in range(4)])  19 us
    ppermute x9, starting transfers between devices, turn(): return lax.ppermute(value, 'y', [(i, (i + step) % 4) for i in range(4)])  11.1 us
    ppermute x4, waiting for transfers between devices, swap(): return lax.ppermute(value, 'xh', [(0, 1), (1, 0)])  10.9 us
    ppermute x4, starting transfers between devices, swap(): return lax.ppermute(value, 'xh', [(0, 1), (1, 0)])  10.9 us
    all_to_all x1, blocking collectives, on_device(): lax.all_to_all(copies, ('z', 'xl'), 0, 0, tiled=True).reshape(448, 256)  10.6 us
    ppermute x2, starting transfers between devices, up(): return lax.ppermute(value, SPACE, [(i, i + 1) for i in range(15)])  7.23 us
    all_to_all x1, starting transfers between devices, on_device(): lax.all_to_all(chip.reshape(16, 56, 256), ('xh', 'z', 'xl'), 0, 0, tiled=...  6.33 us
    pallas_call x1, Pallas kernels, on_device(): call(inner_weight_body, 4, [((2, 448, 256), F32)] * 2 + [((256, 1728), BF...  5.61 us
  transfers between devices with their start and end apart: 20, of which 11 were waited for; matrix products, arithmetic and copies ran while one was open for 2% of the time, Pallas kernels for 17%

profile of v4, /device:TPU:1, one launch (start us, length us, event | category | flops | bytes accessed | tf_op | source)
XLA Modules:
  0.0 133.3 jit_solution(17607845659220310796)
XLA Ops:
  1.7 3.7 %collective-permute-start = (bf16[4,9,32,128]{3,2,1,0:T(8,128)(2,1)S(1)}, bf16[4,9,32,128]{3,2,1,0:T(8,128)(2,1)S(1)}, u32[]{:S(2)}, u32[]{:S(2)}) collective-permute-start(bf16[4,9,32,128]{3,2,1,0:T(8,128)(2,1)S(1)} %constant_dynamic-slice_fusion.1), channel_id=1, source_target_pairs={{0,16},{16,0},{1,17},{17,1},{2,18},{18,2},{3,19},{19,3},{4,20},{20... | collective-permute-start | bytes 884744 | tf_op jit(solution)/shard_map/ppermute | solution.py:368
  6.5 5.2 %collective-permute-done = bf16[4,9,32,128]{3,2,1,0:T(8,128)(2,1)S(1)} collective-permute-done((bf16[4,9,32,128]{3,2,1,0:T(8,128)(2,1)S(1)}, bf16[4,9,32,128]{3,2,1,0:T(8,128)(2,1)S(1)}, u32[]{:S(2)}, u32[]{:S(2)}) %collective-permute-start) | collective-permute-done | bytes 294944 | tf_op jit(solution)/shard_map/ppermute | solution.py:368
  12.5 3.2 %collective-permute-start.7 = (bf16[45,32,256]{2,1,0:T(8,128)(2,1)S(1)}, bf16[45,32,256]{2,1,0:T(8,128)(2,1)S(1)}, u32[]{:S(2)}, u32[]{:S(2)}) collective-permute-start(bf16[45,32,256]{2,1,0:T(8,128)(2,1)S(1)} %get-tuple-element.35.kernel_own), channel_id=1, source_target_pairs={{0,16},{16,0},{1,17},{17,1},{2,18},{18,2},{3,19},{19,3},{4,20},{20... | collective-permute-start | bytes 2211848 | tf_op jit(solution)/shard_map/ppermute | solution.py:368
  17.1 1.5 %collective-permute-start.4 = (bf16[2,9,64,128]{3,2,1,0:T(8,128)(2,1)S(1)}, bf16[2,9,64,128]{3,2,1,0:T(8,128)(2,1)S(1)}, u32[]{:S(2)}, u32[]{:S(2)}) collective-permute-start(bf16[2,9,64,128]{3,2,1,0:T(8,128)(2,1)S(1)} %maximum_select_fusion.2.own_hi), channel_id=1, source_target_pairs={{0,96},{32,0},{64,32},{96,64},{1,97},{33,1},{65,33},{97,65},{2,98}... | collective-permute-start | bytes 884744 | tf_op jit(solution)/shard_map/ppermute | solution.py:374
  18.7 1.5 %collective-permute-start.3 = (bf16[2,9,64,128]{3,2,1,0:T(8,128)(2,1)S(1)}, bf16[2,9,64,128]{3,2,1,0:T(8,128)(2,1)S(1)}, u32[]{:S(2)}, u32[]{:S(2)}) collective-permute-start(bf16[2,9,64,128]{3,2,1,0:T(8,128)(2,1)S(1)} %maximum_select_fusion.1.after.own_lo), channel_id=1, source_target_pairs={{0,96},{32,0},{64,32},{96,64},{1,97},{33,1},{65,33},{97,65},{2,98}... | collective-permute-start | bytes 884744 | tf_op jit(solution)/shard_map/ppermute | solution.py:374
  20.1 3.6 %collective-permute-done.1.left_lo = bf16[2,9,64,128]{3,2,1,0:T(8,128)(2,1)S(1)} collective-permute-done((bf16[2,9,64,128]{3,2,1,0:T(8,128)(2,1)S(1)}, bf16[2,9,64,128]{3,2,1,0:T(8,128)(2,1)S(1)}, u32[]{:S(2)}, u32[]{:S(2)}) %collective-permute-start.1) | collective-permute-done | bytes 294944 | tf_op jit(solution)/shard_map/ppermute | solution.py:374
  23.7 2.7 %collective-permute-start.6 = (bf16[2,9,64,128]{3,2,1,0:T(8,128)(2,1)S(1)}, bf16[2,9,64,128]{3,2,1,0:T(8,128)(2,1)S(1)}, u32[]{:S(2)}, u32[]{:S(2)}) collective-permute-start(bf16[2,9,64,128]{3,2,1,0:T(8,128)(2,1)S(1)} %collective-permute-done.4.right_hi), channel_id=1, source_target_pairs={{0,96},{32,0},{64,32},{96,64},{1,97},{33,1},{65,33},{97,65},{2,98}... | collective-permute-start | bytes 884744 | tf_op jit(solution)/shard_map/ppermute | solution.py:374
  26.4 3.5 %collective-permute-done.3.right_lo = bf16[2,9,64,128]{3,2,1,0:T(8,128)(2,1)S(1)} collective-permute-done((bf16[2,9,64,128]{3,2,1,0:T(8,128)(2,1)S(1)}, bf16[2,9,64,128]{3,2,1,0:T(8,128)(2,1)S(1)}, u32[]{:S(2)}, u32[]{:S(2)}) %collective-permute-start.3) | collective-permute-done | bytes 294944 | tf_op jit(solution)/shard_map/ppermute | solution.py:374
  30.4 6.3 %collective-permute-done.5.far_lo = bf16[2,9,64,128]{3,2,1,0:T(8,128)(2,1)S(1)} collective-permute-done((bf16[2,9,64,128]{3,2,1,0:T(8,128)(2,1)S(1)}, bf16[2,9,64,128]{3,2,1,0:T(8,128)(2,1)S(1)}, u32[]{:S(2)}, u32[]{:S(2)}) %collective-permute-start.5) | collective-permute-done | bytes 294944 | tf_op jit(solution)/shard_map/ppermute | solution.py:374
  37.4 4.6 %collective-permute-start.8 = (bf16[4,9,64,128]{3,2,1,0:T(8,128)(2,1)S(1)}, bf16[4,9,64,128]{3,2,1,0:T(8,128)(2,1)S(1)}, u32[]{:S(2)}, u32[]{:S(2)}) collective-permute-start(bf16[4,9,64,128]{3,2,1,0:T(8,128)(2,1)S(1)} %get-tuple-element.38), channel_id=1, source_target_pairs={{0,1},{1,2},{2,3},{3,4},{4,5},{5,6},{6,7},{7,8},{8,9},{9,10},{10,1... | collective-permute-start | bytes 1769480 | tf_op jit(solution)/shard_map/ppermute | solution.py:377
  42.0 1.9 %collective-permute-start.9 = (bf16[4,9,64,128]{3,2,1,0:T(8,128)(2,1)S(1)}, bf16[4,9,64,128]{3,2,1,0:T(8,128)(2,1)S(1)}, u32[]{:S(2)}, u32[]{:S(2)}) collective-permute-start(bf16[4,9,64,128]{3,2,1,0:T(8,128)(2,1)S(1)} %get-tuple-element.39), channel_id=1, source_target_pairs={{1,0},{2,1},{3,2},{4,3},{5,4},{6,5},{7,6},{8,7},{9,8},{10,9},{11,1... | collective-permute-start | bytes 1769480 | tf_op jit(solution)/shard_map/ppermute | solution.py:380
  43.9 5.0 %shard_map.68 = (bf16[2,8,32,128]{3,2,1,0:T(8,128)(2,1)S(1)}, bf16[2,8,32,128]{3,2,1,0:T(8,128)(2,1)S(1)}, bf16[2,8,64,128]{3,2,1,0:T(8,128)(2,1)S(1)}, bf16[4,1...) custom-call(s32[3]{0:T(128)S(1)} %pad_add_fusion.at, ...), custom_call_target="tpu_custom_call" | custom-call | flops 1800000000 | bytes 8388608 | tf_op jit(solution)/shard_map/pallas_call | solution.py:407
  49.0 5.6 %shard_map.70 = (f32[2,448,256]{2,1,0:T(8,128)S(1)}, f32[2,448,256]{2,1,0:T(8,128)S(1)}, bf16[256,1728]{1,0:T(8,128)(2,1)S(1)}, bf16[256,576]{1,0:T(8,128)(2,1)S(1)}) custom-call(s32[3]{0:T(128)S(1)} %pad_add_fusion.at, bf16[4,10,256,128]{3,2,1,0:T(8,128)(2,1)S(1)} %get-tuple-element.37.field, bf16[2,8,64,128]{3,2,1,0:T(8,128)(2,1)S(1)} %get-tuple-element.44.grad.in_grad, ...), custom_call_target="tpu_custom_call" | custom-call | flops 1800000000 | bytes 8388608 | tf_op jit(solution)/shard_map/pallas_call | solution.py:417
  54.6 3.5 %collective-permute-done.9.high = bf16[4,9,64,128]{3,2,1,0:T(8,128)(2,1)S(1)} collective-permute-done((bf16[4,9,64,128]{3,2,1,0:T(8,128)(2,1)S(1)}, bf16[4,9,64,128]{3,2,1,0:T(8,128)(2,1)S(1)}, u32[]{:S(2)}, u32[]{:S(2)}) %collective-permute-start.9) | collective-permute-done | bytes 589856 | tf_op jit(solution)/shard_map/ppermute | solution.py:380
  58.1 3.8 %shard_map.71 = (bf16[4,8,32,128]{3,2,1,0:T(8,128)(2,1)S(1)}, bf16[4,8,32,128]{3,2,1,0:T(8,128)(2,1)S(1)}, bf16[4,8,64,128]{3,2,1,0:T(8,128)(2,1)S(1)}, bf16[8,6...) custom-call(s32[3]{0:T(128)S(1)} %pad_add_fusion.at, ...), custom_call_target="tpu_custom_call" | custom-call | flops 1800000000 | bytes 8388608 | tf_op jit(solution)/shard_map/pallas_call | solution.py:422
  62.6 5.3 %shard_map.72 = (f32[2,448,256]{2,1,0:T(8,128)S(1)}, f32[2,448,256]{2,1,0:T(8,128)S(1)}) custom-call(s32[3]{0:T(128)S(1)} %pad_add_fusion.at, bf16[4,10,256,128]{3,2,1,0:T(8,128)(2,1)S(1)} %get-tuple-element.37.field, bf16[2,10,256,128]{3,2,1,0:T(8,128)(2,1)S(1)} %get-tuple-element.53.rim, bf16[4,8,64,128]{3,2,1,0:T(8,128)(2,1)S(1)} %get-tuple-element.48.grad.after, ...), custom_call_target="tpu_custom_call" | custom-call | flops 1800000000 | bytes 8388608 | tf_op jit(solution)/shard_map/pallas_call | solution.py:454
  68.0 2.6 %collective-permute-start.11 = (bf16[8,64,128]{2,1,0:T(8,128)(2,1)S(1)}, bf16[8,64,128]{2,1,0:T(8,128)(2,1)S(1)}, u32[]{:S(2)}, u32[]{:S(2)}) collective-permute-start(bf16[8,64,128]{2,1,0:T(8,128)(2,1)S(1)} %get-tuple-element.49), channel_id=1, source_target_pairs={{0,1},{1,2},{2,3},{3,4},{4,5},{5,6},{6,7},{7,8},{8,9},{9,10},{10,1... | collective-permute-start | bytes 393224 | tf_op jit(solution)/shard_map/ppermute | solution.py:377
  70.6 1.9 %collective-permute-start.12 = (bf16[8,64,128]{2,1,0:T(8,128)(2,1)S(1)}, bf16[8,64,128]{2,1,0:T(8,128)(2,1)S(1)}, u32[]{:S(2)}, u32[]{:S(2)}) collective-permute-start(bf16[8,64,128]{2,1,0:T(8,128)(2,1)S(1)} %get-tuple-element.50), channel_id=1, source_target_pairs={{1,0},{2,1},{3,2},{4,3},{5,4},{6,5},{7,6},{8,7},{9,8},{10,9},{11,1... | collective-permute-start | bytes 393224 | tf_op jit(solution)/shard_map/ppermute | solution.py:380
  72.6 4.1 %shard_map.73 = (f32[2,9,64,128]{3,2,1,0:T(8,128)S(1)}, bf16[2,9,64,128]{3,2,1,0:T(8,128)(2,1)S(1)}, bf16[2,9,64,128]{3,2,1,0:T(8,128)(2,1)S(1)}, bf16[2,9,64,128]{3,2,1,0:T(8,128)(2,1)S(1)}) custom-call(s32[3]{0:T(128)S(1)} %pad_add_fusion.at, bf16[4,8,64,128]{3,2,1,0:T(8,128)(2,1)S(1)} %get-tuple-element.48.grad.after, ...), custom_call_target="tpu_custom_call" | custom-call | flops 1800000000 | bytes 8388608 | tf_op jit(solution)/shard_map/pallas_call | solution.py:458
  76.9 5.1 %shard_map.74 = (f32[4,9,64,128]{3,2,1,0:T(8,128)S(1)}, bf16[4,9,64,128]{3,2,1,0:T(8,128)(2,1)S(1)}, bf16[4,9,64,128]{3,2,1,0:T(8,128)(2,1)}, bf16[4,9,64,128]{3,2,1,0:T(8,128)(2,1)S(1)}) custom-call(s32[3]{0:T(128)S(1)} %pad_add_fusion.at, bf16[4,8,64,128]{3,2,1,0:T(8,128)(2,1)S(1)} %get-tuple-element.48.grad.after, ...), custom_call_target="tpu_custom_call" | custom-call | flops 1800000000 | bytes 8388608 | tf_op jit(solution)/shard_map/pallas_call | solution.py:461
  82.0 1.4 %shard_map.77 = bf16[2,448,256]{2,1,0:T(8,128)(2,1)} custom-call(s32[3]{0:T(128)S(1)} %pad_add_fusion.at, f32[2,448,256]{2,1,0:T(8,128)S(1)} %get-tuple-element.55.after.refs_4_.keep, f32[2,448,256]{2,1,0:T(8,128)S(1)} %collective-permute-done.17.got, bf16[4,9,64,128]{3,2,1,0:T(8,128)(2,1)S(1)} %get-tuple-element.61.first.second.third, ...), custom_call_target="tpu_custom_call" | custom-call | flops 1000000 | bytes 8388608 | tf_op jit(solution)/shard_map/pallas_call | solution.py:464
  83.4 6.3 %all-to-all-start = ((bf16[16,56,256]{2,1,0:T(8,128)(2,1)}), bf16[16,56,256]{2,1,0:T(8,128)(2,1)S(1)}, u32[]{:S(2)}, u32[]{:S(2)}) async-start(bf16[16,56,256]{2,1,0:T(8,128)(2,1)} %bitcast.3), calls=%async_computation | async-start | bytes 917504 | tf_op jit(solution)/shard_map/all_to_all | solution.py:467
  89.8 2.7 %collective-permute-start.14 = (bf16[4,9,64,128]{3,2,1,0:T(8,128)(2,1)}, bf16[4,9,64,128]{3,2,1,0:T(8,128)(2,1)S(1)}, u32[]{:S(2)}, u32[]{:S(2)}) collective-permute-start(bf16[4,9,64,128]{3,2,1,0:T(8,128)(2,1)} %get-tuple-element.62), channel_id=1, source_target_pairs={{0,64},{32,96},{64,0},{96,32},{1,65},{33,97},{65,1},{97,33},{2,66}... | collective-permute-start | bytes 1769480 | tf_op jit(solution)/shard_map/ppermute | solution.py:374
  93.9 5.6 %all-to-all-done.pieces = bf16[16,56,256]{2,1,0:T(8,128)(2,1)S(1)} async-done(((bf16[16,56,256]{2,1,0:T(8,128)(2,1)}), bf16[16,56,256]{2,1,0:T(8,128)(2,1)S(1)}, u32[]{:S(2)}, u32[]{:S(2)}) %all-to-all-start) | async-done | bytes 458784 | tf_op jit(solution)/shard_map/all_to_all | solution.py:467
  100.1 10.6 %all_to_all.10 = f32[8,56,256]{2,1,0:T(8,128)S(1)} all-to-all(f32[8,56,256]{2,1,0:T(8,128)S(1)} %shard_map.78), channel_id=1, replica_groups=mesh['y'=4,'xh'=2,'z'=4,'xl'=2,'core'=2] {'z','xl'}, dimensions={0} | all-to-all | bytes 917504 | tf_op jit(solution)/shard_map/all_to_all | solution.py:476
  110.7 2.7 %collective-permute-start.18 = (f32[448,256]{1,0:T(8,128)S(1)}, f32[448,256]{1,0:T(8,128)S(1)}, u32[]{:S(2)}, u32[]{:S(2)}) collective-permute-start(f32[448,256]{1,0:T(8,128)S(1)} %bitcast.5), channel_id=1, source_target_pairs={{0,1},{1,0},{2,3},{3,2},{4,5},{5,4},{6,7},{7,6},{8,9},{9,8},{10,11... | collective-permute-start | bytes 1376264 | tf_op jit(solution)/shard_map/ppermute | solution.py:371
  114.5 4.3 %collective-permute-done.15.back = bf16[4,9,64,128]{3,2,1,0:T(8,128)(2,1)S(1)} collective-permute-done((bf16[4,9,64,128]{3,2,1,0:T(8,128)(2,1)}, bf16[4,9,64,128]{3,2,1,0:T(8,128)(2,1)S(1)}, u32[]{:S(2)}, u32[]{:S(2)}) %collective-permute-start.15) | collective-permute-done | bytes 589856 | tf_op jit(solution)/shard_map/ppermute | solution.py:374
  119.5 1.4 %shard_map.75 = (f32[4,9,32,128]{3,2,1,0:T(8,128)S(1)}, bf16[4,9,32,128]{3,2,1,0:T(8,128)(2,1)S(1)}) custom-call(s32[3]{0:T(128)S(1)} %pad_add_fusion.at, f32[4,9,64,128]{3,2,1,0:T(8,128)S(1)} %get-tuple-element.60.own, bf16[4,9,64,128]{3,2,1,0:T(8,128)(2,1)} %collective-permute-done.13.near, bf16[4,9,64,128]{3,2,1,0:T(8,128)(2,1)S(1)} %collective-permute-done.14.far, ...), custom_call_target="tpu_custom_call" | custom-call | flops 1000000 | bytes 8388608 | tf_op jit(solution)/shard_map/pallas_call | solution.py:471
  120.9 2.9 %collective-permute-start.16 = (bf16[4,9,32,128]{3,2,1,0:T(8,128)(2,1)S(1)}, bf16[4,9,32,128]{3,2,1,0:T(8,128)(2,1)S(1)}, u32[]{:S(2)}, u32[]{:S(2)}) collective-permute-start(bf16[4,9,32,128]{3,2,1,0:T(8,128)(2,1)S(1)} %get-tuple-element.65), channel_id=1, source_target_pairs={{0,16},{16,0},{1,17},{17,1},{2,18},{18,2},{3,19},{19,3},{4,20},{20... | collective-permute-start | bytes 884744 | tf_op jit(solution)/shard_map/ppermute | solution.py:368
  124.6 5.7 %collective-permute-done.16.got = bf16[4,9,32,128]{3,2,1,0:T(8,128)(2,1)S(1)} collective-permute-done((bf16[4,9,32,128]{3,2,1,0:T(8,128)(2,1)S(1)}, bf16[4,9,32,128]{3,2,1,0:T(8,128)(2,1)S(1)}, u32[]{:S(2)}, u32[]{:S(2)}) %collective-permute-start.16) | collective-permute-done | bytes 294944 | tf_op jit(solution)/shard_map/ppermute | solution.py:368
  130.3 1.4 %shard_map.76 = bf16[4,16,32,128]{3,2,1,0:T(8,128)(2,1)} custom-call(s32[3]{0:T(128)S(1)} %pad_add_fusion.at, f32[4,9,32,128]{3,2,1,0:T(8,128)S(1)} %get-tuple-element.64.kept, bf16[4,9,32,128]{3,2,1,0:T(8,128)(2,1)S(1)} %collective-permute-done.16.got), custom_call_target="tpu_custom_call" | custom-call | flops 1000000 | bytes 8388608 | tf_op jit(solution)/shard_map/pallas_call | solution.py:480
  131.7 1.5 %shard_map.79 = f32[27,32,256]{2,1,0:T(8,128)} custom-call(s32[3]{0:T(128)S(1)} %pad_add_fusion.at, f32[448,256]{1,0:T(8,128)S(1)} %bitcast.6, f32[448,256]{1,0:T(8,128)S(1)} %collective-permute-done.18.other), custom_call_target="tpu_custom_call" | custom-call | flops 1000000 | bytes 8388608 | tf_op jit(solution)/shard_map/pallas_call | solution.py:477
  (46 shorter events, 11.5 us)
Async XLA Ops:
  0.6 11.2 %copy-start = (bf16[4,16,32,128]{3,2,1,0:T(8,128)(2,1)S(1)}, bf16[4,16,32,128]{3,2,1,0:T(8,128)(2,1)}, u32[]{:S(2)}) copy-start(bf16[4,16,32,128]{3,2,1,0:T(8,128)(2,1)} %cotangent.1) | copy-start | bytes 1572868
  0.6 11.2 %copy-start.1 = (bf16[27,32,256]{2,1,0:T(8,128)(2,1)S(1)}, bf16[27,32,256]{2,1,0:T(8,128)(2,1)}, u32[]{:S(2)}) copy-start(bf16[27,32,256]{2,1,0:T(8,128)(2,1)} %kernel.1) | copy-start | bytes 1327108
  0.7 11.1 %copy-start.7 = (f32[32]{0:T(128)S(1)}, f32[32]{0:T(128)}, u32[]{:S(2)}) copy-start(f32[32]{0:T(128)} %param.6) | copy-start | bytes 388
  1.7 9.9 %collective-permute-start = (bf16[4,9,32,128]{3,2,1,0:T(8,128)(2,1)S(1)}, bf16[4,9,32,128]{3,2,1,0:T(8,128)(2,1)S(1)}, u32[]{:S(2)}, u32[]{:S(2)}) collective-permute-start(bf16[4,9,32,128]{3,2,1,0:T(8,128)(2,1)S(1)} %constant_dynamic-slice_fusion.1), channel_id=1, source_target_pairs={{0,16},{16,0},{1,17},{17,1},{2,18},{18,2},{3,19},{19,3},{4,20},{20... | collective-permute-start | bytes 884744 | tf_op jit(solution)/shard_map/ppermute | solution.py:368
  12.5 24.2 %collective-permute-start.7 = (bf16[45,32,256]{2,1,0:T(8,128)(2,1)S(1)}, bf16[45,32,256]{2,1,0:T(8,128)(2,1)S(1)}, u32[]{:S(2)}, u32[]{:S(2)}) collective-permute-start(bf16[45,32,256]{2,1,0:T(8,128)(2,1)S(1)} %get-tuple-element.35.kernel_own), channel_id=1, source_target_pairs={{0,16},{16,0},{1,17},{17,1},{2,18},{18,2},{3,19},{19,3},{4,20},{20... | collective-permute-start | bytes 2211848 | tf_op jit(solution)/shard_map/ppermute | solution.py:368
  15.7 8.0 %collective-permute-start.1 = (bf16[2,9,64,128]{3,2,1,0:T(8,128)(2,1)S(1)}, bf16[2,9,64,128]{3,2,1,0:T(8,128)(2,1)S(1)}, u32[]{:S(2)}, u32[]{:S(2)}) collective-permute-start(bf16[2,9,64,128]{3,2,1,0:T(8,128)(2,1)S(1)} %maximum_select_fusion.1.after.own_lo), channel_id=1, source_target_pairs={{0,32},{32,64},{64,96},{96,0},{1,33},{33,65},{65,97},{97,1},{2,34}... | collective-permute-start | bytes 884744 | tf_op jit(solution)/shard_map/ppermute | solution.py:374
  17.1 6.6 %collective-permute-start.4 = (bf16[2,9,64,128]{3,2,1,0:T(8,128)(2,1)S(1)}, bf16[2,9,64,128]{3,2,1,0:T(8,128)(2,1)S(1)}, u32[]{:S(2)}, u32[]{:S(2)}) collective-permute-start(bf16[2,9,64,128]{3,2,1,0:T(8,128)(2,1)S(1)} %maximum_select_fusion.2.own_hi), channel_id=1, source_target_pairs={{0,96},{32,0},{64,32},{96,64},{1,97},{33,1},{65,33},{97,65},{2,98}... | collective-permute-start | bytes 884744 | tf_op jit(solution)/shard_map/ppermute | solution.py:374
  18.7 11.3 %collective-permute-start.3 = (bf16[2,9,64,128]{3,2,1,0:T(8,128)(2,1)S(1)}, bf16[2,9,64,128]{3,2,1,0:T(8,128)(2,1)S(1)}, u32[]{:S(2)}, u32[]{:S(2)}) collective-permute-start(bf16[2,9,64,128]{3,2,1,0:T(8,128)(2,1)S(1)} %maximum_select_fusion.1.after.own_lo), channel_id=1, source_target_pairs={{0,96},{32,0},{64,32},{96,64},{1,97},{33,1},{65,33},{97,65},{2,98}... | collective-permute-start | bytes 884744 | tf_op jit(solution)/shard_map/ppermute | solution.py:374
  20.1 10.3 %collective-permute-start.2 = (bf16[2,9,64,128]{3,2,1,0:T(8,128)(2,1)S(1)}, bf16[2,9,64,128]{3,2,1,0:T(8,128)(2,1)S(1)}, u32[]{:S(2)}, u32[]{:S(2)}) collective-permute-start(bf16[2,9,64,128]{3,2,1,0:T(8,128)(2,1)S(1)} %maximum_select_fusion.2.own_hi), channel_id=1, source_target_pairs={{0,32},{32,64},{64,96},{96,0},{1,33},{33,65},{65,97},{97,1},{2,34}... | collective-permute-start | bytes 884744 | tf_op jit(solution)/shard_map/ppermute | solution.py:374
  23.7 13.0 %collective-permute-start.5 = (bf16[2,9,64,128]{3,2,1,0:T(8,128)(2,1)S(1)}, bf16[2,9,64,128]{3,2,1,0:T(8,128)(2,1)S(1)}, u32[]{:S(2)}, u32[]{:S(2)}) collective-permute-start(bf16[2,9,64,128]{3,2,1,0:T(8,128)(2,1)S(1)} %collective-permute-done.1.left_lo), channel_id=1, source_target_pairs={{0,32},{32,64},{64,96},{96,0},{1,33},{33,65},{65,97},{97,1},{2,34}... | collective-permute-start | bytes 884744 | tf_op jit(solution)/shard_map/ppermute | solution.py:374
  23.7 13.0 %collective-permute-start.6 = (bf16[2,9,64,128]{3,2,1,0:T(8,128)(2,1)S(1)}, bf16[2,9,64,128]{3,2,1,0:T(8,128)(2,1)S(1)}, u32[]{:S(2)}, u32[]{:S(2)}) collective-permute-start(bf16[2,9,64,128]{3,2,1,0:T(8,128)(2,1)S(1)} %collective-permute-done.4.right_hi), channel_id=1, source_target_pairs={{0,96},{32,0},{64,32},{96,64},{1,97},{33,1},{65,33},{97,65},{2,98}... | collective-permute-start | bytes 884744 | tf_op jit(solution)/shard_map/ppermute | solution.py:374
  37.4 17.3 %collective-permute-start.8 = (bf16[4,9,64,128]{3,2,1,0:T(8,128)(2,1)S(1)}, bf16[4,9,64,128]{3,2,1,0:T(8,128)(2,1)S(1)}, u32[]{:S(2)}, u32[]{:S(2)}) collective-permute-start(bf16[4,9,64,128]{3,2,1,0:T(8,128)(2,1)S(1)} %get-tuple-element.38), channel_id=1, source_target_pairs={{0,1},{1,2},{2,3},{3,4},{4,5},{5,6},{6,7},{7,8},{8,9},{9,10},{10,1... | collective-permute-start | bytes 1769480 | tf_op jit(solution)/shard_map/ppermute | solution.py:377
  42.0 16.1 %collective-permute-start.9 = (bf16[4,9,64,128]{3,2,1,0:T(8,128)(2,1)S(1)}, bf16[4,9,64,128]{3,2,1,0:T(8,128)(2,1)S(1)}, u32[]{:S(2)}, u32[]{:S(2)}) collective-permute-start(bf16[4,9,64,128]{3,2,1,0:T(8,128)(2,1)S(1)} %get-tuple-element.39), channel_id=1, source_target_pairs={{1,0},{2,1},{3,2},{4,3},{5,4},{6,5},{7,6},{8,7},{9,8},{10,9},{11,1... | collective-permute-start | bytes 1769480 | tf_op jit(solution)/shard_map/ppermute | solution.py:380
  61.9 0.7 copy-start.5
  62.6 5.3 %copy-start.2 = (bf16[4,8,32,128]{3,2,1,0:T(8,128)(2,1)}, bf16[4,8,32,128]{3,2,1,0:T(8,128)(2,1)S(1)}, u32[]{:S(2)}) copy-start(bf16[4,8,32,128]{3,2,1,0:T(8,128)(2,1)S(1)} %get-tuple-element.46) | copy-start | bytes 786436
  68.0 14.1 %collective-permute-start.17 = (f32[2,448,256]{2,1,0:T(8,128)S(1)}, f32[2,448,256]{2,1,0:T(8,128)S(1)}, u32[]{:S(2)}, u32[]{:S(2)}) collective-permute-start(f32[2,448,256]{2,1,0:T(8,128)S(1)} %get-tuple-element.66), channel_id=1, source_target_pairs={{0,1},{1,0},{2,3},{3,2},{4,5},{5,4},{6,7},{7,6},{8,9},{9,8},{10,11... | collective-permute-start | bytes 2752520 | tf_op jit(solution)/shard_map/ppermute | solution.py:371
  68.0 8.6 %collective-permute-start.11 = (bf16[8,64,128]{2,1,0:T(8,128)(2,1)S(1)}, bf16[8,64,128]{2,1,0:T(8,128)(2,1)S(1)}, u32[]{:S(2)}, u32[]{:S(2)}) collective-permute-start(bf16[8,64,128]{2,1,0:T(8,128)(2,1)S(1)} %get-tuple-element.49), channel_id=1, source_target_pairs={{0,1},{1,2},{2,3},{3,4},{4,5},{5,6},{6,7},{7,8},{8,9},{9,10},{10,1... | collective-permute-start | bytes 393224 | tf_op jit(solution)/shard_map/ppermute | solution.py:377
  70.6 6.3 %collective-permute-start.12 = (bf16[8,64,128]{2,1,0:T(8,128)(2,1)S(1)}, bf16[8,64,128]{2,1,0:T(8,128)(2,1)S(1)}, u32[]{:S(2)}, u32[]{:S(2)}) collective-permute-start(bf16[8,64,128]{2,1,0:T(8,128)(2,1)S(1)} %get-tuple-element.50), channel_id=1, source_target_pairs={{1,0},{2,1},{3,2},{4,3},{5,4},{6,5},{7,6},{8,7},{9,8},{10,9},{11,1... | collective-permute-start | bytes 393224 | tf_op jit(solution)/shard_map/ppermute | solution.py:380
  82.0 1.4 %copy-start.4 = (bf16[4,9,64,128]{3,2,1,0:T(8,128)(2,1)}, bf16[4,9,64,128]{3,2,1,0:T(8,128)(2,1)S(1)}, u32[]{:S(2)}) copy-start(bf16[4,9,64,128]{3,2,1,0:T(8,128)(2,1)S(1)} %get-tuple-element.63) | copy-start | bytes 1769476
  83.4 16.1 %all-to-all-start = ((bf16[16,56,256]{2,1,0:T(8,128)(2,1)}), bf16[16,56,256]{2,1,0:T(8,128)(2,1)S(1)}, u32[]{:S(2)}, u32[]{:S(2)}) async-start(bf16[16,56,256]{2,1,0:T(8,128)(2,1)} %bitcast.3), calls=%async_computation | async-start | bytes 917504 | tf_op jit(solution)/shard_map/all_to_all | solution.py:467
  89.8 24.8 %collective-permute-start.14 = (bf16[4,9,64,128]{3,2,1,0:T(8,128)(2,1)}, bf16[4,9,64,128]{3,2,1,0:T(8,128)(2,1)S(1)}, u32[]{:S(2)}, u32[]{:S(2)}) collective-permute-start(bf16[4,9,64,128]{3,2,1,0:T(8,128)(2,1)} %get-tuple-element.62), channel_id=1, source_target_pairs={{0,64},{32,96},{64,0},{96,32},{1,65},{33,97},{65,1},{97,33},{2,66}... | collective-permute-start | bytes 1769480 | tf_op jit(solution)/shard_map/ppermute | solution.py:374
  92.5 26.3 %collective-permute-start.15 = (bf16[4,9,64,128]{3,2,1,0:T(8,128)(2,1)}, bf16[4,9,64,128]{3,2,1,0:T(8,128)(2,1)S(1)}, u32[]{:S(2)}, u32[]{:S(2)}) collective-permute-start(bf16[4,9,64,128]{3,2,1,0:T(8,128)(2,1)} %copy-done.4), channel_id=1, source_target_pairs={{0,96},{32,0},{64,32},{96,64},{1,97},{33,1},{65,33},{97,65},{2,98}... | collective-permute-start | bytes 1769480 | tf_op jit(solution)/shard_map/ppermute | solution.py:374
  93.5 26.0 %collective-permute-start.13 = (bf16[4,9,64,128]{3,2,1,0:T(8,128)(2,1)S(1)}, bf16[4,9,64,128]{3,2,1,0:T(8,128)(2,1)}, u32[]{:S(2)}, u32[]{:S(2)}) collective-permute-start(bf16[4,9,64,128]{3,2,1,0:T(8,128)(2,1)S(1)} %get-tuple-element.61.first.second.third), channel_id=1, source_target_pairs={{0,32},{32,64},{64,96},{96,0},{1,33},{33,65},{65,97},{97,1},{2,34}... | collective-permute-start | bytes 1769480 | tf_op jit(solution)/shard_map/ppermute | solution.py:374
  99.5 13.8 %copy-start.6 = (bf16[4,8,32,128]{3,2,1,0:T(8,128)(2,1)S(1)}, bf16[4,8,32,128]{3,2,1,0:T(8,128)(2,1)}, u32[]{:S(2)}) copy-start(bf16[4,8,32,128]{3,2,1,0:T(8,128)(2,1)} %copy-done.5) | copy-start | bytes 786436
  110.7 21.0 %collective-permute-start.18 = (f32[448,256]{1,0:T(8,128)S(1)}, f32[448,256]{1,0:T(8,128)S(1)}, u32[]{:S(2)}, u32[]{:S(2)}) collective-permute-start(f32[448,256]{1,0:T(8,128)S(1)} %bitcast.5), channel_id=1, source_target_pairs={{0,1},{1,0},{2,3},{3,2},{4,5},{5,4},{6,7},{7,6},{8,9},{9,8},{10,11... | collective-permute-start | bytes 1376264 | tf_op jit(solution)/shard_map/ppermute | solution.py:371
  113.4 10.4 %collective-permute-start.10 = (bf16[4,8,32,128]{3,2,1,0:T(8,128)(2,1)S(1)}, bf16[4,8,32,128]{3,2,1,0:T(8,128)(2,1)S(1)}, u32[]{:S(2)}, u32[]{:S(2)}) collective-permute-start(bf16[4,8,32,128]{3,2,1,0:T(8,128)(2,1)S(1)} %copy-done.6), channel_id=1, source_target_pairs={{0,16},{16,0},{1,17},{17,1},{2,18},{18,2},{3,19},{19,3},{4,20},{20... | collective-permute-start | bytes 786440 | tf_op jit(solution)/shard_map/ppermute | solution.py:368
  119.5 4.3 %copy-start.3 = (bf16[4,8,32,128]{3,2,1,0:T(8,128)(2,1)S(1)}, bf16[4,8,32,128]{3,2,1,0:T(8,128)(2,1)}, u32[]{:S(2)}) copy-start(bf16[4,8,32,128]{3,2,1,0:T(8,128)(2,1)} %copy-done.2) | copy-start | bytes 786436
  120.9 9.4 %collective-permute-start.16 = (bf16[4,9,32,128]{3,2,1,0:T(8,128)(2,1)S(1)}, bf16[4,9,32,128]{3,2,1,0:T(8,128)(2,1)S(1)}, u32[]{:S(2)}, u32[]{:S(2)}) collective-permute-start(bf16[4,9,32,128]{3,2,1,0:T(8,128)(2,1)S(1)} %get-tuple-element.65), channel_id=1, source_target_pairs={{0,16},{16,0},{1,17},{17,1},{2,18},{18,2},{3,19},{19,3},{4,20},{20... | collective-permute-start | bytes 884744 | tf_op jit(solution)/shard_map/ppermute | solution.py:368

commit v5 on v4

--- a/solution.py
+++ b/solution.py
@@ -171,14 +171,15 @@
     for a in range(3):
 
         def step(b, carry):
-            total = jnp.zeros((3 * outs, 256), F32)
+            total = jnp.zeros((256, 3 * outs), F32)
             for k in range(planes):
                 grads = jnp.concatenate([stacked[k, row] for row in range(rows)], axis=1)
                 ref, plane = cells_of(k, a)
                 cells = jnp.concatenate([ref[plane, row + b] for row in range(rows)], axis=1)
                 total = total + lax.dot_general(
-                    grads, cells, (((1,), (1,)), ((), ())), preferred_element_type=F32
+                    cells, grads, (((1,), (1,)), ((), ())), preferred_element_type=F32
                 )
+            total = total.T
             for c in range(3):
                 line = pl.multiple_of(16 * (9 * a + 3 * b + c), 16)
                 for side in range(2):
@@ -288,7 +289,7 @@
     input_terms(at, lines, [(0, 0), (3, 3)], turned, turned_edge, outs, stacked, held)
 
 
-def total_body(at, own, near, far, back, kept, sent):
+def total_body(at, own, near, far, back, kept, edges, sent):
     half = at[1]
     mine = pl.multiple_of(32 * half, 32)
     others = pl.multiple_of(32 * (1 - half), 32)
@@ -300,24 +301,25 @@
         return value
 
     for plane in range(4):
+        for row in range(8):
+            kept[plane, row] = sums(plane, row, mine).astype(BF16)
+        edges[plane, 0] = sums(plane, 7 * (1 - half), mine)
+        edges[plane, 1] = sums(plane, 8, mine)
         for row in range(9):
-            kept[plane, row] = sums(plane, row, mine)
             sent[plane, row] = sums(plane, row, others).astype(BF16)
 
 
-def join_body(at, kept, got, joined):
+def join_body(at, kept, edges, got, after, joined):
     half = at[1]
     for plane in range(4):
         for row in range(8):
-            joined[plane, 8 * half + row] = kept[plane, row].astype(BF16)
+            joined[plane, 8 * half + row] = kept[plane, row]
             joined[plane, 8 - 8 * half + row] = got[plane, row]
-        beside = 7 * (1 - half)
-        joined[plane, 8 * half + beside] = (
-            kept[plane, beside] + got[plane, 8].astype(F32)
+        joined[plane, 8 * half + 7 * (1 - half)] = (
+            edges[plane, 0] + got[plane, 8].astype(F32)
         ).astype(BF16)
-        beyond = 7 * half
-        joined[plane, 8 - 8 * half + beyond] = (
-            kept[plane, 8] + got[plane, beyond].astype(F32)
+        joined[plane, 8 - 8 * half + 7 * half] = (
+            edges[plane, 1] + got[plane, 7 * half].astype(F32)
         ).astype(BF16)
 
 
@@ -380,7 +382,8 @@
         return lax.ppermute(value, SPACE, [(i + 1, i) for i in range(15)])
 
     mine = lax.dynamic_slice_in_dim(volume, 7 * half, 9, axis=1)
-    got = swap(lax.dynamic_slice_in_dim(volume, 7 * (1 - half), 9, axis=1))
+    theirs = lax.dynamic_slice_in_dim(volume, 7 * (1 - half), 9, axis=1)
+    got = swap(theirs)
     own_lo, own_hi = (
         jnp.where(
             half == 0,
@@ -395,7 +398,7 @@
     kernel_sent, cot_own = call(
         ready_body, 4, [((45, 32, 256), BF16), ((4, 8, 32, 128), BF16)],
         [], 10**6, 1,
-    )(at, kernel, jnp.broadcast_to(bias[:, None], (32, 128)), cotangent, own_lo)
+    )(at, kernel, jnp.broadcast_to(bias[:, None], (32, 128)), cotangent, theirs)
     kernel_other = swap(kernel_sent)
     up_rim, down_rim = call(rims_body, 9, [((4, 9, 64, 128), BF16)] * 2, [], 10**6, 1)(
         at, own_lo, own_hi, left_lo, left_hi, right_lo, right_hi, far_lo, far_hi,
@@ -468,8 +471,9 @@
         chip.reshape(16, 56, 256), ("xh", "z", "xl"), 0, 0, tiled=True
     )
     near, back, far = turn(near, 1), turn(back, -1), turn(far, 2)
-    kept, sent = call(
-        total_body, 5, [((4, 9, 32, 128), F32), ((4, 9, 32, 128), BF16)], [], 10**6
+    kept, edges, sent = call(
+        total_body, 5,
+        [((4, 8, 32, 128), BF16), ((4, 2, 32, 128), F32), ((4, 9, 32, 128), BF16)], [], 10**6,
     )(at, own, near, far, back)
     got = swap(sent)
     (copies,) = call(mean_body, 2, [((8, 56, 256), F32)], [], 10**6)(at, pieces)
@@ -477,7 +481,9 @@
     (weight_grad,) = call(weave_body, 3, [((27, 32, 256), F32)], [], 10**6)(
         at, everyone, swap_core(everyone)
     )
-    (input_grad,) = call(join_body, 3, [((4, 16, 32, 128), BF16)], [], 10**6)(at, kept, got)
+    (input_grad,) = call(join_body, 4, [((4, 16, 32, 128), BF16)], [], 10**6, 1)(
+        at, kept, edges, got, weight_grad
+    )
     return output, input_grad, weight_grad
 
 

time: 134 us -> 132 us (0.985)
  waiting for transfers between devices: 39.2 us -> 33.9 us
  local copies, waits for them, and re-layouts: 2.88 us -> 5.76 us
    ppermute x4, waiting for transfers between devices: 10.9 us -> 7.37 us  [swap(): return lax.ppermute(value, 'xh', [(0, 1), (1, 0)])]
    unnamed x16 -> x18, local copies, waits for them, and re-layouts: 0.73 us -> 3.94 us
    ppermute x4, starting transfers between devices: 10.9 us -> 7.67 us  [swap(): return lax.ppermute(value, 'xh', [(0, 1), (1, 0)])]
    ppermute x2, starting transfers between devices: 7.23 us -> 9.02 us  [up(): return lax.ppermute(value, SPACE, [(i, i + 1) for i in range(15)])]
  transfers between devices with their start and end apart: 20 -> 20, of which waited for: 11 -> 12; matrix products, arithmetic and copies ran while one was open for 2% -> 1% of each run, Pallas kernels for 17% -> 18%
where the time goes in v5:
time: 132 us; the launch traced here: 131 us
  starting transfers between devices  42 us (32%)
  Pallas kernels  36.8 us (28%)
  waiting for transfers between devices  33.9 us (26%)
  blocking collectives  10.9 us (8%)
  local copies, waits for them, and re-layouts  5.76 us (4%)
    ppermute x9, waiting for transfers between devices, turn(): return lax.ppermute(value, 'y', [(i, (i + step) % 4) for i in range(4)])  18.7 us
    ppermute x9, starting transfers between devices, turn(): return lax.ppermute(value, 'y', [(i, (i + step) % 4) for i in range(4)])  11.6 us
    all_to_all x1, blocking collectives, on_device(): lax.all_to_all(copies, ('z', 'xl'), 0, 0, tiled=True).reshape(448, 256)  10.9 us
    ppermute x2, starting transfers between devices, up(): return lax.ppermute(value, SPACE, [(i, i + 1) for i in range(15)])  9.02 us
    ppermute x4, starting transfers between devices, swap(): return lax.ppermute(value, 'xh', [(0, 1), (1, 0)])  7.67 us
    ppermute x4, waiting for transfers between devices, swap(): return lax.ppermute(value, 'xh', [(0, 1), (1, 0)])  7.37 us
    all_to_all x1, starting transfers between devices, on_device(): lax.all_to_all(chip.reshape(16, 56, 256), ('xh', 'z', 'xl'), 0, 0, tiled=...  7.16 us
    pallas_call x1, Pallas kernels, on_device(): call(inner_weight_body, 4, [((2, 448, 256), F32)] * 2 + [((256, 1728), BF...  5.77 us
  transfers between devices with their start and end apart: 20, of which 12 were waited for; matrix products, arithmetic and copies ran while one was open for 1% of the time, Pallas kernels for 18%

profile of v5, /device:TPU:1, one launch (start us, length us, event | category | flops | bytes accessed | tf_op | source)
XLA Modules:
  0.0 131.3 jit_solution(5560673272921340871)
XLA Ops:
  1.7 3.7 %collective-permute-start = (bf16[4,9,32,128]{3,2,1,0:T(8,128)(2,1)S(1)}, bf16[4,9,32,128]{3,2,1,0:T(8,128)(2,1)S(1)}, u32[]{:S(2)}, u32[]{:S(2)}) collective-permute-start(bf16[4,9,32,128]{3,2,1,0:T(8,128)(2,1)S(1)} %constant_dynamic-slice_fusion.1.after), channel_id=1, source_target_pairs={{0,16},{16,0},{1,17},{17,1},{2,18},{18,2},{3,19},{19,3},{4,20},{20... | collective-permute-start | bytes 884744 | tf_op jit(solution)/shard_map/ppermute | solution.py:370
  9.0 2.6 %collective-permute-done = bf16[4,9,32,128]{3,2,1,0:T(8,128)(2,1)S(1)} collective-permute-done((bf16[4,9,32,128]{3,2,1,0:T(8,128)(2,1)S(1)}, bf16[4,9,32,128]{3,2,1,0:T(8,128)(2,1)S(1)}, u32[]{:S(2)}, u32[]{:S(2)}) %collective-permute-start) | collective-permute-done | bytes 294944 | tf_op jit(solution)/shard_map/ppermute | solution.py:370
  11.8 1.7 %collective-permute-start.1 = (bf16[2,9,64,128]{3,2,1,0:T(8,128)(2,1)S(1)}, bf16[2,9,64,128]{3,2,1,0:T(8,128)(2,1)S(1)}, u32[]{:S(2)}, u32[]{:S(2)}) collective-permute-start(bf16[2,9,64,128]{3,2,1,0:T(8,128)(2,1)S(1)} %maximum_select_fusion.1.own_lo), channel_id=1, source_target_pairs={{0,32},{32,64},{64,96},{96,0},{1,33},{33,65},{65,97},{97,1},{2,34}... | collective-permute-start | bytes 884744 | tf_op jit(solution)/shard_map/ppermute | solution.py:376
  13.6 1.5 %collective-permute-start.4 = (bf16[2,9,64,128]{3,2,1,0:T(8,128)(2,1)S(1)}, bf16[2,9,64,128]{3,2,1,0:T(8,128)(2,1)S(1)}, u32[]{:S(2)}, u32[]{:S(2)}) collective-permute-start(bf16[2,9,64,128]{3,2,1,0:T(8,128)(2,1)S(1)} %maximum_select_fusion.2.own_hi), channel_id=1, source_target_pairs={{0,96},{32,0},{64,32},{96,64},{1,97},{33,1},{65,33},{97,65},{2,98}... | collective-permute-start | bytes 884744 | tf_op jit(solution)/shard_map/ppermute | solution.py:376
  15.1 1.5 %collective-permute-start.3 = (bf16[2,9,64,128]{3,2,1,0:T(8,128)(2,1)S(1)}, bf16[2,9,64,128]{3,2,1,0:T(8,128)(2,1)S(1)}, u32[]{:S(2)}, u32[]{:S(2)}) collective-permute-start(bf16[2,9,64,128]{3,2,1,0:T(8,128)(2,1)S(1)} %maximum_select_fusion.1.own_lo), channel_id=1, source_target_pairs={{0,96},{32,0},{64,32},{96,64},{1,97},{33,1},{65,33},{97,65},{2,98}... | collective-permute-start | bytes 884744 | tf_op jit(solution)/shard_map/ppermute | solution.py:376
  16.6 3.7 %collective-permute-done.1.left_lo = bf16[2,9,64,128]{3,2,1,0:T(8,128)(2,1)S(1)} collective-permute-done((bf16[2,9,64,128]{3,2,1,0:T(8,128)(2,1)S(1)}, bf16[2,9,64,128]{3,2,1,0:T(8,128)(2,1)S(1)}, u32[]{:S(2)}, u32[]{:S(2)}) %collective-permute-start.1) | collective-permute-done | bytes 294944 | tf_op jit(solution)/shard_map/ppermute | solution.py:376
  20.3 2.7 %collective-permute-start.6 = (bf16[2,9,64,128]{3,2,1,0:T(8,128)(2,1)S(1)}, bf16[2,9,64,128]{3,2,1,0:T(8,128)(2,1)S(1)}, u32[]{:S(2)}, u32[]{:S(2)}) collective-permute-start(bf16[2,9,64,128]{3,2,1,0:T(8,128)(2,1)S(1)} %collective-permute-done.4.right_hi), channel_id=1, source_target_pairs={{0,96},{32,0},{64,32},{96,64},{1,97},{33,1},{65,33},{97,65},{2,98}... | collective-permute-start | bytes 884744 | tf_op jit(solution)/shard_map/ppermute | solution.py:376
  23.0 3.5 %collective-permute-done.3.right_lo = bf16[2,9,64,128]{3,2,1,0:T(8,128)(2,1)S(1)} collective-permute-done((bf16[2,9,64,128]{3,2,1,0:T(8,128)(2,1)S(1)}, bf16[2,9,64,128]{3,2,1,0:T(8,128)(2,1)S(1)}, u32[]{:S(2)}, u32[]{:S(2)}) %collective-permute-start.3) | collective-permute-done | bytes 294944 | tf_op jit(solution)/shard_map/ppermute | solution.py:376
  27.5 5.8 %collective-permute-done.5.far_lo = bf16[2,9,64,128]{3,2,1,0:T(8,128)(2,1)S(1)} collective-permute-done((bf16[2,9,64,128]{3,2,1,0:T(8,128)(2,1)S(1)}, bf16[2,9,64,128]{3,2,1,0:T(8,128)(2,1)S(1)}, u32[]{:S(2)}, u32[]{:S(2)}) %collective-permute-start.5) | collective-permute-done | bytes 294944 | tf_op jit(solution)/shard_map/ppermute | solution.py:376
  33.8 5.5 %collective-permute-start.8 = (bf16[4,9,64,128]{3,2,1,0:T(8,128)(2,1)S(1)}, bf16[4,9,64,128]{3,2,1,0:T(8,128)(2,1)S(1)}, u32[]{:S(2)}, u32[]{:S(2)}) collective-permute-start(bf16[4,9,64,128]{3,2,1,0:T(8,128)(2,1)S(1)} %get-tuple-element.39), channel_id=1, source_target_pairs={{0,1},{1,2},{2,3},{3,4},{4,5},{5,6},{6,7},{7,8},{8,9},{9,10},{10,1... | collective-permute-start | bytes 1769480 | tf_op jit(solution)/shard_map/ppermute | solution.py:379
  39.4 1.9 %collective-permute-start.9 = (bf16[4,9,64,128]{3,2,1,0:T(8,128)(2,1)S(1)}, bf16[4,9,64,128]{3,2,1,0:T(8,128)(2,1)S(1)}, u32[]{:S(2)}, u32[]{:S(2)}) collective-permute-start(bf16[4,9,64,128]{3,2,1,0:T(8,128)(2,1)S(1)} %get-tuple-element.40), channel_id=1, source_target_pairs={{1,0},{2,1},{3,2},{4,3},{5,4},{6,5},{7,6},{8,7},{9,8},{10,9},{11,1... | collective-permute-start | bytes 1769480 | tf_op jit(solution)/shard_map/ppermute | solution.py:382
  41.3 5.0 %shard_map.68 = (bf16[2,8,32,128]{3,2,1,0:T(8,128)(2,1)S(1)}, bf16[2,8,32,128]{3,2,1,0:T(8,128)(2,1)S(1)}, bf16[2,8,64,128]{3,2,1,0:T(8,128)(2,1)S(1)}, bf16[4,1...) custom-call(s32[3]{0:T(128)S(1)} %pad_add_fusion.at, ...), custom_call_target="tpu_custom_call" | custom-call | flops 1800000000 | bytes 8388608 | tf_op jit(solution)/shard_map/pallas_call | solution.py:410
  46.4 5.8 %shard_map.70 = (f32[2,448,256]{2,1,0:T(8,128)S(1)}, f32[2,448,256]{2,1,0:T(8,128)S(1)}, bf16[256,1728]{1,0:T(8,128)(2,1)S(1)}, bf16[256,576]{1,0:T(8,128)(2,1)S(1)}) custom-call(s32[3]{0:T(128)S(1)} %pad_add_fusion.at, bf16[4,10,256,128]{3,2,1,0:T(8,128)(2,1)S(1)} %get-tuple-element.38.field, bf16[2,8,64,128]{3,2,1,0:T(8,128)(2,1)S(1)} %get-tuple-element.45.grad.in_grad, ...), custom_call_target="tpu_custom_call" | custom-call | flops 1800000000 | bytes 8388608 | tf_op jit(solution)/shard_map/pallas_call | solution.py:420
  52.2 2.4 %collective-permute-done.9.high = bf16[4,9,64,128]{3,2,1,0:T(8,128)(2,1)S(1)} collective-permute-done((bf16[4,9,64,128]{3,2,1,0:T(8,128)(2,1)S(1)}, bf16[4,9,64,128]{3,2,1,0:T(8,128)(2,1)S(1)}, u32[]{:S(2)}, u32[]{:S(2)}) %collective-permute-start.9) | collective-permute-done | bytes 589856 | tf_op jit(solution)/shard_map/ppermute | solution.py:382
  54.6 3.8 %shard_map.71 = (bf16[4,8,32,128]{3,2,1,0:T(8,128)(2,1)S(1)}, bf16[4,8,32,128]{3,2,1,0:T(8,128)(2,1)S(1)}, bf16[4,8,64,128]{3,2,1,0:T(8,128)(2,1)S(1)}, bf16[8,6...) custom-call(s32[3]{0:T(128)S(1)} %pad_add_fusion.at, ...), custom_call_target="tpu_custom_call" | custom-call | flops 1800000000 | bytes 8388608 | tf_op jit(solution)/shard_map/pallas_call | solution.py:425
  59.1 5.5 %shard_map.72 = (f32[2,448,256]{2,1,0:T(8,128)S(1)}, f32[2,448,256]{2,1,0:T(8,128)S(1)}) custom-call(s32[3]{0:T(128)S(1)} %pad_add_fusion.at, bf16[4,10,256,128]{3,2,1,0:T(8,128)(2,1)S(1)} %get-tuple-element.38.field, bf16[2,10,256,128]{3,2,1,0:T(8,128)(2,1)S(1)} %get-tuple-element.54.rim, bf16[4,8,64,128]{3,2,1,0:T(8,128)(2,1)S(1)} %get-tuple-element.49.grad.after, ...), custom_call_target="tpu_custom_call" | custom-call | flops 1800000000 | bytes 8388608 | tf_op jit(solution)/shard_map/pallas_call | solution.py:457
  64.7 3.5 %collective-permute-start.11 = (bf16[8,64,128]{2,1,0:T(8,128)(2,1)S(1)}, bf16[8,64,128]{2,1,0:T(8,128)(2,1)S(1)}, u32[]{:S(2)}, u32[]{:S(2)}) collective-permute-start(bf16[8,64,128]{2,1,0:T(8,128)(2,1)S(1)} %get-tuple-element.50), channel_id=1, source_target_pairs={{0,1},{1,2},{2,3},{3,4},{4,5},{5,6},{6,7},{7,8},{8,9},{9,10},{10,1... | collective-permute-start | bytes 393224 | tf_op jit(solution)/shard_map/ppermute | solution.py:379
  68.2 1.9 %collective-permute-start.12 = (bf16[8,64,128]{2,1,0:T(8,128)(2,1)S(1)}, bf16[8,64,128]{2,1,0:T(8,128)(2,1)S(1)}, u32[]{:S(2)}, u32[]{:S(2)}) collective-permute-start(bf16[8,64,128]{2,1,0:T(8,128)(2,1)S(1)} %get-tuple-element.51), channel_id=1, source_target_pairs={{1,0},{2,1},{3,2},{4,3},{5,4},{6,5},{7,6},{8,7},{9,8},{10,9},{11,1... | collective-permute-start | bytes 393224 | tf_op jit(solution)/shard_map/ppermute | solution.py:382
  70.1 4.1 %shard_map.73 = (f32[2,9,64,128]{3,2,1,0:T(8,128)S(1)}, bf16[2,9,64,128]{3,2,1,0:T(8,128)(2,1)S(1)}, bf16[2,9,64,128]{3,2,1,0:T(8,128)(2,1)S(1)}, bf16[2,9,64,128]{3,2,1,0:T(8,128)(2,1)S(1)}) custom-call(s32[3]{0:T(128)S(1)} %pad_add_fusion.at, bf16[4,8,64,128]{3,2,1,0:T(8,128)(2,1)S(1)} %get-tuple-element.49.grad.after, ...), custom_call_target="tpu_custom_call" | custom-call | flops 1800000000 | bytes 8388608 | tf_op jit(solution)/shard_map/pallas_call | solution.py:461
  74.5 5.1 %shard_map.74 = (f32[4,9,64,128]{3,2,1,0:T(8,128)S(1)}, bf16[4,9,64,128]{3,2,1,0:T(8,128)(2,1)S(1)}, bf16[4,9,64,128]{3,2,1,0:T(8,128)(2,1)}, bf16[4,9,64,128]{3,2,1,0:T(8,128)(2,1)S(1)}) custom-call(s32[3]{0:T(128)S(1)} %pad_add_fusion.at, bf16[4,8,64,128]{3,2,1,0:T(8,128)(2,1)S(1)} %get-tuple-element.49.grad.after, ...), custom_call_target="tpu_custom_call" | custom-call | flops 1800000000 | bytes 8388608 | tf_op jit(solution)/shard_map/pallas_call | solution.py:464
  79.6 1.4 %shard_map.76 = bf16[2,448,256]{2,1,0:T(8,128)(2,1)} custom-call(s32[3]{0:T(128)S(1)} %pad_add_fusion.at, f32[2,448,256]{2,1,0:T(8,128)S(1)} %get-tuple-element.56.after.refs_4_.keep, f32[2,448,256]{2,1,0:T(8,128)S(1)} %collective-permute-done.17.got, bf16[4,9,64,128]{3,2,1,0:T(8,128)(2,1)S(1)} %get-tuple-element.62.first.second.third, ...), custom_call_target="tpu_custom_call" | custom-call | flops 1000000 | bytes 8388608 | tf_op jit(solution)/shard_map/pallas_call | solution.py:467
  81.0 7.2 %all-to-all-start = ((bf16[16,56,256]{2,1,0:T(8,128)(2,1)}), bf16[16,56,256]{2,1,0:T(8,128)(2,1)S(1)}, u32[]{:S(2)}, u32[]{:S(2)}) async-start(bf16[16,56,256]{2,1,0:T(8,128)(2,1)} %bitcast.3), calls=%async_computation | async-start | bytes 917504 | tf_op jit(solution)/shard_map/all_to_all | solution.py:470
  88.1 2.7 %collective-permute-start.14 = (bf16[4,9,64,128]{3,2,1,0:T(8,128)(2,1)}, bf16[4,9,64,128]{3,2,1,0:T(8,128)(2,1)S(1)}, u32[]{:S(2)}, u32[]{:S(2)}) collective-permute-start(bf16[4,9,64,128]{3,2,1,0:T(8,128)(2,1)} %get-tuple-element.63), channel_id=1, source_target_pairs={{0,64},{32,96},{64,0},{96,32},{1,65},{33,97},{65,1},{97,33},{2,66}... | collective-permute-start | bytes 1769480 | tf_op jit(solution)/shard_map/ppermute | solution.py:376
  92.3 5.2 %all-to-all-done.pieces = bf16[16,56,256]{2,1,0:T(8,128)(2,1)S(1)} async-done(((bf16[16,56,256]{2,1,0:T(8,128)(2,1)}), bf16[16,56,256]{2,1,0:T(8,128)(2,1)S(1)}, u32[]{:S(2)}, u32[]{:S(2)}) %all-to-all-start) | async-done | bytes 458784 | tf_op jit(solution)/shard_map/all_to_all | solution.py:470
  98.1 10.9 %all_to_all.10 = f32[8,56,256]{2,1,0:T(8,128)S(1)} all-to-all(f32[8,56,256]{2,1,0:T(8,128)S(1)} %shard_map.77), channel_id=1, replica_groups=mesh['y'=4,'xh'=2,'z'=4,'xl'=2,'core'=2] {'z','xl'}, dimensions={0} | all-to-all | bytes 917504 | tf_op jit(solution)/shard_map/all_to_all | solution.py:480
  108.9 2.6 %collective-permute-start.18 = (f32[448,256]{1,0:T(8,128)S(1)}, f32[448,256]{1,0:T(8,128)S(1)}, u32[]{:S(2)}, u32[]{:S(2)}) collective-permute-start(f32[448,256]{1,0:T(8,128)S(1)} %bitcast.5), channel_id=1, source_target_pairs={{0,1},{1,0},{2,3},{3,2},{4,5},{5,4},{6,7},{7,6},{8,9},{9,8},{10,11... | collective-permute-start | bytes 1376264 | tf_op jit(solution)/shard_map/ppermute | solution.py:373
  112.6 4.5 %collective-permute-done.15.back = bf16[4,9,64,128]{3,2,1,0:T(8,128)(2,1)S(1)} collective-permute-done((bf16[4,9,64,128]{3,2,1,0:T(8,128)(2,1)}, bf16[4,9,64,128]{3,2,1,0:T(8,128)(2,1)S(1)}, u32[]{:S(2)}, u32[]{:S(2)}) %collective-permute-start.15) | collective-permute-done | bytes 589856 | tf_op jit(solution)/shard_map/ppermute | solution.py:376
  117.9 1.4 %shard_map.75 = (bf16[4,8,32,128]{3,2,1,0:T(8,128)(2,1)S(1)}, f32[4,2,32,128]{3,2,1,0:T(8,128)S(1)}, bf16[4,9,32,128]{3,2,1,0:T(8,128)(2,1)S(1)}) custom-call(s32[3]{0:T(128)S(1)} %pad_add_fusion.at, f32[4,9,64,128]{3,2,1,0:T(8,128)S(1)} %get-tuple-element.61.own, bf16[4,9,64,128]{3,2,1,0:T(8,128)(2,1)} %collective-permute-done.13.near, ...), custom_call_target="tpu_custom_call" | custom-call | flops 1000000 | bytes 8388608 | tf_op jit(solution)/shard_map/pallas_call | solution.py:474
  119.3 2.9 %collective-permute-start.16 = (bf16[4,9,32,128]{3,2,1,0:T(8,128)(2,1)S(1)}, bf16[4,9,32,128]{3,2,1,0:T(8,128)(2,1)S(1)}, u32[]{:S(2)}, u32[]{:S(2)}) collective-permute-start(bf16[4,9,32,128]{3,2,1,0:T(8,128)(2,1)S(1)} %get-tuple-element.67), channel_id=1, source_target_pairs={{0,16},{16,0},{1,17},{17,1},{2,18},{18,2},{3,19},{19,3},{4,20},{20... | collective-permute-start | bytes 884744 | tf_op jit(solution)/shard_map/ppermute | solution.py:370
  123.1 1.5 %shard_map.78.after = f32[27,32,256]{2,1,0:T(8,128)} custom-call(s32[3]{0:T(128)S(1)} %pad_add_fusion.at, f32[448,256]{1,0:T(8,128)S(1)} %bitcast.6, f32[448,256]{1,0:T(8,128)S(1)} %collective-permute-done.18.other), custom_call_target="tpu_custom_call" | custom-call | flops 1000000 | bytes 8388608 | tf_op jit(solution)/shard_map/pallas_call | solution.py:481
  124.6 4.2 %collective-permute-done.16.got = bf16[4,9,32,128]{3,2,1,0:T(8,128)(2,1)S(1)} collective-permute-done((bf16[4,9,32,128]{3,2,1,0:T(8,128)(2,1)S(1)}, bf16[4,9,32,128]{3,2,1,0:T(8,128)(2,1)S(1)}, u32[]{:S(2)}, u32[]{:S(2)}) %collective-permute-start.16) | collective-permute-done | bytes 294944 | tf_op jit(solution)/shard_map/ppermute | solution.py:370
  129.9 1.4 %shard_map.79 = bf16[4,16,32,128]{3,2,1,0:T(8,128)(2,1)} custom-call(s32[3]{0:T(128)S(1)} %pad_add_fusion.at, bf16[4,8,32,128]{3,2,1,0:T(8,128)(2,1)S(1)} %get-tuple-element.65.kept, f32[4,2,32,128]{3,2,1,0:T(8,128)S(1)} %get-tuple-element.66.edges, bf16[4,9,32,128]{3,2,1,0:T(8,128)(2,1)S(1)} %collective-permute-done.16.got, f32[27,32,256]{2,1,0:T(8,128)S(1)} %copy-done), custom_call_target="tpu_custom_call" | custom-call | flops 1000000 | bytes 8388608 | tf_op jit(solution)/shard_map/pallas_call | solution.py:484
  (48 shorter events, 13.5 us)
Async XLA Ops:
  0.6 8.3 %copy-start.8 = (bf16[4,16,32,128]{3,2,1,0:T(8,128)(2,1)S(1)}, bf16[4,16,32,128]{3,2,1,0:T(8,128)(2,1)}, u32[]{:S(2)}) copy-start(bf16[4,16,32,128]{3,2,1,0:T(8,128)(2,1)} %param.4) | copy-start | bytes 1572868
  1.7 9.9 %collective-permute-start = (bf16[4,9,32,128]{3,2,1,0:T(8,128)(2,1)S(1)}, bf16[4,9,32,128]{3,2,1,0:T(8,128)(2,1)S(1)}, u32[]{:S(2)}, u32[]{:S(2)}) collective-permute-start(bf16[4,9,32,128]{3,2,1,0:T(8,128)(2,1)S(1)} %constant_dynamic-slice_fusion.1.after), channel_id=1, source_target_pairs={{0,16},{16,0},{1,17},{17,1},{2,18},{18,2},{3,19},{19,3},{4,20},{20... | collective-permute-start | bytes 884744 | tf_op jit(solution)/shard_map/ppermute | solution.py:370
  6.1 1.0 copy-start.1
  7.2 1.0 copy-start.2
  8.8 18.6 %collective-permute-start.7 = (bf16[45,32,256]{2,1,0:T(8,128)(2,1)S(1)}, bf16[45,32,256]{2,1,0:T(8,128)(2,1)S(1)}, u32[]{:S(2)}, u32[]{:S(2)}) collective-permute-start(bf16[45,32,256]{2,1,0:T(8,128)(2,1)S(1)} %get-tuple-element.36.kernel_own), channel_id=1, source_target_pairs={{0,16},{16,0},{1,17},{17,1},{2,18},{18,2},{3,19},{19,3},{4,20},{20... | collective-permute-start | bytes 2211848 | tf_op jit(solution)/shard_map/ppermute | solution.py:370
  11.8 8.6 %collective-permute-start.1 = (bf16[2,9,64,128]{3,2,1,0:T(8,128)(2,1)S(1)}, bf16[2,9,64,128]{3,2,1,0:T(8,128)(2,1)S(1)}, u32[]{:S(2)}, u32[]{:S(2)}) collective-permute-start(bf16[2,9,64,128]{3,2,1,0:T(8,128)(2,1)S(1)} %maximum_select_fusion.1.own_lo), channel_id=1, source_target_pairs={{0,32},{32,64},{64,96},{96,0},{1,33},{33,65},{65,97},{97,1},{2,34}... | collective-permute-start | bytes 884744 | tf_op jit(solution)/shard_map/ppermute | solution.py:376
  13.6 6.7 %collective-permute-start.4 = (bf16[2,9,64,128]{3,2,1,0:T(8,128)(2,1)S(1)}, bf16[2,9,64,128]{3,2,1,0:T(8,128)(2,1)S(1)}, u32[]{:S(2)}, u32[]{:S(2)}) collective-permute-start(bf16[2,9,64,128]{3,2,1,0:T(8,128)(2,1)S(1)} %maximum_select_fusion.2.own_hi), channel_id=1, source_target_pairs={{0,96},{32,0},{64,32},{96,64},{1,97},{33,1},{65,33},{97,65},{2,98}... | collective-permute-start | bytes 884744 | tf_op jit(solution)/shard_map/ppermute | solution.py:376
  15.1 11.4 %collective-permute-start.3 = (bf16[2,9,64,128]{3,2,1,0:T(8,128)(2,1)S(1)}, bf16[2,9,64,128]{3,2,1,0:T(8,128)(2,1)S(1)}, u32[]{:S(2)}, u32[]{:S(2)}) collective-permute-start(bf16[2,9,64,128]{3,2,1,0:T(8,128)(2,1)S(1)} %maximum_select_fusion.1.own_lo), channel_id=1, source_target_pairs={{0,96},{32,0},{64,32},{96,64},{1,97},{33,1},{65,33},{97,65},{2,98}... | collective-permute-start | bytes 884744 | tf_op jit(solution)/shard_map/ppermute | solution.py:376
  16.6 10.3 %collective-permute-start.2 = (bf16[2,9,64,128]{3,2,1,0:T(8,128)(2,1)S(1)}, bf16[2,9,64,128]{3,2,1,0:T(8,128)(2,1)S(1)}, u32[]{:S(2)}, u32[]{:S(2)}) collective-permute-start(bf16[2,9,64,128]{3,2,1,0:T(8,128)(2,1)S(1)} %maximum_select_fusion.2.own_hi), channel_id=1, source_target_pairs={{0,32},{32,64},{64,96},{96,0},{1,33},{33,65},{65,97},{97,1},{2,34}... | collective-permute-start | bytes 884744 | tf_op jit(solution)/shard_map/ppermute | solution.py:376
  20.3 12.9 %collective-permute-start.5 = (bf16[2,9,64,128]{3,2,1,0:T(8,128)(2,1)S(1)}, bf16[2,9,64,128]{3,2,1,0:T(8,128)(2,1)S(1)}, u32[]{:S(2)}, u32[]{:S(2)}) collective-permute-start(bf16[2,9,64,128]{3,2,1,0:T(8,128)(2,1)S(1)} %collective-permute-done.1.left_lo), channel_id=1, source_target_pairs={{0,32},{32,64},{64,96},{96,0},{1,33},{33,65},{65,97},{97,1},{2,34}... | collective-permute-start | bytes 884744 | tf_op jit(solution)/shard_map/ppermute | solution.py:376
  20.3 12.9 %collective-permute-start.6 = (bf16[2,9,64,128]{3,2,1,0:T(8,128)(2,1)S(1)}, bf16[2,9,64,128]{3,2,1,0:T(8,128)(2,1)S(1)}, u32[]{:S(2)}, u32[]{:S(2)}) collective-permute-start(bf16[2,9,64,128]{3,2,1,0:T(8,128)(2,1)S(1)} %collective-permute-done.4.right_hi), channel_id=1, source_target_pairs={{0,96},{32,0},{64,32},{96,64},{1,97},{33,1},{65,33},{97,65},{2,98}... | collective-permute-start | bytes 884744 | tf_op jit(solution)/shard_map/ppermute | solution.py:376
  33.8 18.3 %collective-permute-start.8 = (bf16[4,9,64,128]{3,2,1,0:T(8,128)(2,1)S(1)}, bf16[4,9,64,128]{3,2,1,0:T(8,128)(2,1)S(1)}, u32[]{:S(2)}, u32[]{:S(2)}) collective-permute-start(bf16[4,9,64,128]{3,2,1,0:T(8,128)(2,1)S(1)} %get-tuple-element.39), channel_id=1, source_target_pairs={{0,1},{1,2},{2,3},{3,4},{4,5},{5,6},{6,7},{7,8},{8,9},{9,10},{10,1... | collective-permute-start | bytes 1769480 | tf_op jit(solution)/shard_map/ppermute | solution.py:379
  39.4 15.2 %collective-permute-start.9 = (bf16[4,9,64,128]{3,2,1,0:T(8,128)(2,1)S(1)}, bf16[4,9,64,128]{3,2,1,0:T(8,128)(2,1)S(1)}, u32[]{:S(2)}, u32[]{:S(2)}) collective-permute-start(bf16[4,9,64,128]{3,2,1,0:T(8,128)(2,1)S(1)} %get-tuple-element.40), channel_id=1, source_target_pairs={{1,0},{2,1},{3,2},{4,3},{5,4},{6,5},{7,6},{8,7},{9,8},{10,9},{11,1... | collective-permute-start | bytes 1769480 | tf_op jit(solution)/shard_map/ppermute | solution.py:382
  58.4 0.7 copy-start.6
  59.1 5.5 %copy-start.3 = (bf16[4,8,32,128]{3,2,1,0:T(8,128)(2,1)}, bf16[4,8,32,128]{3,2,1,0:T(8,128)(2,1)S(1)}, u32[]{:S(2)}) copy-start(bf16[4,8,32,128]{3,2,1,0:T(8,128)(2,1)S(1)} %get-tuple-element.47) | copy-start | bytes 786436
  64.6 15.0 %collective-permute-start.17 = (f32[2,448,256]{2,1,0:T(8,128)S(1)}, f32[2,448,256]{2,1,0:T(8,128)S(1)}, u32[]{:S(2)}, u32[]{:S(2)}) collective-permute-start(f32[2,448,256]{2,1,0:T(8,128)S(1)} %get-tuple-element.68), channel_id=1, source_target_pairs={{0,1},{1,0},{2,3},{3,2},{4,5},{5,4},{6,7},{7,6},{8,9},{9,8},{10,11... | collective-permute-start | bytes 2752520 | tf_op jit(solution)/shard_map/ppermute | solution.py:373
  64.7 9.5 %collective-permute-start.11 = (bf16[8,64,128]{2,1,0:T(8,128)(2,1)S(1)}, bf16[8,64,128]{2,1,0:T(8,128)(2,1)S(1)}, u32[]{:S(2)}, u32[]{:S(2)}) collective-permute-start(bf16[8,64,128]{2,1,0:T(8,128)(2,1)S(1)} %get-tuple-element.50), channel_id=1, source_target_pairs={{0,1},{1,2},{2,3},{3,4},{4,5},{5,6},{6,7},{7,8},{8,9},{9,10},{10,1... | collective-permute-start | bytes 393224 | tf_op jit(solution)/shard_map/ppermute | solution.py:379
  68.2 6.3 %collective-permute-start.12 = (bf16[8,64,128]{2,1,0:T(8,128)(2,1)S(1)}, bf16[8,64,128]{2,1,0:T(8,128)(2,1)S(1)}, u32[]{:S(2)}, u32[]{:S(2)}) collective-permute-start(bf16[8,64,128]{2,1,0:T(8,128)(2,1)S(1)} %get-tuple-element.51), channel_id=1, source_target_pairs={{1,0},{2,1},{3,2},{4,3},{5,4},{6,5},{7,6},{8,7},{9,8},{10,9},{11,1... | collective-permute-start | bytes 393224 | tf_op jit(solution)/shard_map/ppermute | solution.py:382
  79.6 1.4 %copy-start.5 = (bf16[4,9,64,128]{3,2,1,0:T(8,128)(2,1)}, bf16[4,9,64,128]{3,2,1,0:T(8,128)(2,1)S(1)}, u32[]{:S(2)}) copy-start(bf16[4,9,64,128]{3,2,1,0:T(8,128)(2,1)S(1)} %get-tuple-element.64) | copy-start | bytes 1769476
  81.0 16.5 %all-to-all-start = ((bf16[16,56,256]{2,1,0:T(8,128)(2,1)}), bf16[16,56,256]{2,1,0:T(8,128)(2,1)S(1)}, u32[]{:S(2)}, u32[]{:S(2)}) async-start(bf16[16,56,256]{2,1,0:T(8,128)(2,1)} %bitcast.3), calls=%async_computation | async-start | bytes 917504 | tf_op jit(solution)/shard_map/all_to_all | solution.py:470
  88.1 24.5 %collective-permute-start.14 = (bf16[4,9,64,128]{3,2,1,0:T(8,128)(2,1)}, bf16[4,9,64,128]{3,2,1,0:T(8,128)(2,1)S(1)}, u32[]{:S(2)}, u32[]{:S(2)}) collective-permute-start(bf16[4,9,64,128]{3,2,1,0:T(8,128)(2,1)} %get-tuple-element.63), channel_id=1, source_target_pairs={{0,64},{32,96},{64,0},{96,32},{1,65},{33,97},{65,1},{97,33},{2,66}... | collective-permute-start | bytes 1769480 | tf_op jit(solution)/shard_map/ppermute | solution.py:376
  90.8 26.3 %collective-permute-start.15 = (bf16[4,9,64,128]{3,2,1,0:T(8,128)(2,1)}, bf16[4,9,64,128]{3,2,1,0:T(8,128)(2,1)S(1)}, u32[]{:S(2)}, u32[]{:S(2)}) collective-permute-start(bf16[4,9,64,128]{3,2,1,0:T(8,128)(2,1)} %copy-done.5), channel_id=1, source_target_pairs={{0,96},{32,0},{64,32},{96,64},{1,97},{33,1},{65,33},{97,65},{2,98}... | collective-permute-start | bytes 1769480 | tf_op jit(solution)/shard_map/ppermute | solution.py:376
  91.9 26.0 %collective-permute-start.13 = (bf16[4,9,64,128]{3,2,1,0:T(8,128)(2,1)S(1)}, bf16[4,9,64,128]{3,2,1,0:T(8,128)(2,1)}, u32[]{:S(2)}, u32[]{:S(2)}) collective-permute-start(bf16[4,9,64,128]{3,2,1,0:T(8,128)(2,1)S(1)} %get-tuple-element.62.first.second.third), channel_id=1, source_target_pairs={{0,32},{32,64},{64,96},{96,0},{1,33},{33,65},{65,97},{97,1},{2,34}... | collective-permute-start | bytes 1769480 | tf_op jit(solution)/shard_map/ppermute | solution.py:376
  97.4 14.1 %copy-start.7 = (bf16[4,8,32,128]{3,2,1,0:T(8,128)(2,1)S(1)}, bf16[4,8,32,128]{3,2,1,0:T(8,128)(2,1)}, u32[]{:S(2)}) copy-start(bf16[4,8,32,128]{3,2,1,0:T(8,128)(2,1)} %copy-done.6) | copy-start | bytes 786436
  108.9 14.1 %collective-permute-start.18 = (f32[448,256]{1,0:T(8,128)S(1)}, f32[448,256]{1,0:T(8,128)S(1)}, u32[]{:S(2)}, u32[]{:S(2)}) collective-permute-start(f32[448,256]{1,0:T(8,128)S(1)} %bitcast.5), channel_id=1, source_target_pairs={{0,1},{1,0},{2,3},{3,2},{4,5},{5,4},{6,7},{7,6},{8,9},{9,8},{10,11... | collective-permute-start | bytes 1376264 | tf_op jit(solution)/shard_map/ppermute | solution.py:373
  111.6 10.6 %collective-permute-start.10 = (bf16[4,8,32,128]{3,2,1,0:T(8,128)(2,1)S(1)}, bf16[4,8,32,128]{3,2,1,0:T(8,128)(2,1)S(1)}, u32[]{:S(2)}, u32[]{:S(2)}) collective-permute-start(bf16[4,8,32,128]{3,2,1,0:T(8,128)(2,1)S(1)} %copy-done.7), channel_id=1, source_target_pairs={{0,16},{16,0},{1,17},{17,1},{2,18},{18,2},{3,19},{19,3},{4,20},{20... | collective-permute-start | bytes 786440 | tf_op jit(solution)/shard_map/ppermute | solution.py:370
  117.9 4.3 %copy-start.4 = (bf16[4,8,32,128]{3,2,1,0:T(8,128)(2,1)S(1)}, bf16[4,8,32,128]{3,2,1,0:T(8,128)(2,1)}, u32[]{:S(2)}) copy-start(bf16[4,8,32,128]{3,2,1,0:T(8,128)(2,1)} %copy-done.3) | copy-start | bytes 786436
  119.3 9.4 %collective-permute-start.16 = (bf16[4,9,32,128]{3,2,1,0:T(8,128)(2,1)S(1)}, bf16[4,9,32,128]{3,2,1,0:T(8,128)(2,1)S(1)}, u32[]{:S(2)}, u32[]{:S(2)}) collective-permute-start(bf16[4,9,32,128]{3,2,1,0:T(8,128)(2,1)S(1)} %get-tuple-element.67), channel_id=1, source_target_pairs={{0,16},{16,0},{1,17},{17,1},{2,18},{18,2},{3,19},{19,3},{4,20},{20... | collective-permute-start | bytes 884744 | tf_op jit(solution)/shard_map/ppermute | solution.py:370
  128.8 1.2 copy-start

commit v6 on v5

--- a/solution.py
+++ b/solution.py
@@ -228,7 +228,7 @@
     )
 
 
-def input_terms(at, lines, planes, turned, turned_edge, outs, stacked, held):
+def input_terms(at, lines, planes, place, turned, turned_edge, outs, stacked, held):
     half, starts = at[1], starts_of(at[0])
     rows, width = 8, stacked.shape[2] // 3
     for plane, line_of in enumerate(lines):
@@ -249,7 +249,7 @@
         for first, plane in planes:
             terms = jnp.concatenate(
                 [
-                    pair_of(stacked, first + 2 - a, row + 2 - b)
+                    pair_of(*place(first + 2 - a), row + 2 - b)
                     for a in range(3)
                     for b in range(3)
                 ],
@@ -261,9 +261,14 @@
 
     lax.fori_loop(0, rows // 2, step, 0)
     nearest = 8 - 7 * half
+
+    def line_at(plane):
+        ref, plane = place(plane)
+        return ref[plane, nearest]
+
     terms = jnp.concatenate(
         [
-            jnp.concatenate([stacked[first + 2 - a, nearest] for first, _ in planes], axis=1)
+            jnp.concatenate([line_at(first + 2 - a) for first, _ in planes], axis=1)
             for a in range(3)
         ],
         axis=0,
@@ -275,18 +280,22 @@
 def inner_input_body(at, grad, turned, turned_edge, after, own, near, far, back, stacked, held):
     lines = [lambda row, k=k: grad[k, row] for k in range(4)]
     input_terms(
-        at, lines, [(0, 0), (1, 1)], turned, turned_edge, (own, near, far, back), stacked, held
-    )
-
-
-def outer_input_body(at, grad, low, high, turned, turned_edge, *refs):
+        at, lines, [(0, 0), (1, 1)], lambda plane: (stacked, plane), turned, turned_edge,
+        (own, near, far, back), stacked, held,
+    )
+
+
+def outer_input_body(at, inner, low, high, turned, turned_edge, *refs):
     given, outs, (stacked, held) = refs[:4], refs[5:9], refs[9:]
     for source, ref in zip(given, outs):
         for plane in range(2):
             ref[plane + 1] = source[plane]
-    lines = [lambda row, k=k: grad[k, row] for k in range(4)]
-    lines = [lambda row: low[row]] + lines + [lambda row: high[row]]
-    input_terms(at, lines, [(0, 0), (3, 3)], turned, turned_edge, outs, stacked, held)
+    lines = [lambda row: low[row], lambda row: high[row]]
+
+    def place(plane):
+        return (inner, plane - 1) if 0 < plane < 5 else (stacked, plane // 5)
+
+    input_terms(at, lines, [(0, 0), (3, 3)], place, turned, turned_edge, outs, stacked, held)
 
 
 def total_body(at, own, near, far, back, kept, edges, sent):
@@ -452,18 +461,19 @@
         return [((planes, 9, 64, 128), F32)] + [((planes, 9, 64, 128), BF16)] * 3
 
     def input_scratch(planes):
-        return [pltpu.VMEM((planes, 10, 192, 128), BF16), pltpu.VMEM((256, 256), F32)]
+        lines = [pltpu.VMEM((planes, 10, 192, 128), BF16)] if planes else []
+        return lines + [pltpu.VMEM((256, 256), F32)]
 
     keep, give = call(
         outer_weight_body, 6, [((2, 448, 256), F32)] * 2,
         [pltpu.VMEM((2, 8, 192, 128), BF16)], flops // 2, 1,
     )(at, field, rim, grad, keep, give, grad)
-    parts = call(
-        inner_input_body, 4, input_shapes(2), input_scratch(4), flops // 2, 1
+    *parts, lines = call(
+        inner_input_body, 4, input_shapes(2) + [((4, 10, 192, 128), BF16)], input_scratch(0), flops // 2, 1
     )(at, grad, turned, turned_edge, keep)
     own, near, far, back = call(
-        outer_input_body, 10, input_shapes(4), input_scratch(6), flops // 2, 1
-    )(at, grad, grad_low, grad_high, turned, turned_edge, *parts, keep)
+        outer_input_body, 10, input_shapes(4), input_scratch(2), flops // 2, 1
+    )(at, lines, grad_low, grad_high, turned, turned_edge, *parts, keep)
     (chip,) = call(add_body, 3, [((2, 448, 256), BF16)], [], 10**6, 3)(
         at, keep, swap_core(give), near, near, near
     )

time: 132 us -> 132 us (level)
    unnamed x18 -> x16, local copies, waits for them, and re-layouts: 3.94 us -> 3.94 us
where the time goes in v6:
time: 132 us; the launch traced here: 131 us
  starting transfers between devices  42 us (32%)
  Pallas kernels  36.4 us (28%)
  waiting for transfers between devices  33.7 us (26%)
  blocking collectives  11 us (8%)
  local copies, waits for them, and re-layouts  5.75 us (4%)
    ppermute x9, waiting for transfers between devices, turn(): return lax.ppermute(value, 'y', [(i, (i + step) % 4) for i in range(4)])  18.5 us
    ppermute x9, starting transfers between devices, turn(): return lax.ppermute(value, 'y', [(i, (i + step) % 4) for i in range(4)])  11.6 us
    all_to_all x1, blocking collectives, on_device(): lax.all_to_all(copies, ('z', 'xl'), 0, 0, tiled=True).reshape(448, 256)  11 us
    ppermute x2, starting transfers between devices, up(): return lax.ppermute(value, SPACE, [(i, i + 1) for i in range(15)])  9.02 us
    ppermute x4, starting transfers between devices, swap(): return lax.ppermute(value, 'xh', [(0, 1), (1, 0)])  7.68 us
    ppermute x4, waiting for transfers between devices, swap(): return lax.ppermute(value, 'xh', [(0, 1), (1, 0)])  7.37 us
    all_to_all x1, starting transfers between devices, on_device(): lax.all_to_all(chip.reshape(16, 56, 256), ('xh', 'z', 'xl'), 0, 0, tiled=...  7.16 us
    pallas_call x1, Pallas kernels, on_device(): call(inner_weight_body, 4, [((2, 448, 256), F32)] * 2 + [((256, 1728), BF...  5.77 us
  transfers between devices with their start and end apart: 20, of which 12 were waited for; matrix products, arithmetic and copies ran while one was open for 1% of the time, Pallas kernels for 18%

profile of v6, /device:TPU:1, one launch (start us, length us, event | category | flops | bytes accessed | tf_op | source)
XLA Modules:
  0.0 130.9 jit_solution(1747694684143639953)
XLA Ops:
  1.7 3.7 %collective-permute-start = (bf16[4,9,32,128]{3,2,1,0:T(8,128)(2,1)S(1)}, bf16[4,9,32,128]{3,2,1,0:T(8,128)(2,1)S(1)}, u32[]{:S(2)}, u32[]{:S(2)}) collective-permute-start(bf16[4,9,32,128]{3,2,1,0:T(8,128)(2,1)S(1)} %constant_dynamic-slice_fusion.1.after), channel_id=1, source_target_pairs={{0,16},{16,0},{1,17},{17,1},{2,18},{18,2},{3,19},{19,3},{4,20},{20... | collective-permute-start | bytes 884744 | tf_op jit(solution)/shard_map/ppermute | solution.py:379
  9.0 2.6 %collective-permute-done = bf16[4,9,32,128]{3,2,1,0:T(8,128)(2,1)S(1)} collective-permute-done((bf16[4,9,32,128]{3,2,1,0:T(8,128)(2,1)S(1)}, bf16[4,9,32,128]{3,2,1,0:T(8,128)(2,1)S(1)}, u32[]{:S(2)}, u32[]{:S(2)}) %collective-permute-start) | collective-permute-done | bytes 294944 | tf_op jit(solution)/shard_map/ppermute | solution.py:379
  11.8 1.7 %collective-permute-start.1 = (bf16[2,9,64,128]{3,2,1,0:T(8,128)(2,1)S(1)}, bf16[2,9,64,128]{3,2,1,0:T(8,128)(2,1)S(1)}, u32[]{:S(2)}, u32[]{:S(2)}) collective-permute-start(bf16[2,9,64,128]{3,2,1,0:T(8,128)(2,1)S(1)} %maximum_select_fusion.1.own_lo), channel_id=1, source_target_pairs={{0,32},{32,64},{64,96},{96,0},{1,33},{33,65},{65,97},{97,1},{2,34}... | collective-permute-start | bytes 884744 | tf_op jit(solution)/shard_map/ppermute | solution.py:385
  13.6 1.5 %collective-permute-start.4 = (bf16[2,9,64,128]{3,2,1,0:T(8,128)(2,1)S(1)}, bf16[2,9,64,128]{3,2,1,0:T(8,128)(2,1)S(1)}, u32[]{:S(2)}, u32[]{:S(2)}) collective-permute-start(bf16[2,9,64,128]{3,2,1,0:T(8,128)(2,1)S(1)} %maximum_select_fusion.2.own_hi), channel_id=1, source_target_pairs={{0,96},{32,0},{64,32},{96,64},{1,97},{33,1},{65,33},{97,65},{2,98}... | collective-permute-start | bytes 884744 | tf_op jit(solution)/shard_map/ppermute | solution.py:385
  15.1 1.5 %collective-permute-start.3 = (bf16[2,9,64,128]{3,2,1,0:T(8,128)(2,1)S(1)}, bf16[2,9,64,128]{3,2,1,0:T(8,128)(2,1)S(1)}, u32[]{:S(2)}, u32[]{:S(2)}) collective-permute-start(bf16[2,9,64,128]{3,2,1,0:T(8,128)(2,1)S(1)} %maximum_select_fusion.1.own_lo), channel_id=1, source_target_pairs={{0,96},{32,0},{64,32},{96,64},{1,97},{33,1},{65,33},{97,65},{2,98}... | collective-permute-start | bytes 884744 | tf_op jit(solution)/shard_map/ppermute | solution.py:385
  16.6 3.7 %collective-permute-done.1.left_lo = bf16[2,9,64,128]{3,2,1,0:T(8,128)(2,1)S(1)} collective-permute-done((bf16[2,9,64,128]{3,2,1,0:T(8,128)(2,1)S(1)}, bf16[2,9,64,128]{3,2,1,0:T(8,128)(2,1)S(1)}, u32[]{:S(2)}, u32[]{:S(2)}) %collective-permute-start.1) | collective-permute-done | bytes 294944 | tf_op jit(solution)/shard_map/ppermute | solution.py:385
  20.3 2.7 %collective-permute-start.6 = (bf16[2,9,64,128]{3,2,1,0:T(8,128)(2,1)S(1)}, bf16[2,9,64,128]{3,2,1,0:T(8,128)(2,1)S(1)}, u32[]{:S(2)}, u32[]{:S(2)}) collective-permute-start(bf16[2,9,64,128]{3,2,1,0:T(8,128)(2,1)S(1)} %collective-permute-done.4.right_hi), channel_id=1, source_target_pairs={{0,96},{32,0},{64,32},{96,64},{1,97},{33,1},{65,33},{97,65},{2,98}... | collective-permute-start | bytes 884744 | tf_op jit(solution)/shard_map/ppermute | solution.py:385
  23.0 3.5 %collective-permute-done.3.right_lo = bf16[2,9,64,128]{3,2,1,0:T(8,128)(2,1)S(1)} collective-permute-done((bf16[2,9,64,128]{3,2,1,0:T(8,128)(2,1)S(1)}, bf16[2,9,64,128]{3,2,1,0:T(8,128)(2,1)S(1)}, u32[]{:S(2)}, u32[]{:S(2)}) %collective-permute-start.3) | collective-permute-done | bytes 294944 | tf_op jit(solution)/shard_map/ppermute | solution.py:385
  27.5 5.8 %collective-permute-done.5.far_lo = bf16[2,9,64,128]{3,2,1,0:T(8,128)(2,1)S(1)} collective-permute-done((bf16[2,9,64,128]{3,2,1,0:T(8,128)(2,1)S(1)}, bf16[2,9,64,128]{3,2,1,0:T(8,128)(2,1)S(1)}, u32[]{:S(2)}, u32[]{:S(2)}) %collective-permute-start.5) | collective-permute-done | bytes 294944 | tf_op jit(solution)/shard_map/ppermute | solution.py:385
  33.8 5.5 %collective-permute-start.8 = (bf16[4,9,64,128]{3,2,1,0:T(8,128)(2,1)S(1)}, bf16[4,9,64,128]{3,2,1,0:T(8,128)(2,1)S(1)}, u32[]{:S(2)}, u32[]{:S(2)}) collective-permute-start(bf16[4,9,64,128]{3,2,1,0:T(8,128)(2,1)S(1)} %get-tuple-element.40), channel_id=1, source_target_pairs={{0,1},{1,2},{2,3},{3,4},{4,5},{5,6},{6,7},{7,8},{8,9},{9,10},{10,1... | collective-permute-start | bytes 1769480 | tf_op jit(solution)/shard_map/ppermute | solution.py:388
  39.4 1.9 %collective-permute-start.9 = (bf16[4,9,64,128]{3,2,1,0:T(8,128)(2,1)S(1)}, bf16[4,9,64,128]{3,2,1,0:T(8,128)(2,1)S(1)}, u32[]{:S(2)}, u32[]{:S(2)}) collective-permute-start(bf16[4,9,64,128]{3,2,1,0:T(8,128)(2,1)S(1)} %get-tuple-element.41), channel_id=1, source_target_pairs={{1,0},{2,1},{3,2},{4,3},{5,4},{6,5},{7,6},{8,7},{9,8},{10,9},{11,1... | collective-permute-start | bytes 1769480 | tf_op jit(solution)/shard_map/ppermute | solution.py:391
  41.3 5.0 %shard_map.68 = (bf16[2,8,32,128]{3,2,1,0:T(8,128)(2,1)S(1)}, bf16[2,8,32,128]{3,2,1,0:T(8,128)(2,1)S(1)}, bf16[2,8,64,128]{3,2,1,0:T(8,128)(2,1)S(1)}, bf16[4,1...) custom-call(s32[3]{0:T(128)S(1)} %pad_add_fusion.at, ...), custom_call_target="tpu_custom_call" | custom-call | flops 1800000000 | bytes 8388608 | tf_op jit(solution)/shard_map/pallas_call | solution.py:419
  46.4 5.8 %shard_map.70 = (f32[2,448,256]{2,1,0:T(8,128)S(1)}, f32[2,448,256]{2,1,0:T(8,128)S(1)}, bf16[256,1728]{1,0:T(8,128)(2,1)S(1)}, bf16[256,576]{1,0:T(8,128)(2,1)S(1)}) custom-call(s32[3]{0:T(128)S(1)} %pad_add_fusion.at, bf16[4,10,256,128]{3,2,1,0:T(8,128)(2,1)S(1)} %get-tuple-element.39.field, bf16[2,8,64,128]{3,2,1,0:T(8,128)(2,1)S(1)} %get-tuple-element.46.grad.in_grad, ...), custom_call_target="tpu_custom_call" | custom-call | flops 1800000000 | bytes 8388608 | tf_op jit(solution)/shard_map/pallas_call | solution.py:429
  52.2 2.4 %collective-permute-done.9.high = bf16[4,9,64,128]{3,2,1,0:T(8,128)(2,1)S(1)} collective-permute-done((bf16[4,9,64,128]{3,2,1,0:T(8,128)(2,1)S(1)}, bf16[4,9,64,128]{3,2,1,0:T(8,128)(2,1)S(1)}, u32[]{:S(2)}, u32[]{:S(2)}) %collective-permute-start.9) | collective-permute-done | bytes 589856 | tf_op jit(solution)/shard_map/ppermute | solution.py:391
  54.6 3.8 %shard_map.71 = (bf16[4,8,32,128]{3,2,1,0:T(8,128)(2,1)S(1)}, bf16[4,8,32,128]{3,2,1,0:T(8,128)(2,1)S(1)}, bf16[4,8,64,128]{3,2,1,0:T(8,128)(2,1)S(1)}, bf16[8,6...) custom-call(s32[3]{0:T(128)S(1)} %pad_add_fusion.at, ...), custom_call_target="tpu_custom_call" | custom-call | flops 1800000000 | bytes 8388608 | tf_op jit(solution)/shard_map/pallas_call | solution.py:434
  59.1 5.5 %shard_map.72 = (f32[2,448,256]{2,1,0:T(8,128)S(1)}, f32[2,448,256]{2,1,0:T(8,128)S(1)}) custom-call(s32[3]{0:T(128)S(1)} %pad_add_fusion.at, bf16[4,10,256,128]{3,2,1,0:T(8,128)(2,1)S(1)} %get-tuple-element.39.field, bf16[2,10,256,128]{3,2,1,0:T(8,128)(2,1)S(1)} %get-tuple-element.53.rim, bf16[4,8,64,128]{3,2,1,0:T(8,128)(2,1)S(1)} %get-tuple-element.50.grad.after, ...), custom_call_target="tpu_custom_call" | custom-call | flops 1800000000 | bytes 8388608 | tf_op jit(solution)/shard_map/pallas_call | solution.py:467
  64.7 3.5 %collective-permute-start.11 = (bf16[8,64,128]{2,1,0:T(8,128)(2,1)S(1)}, bf16[8,64,128]{2,1,0:T(8,128)(2,1)S(1)}, u32[]{:S(2)}, u32[]{:S(2)}) collective-permute-start(bf16[8,64,128]{2,1,0:T(8,128)(2,1)S(1)} %get-tuple-element.57), channel_id=1, source_target_pairs={{0,1},{1,2},{2,3},{3,4},{4,5},{5,6},{6,7},{7,8},{8,9},{9,10},{10,1... | collective-permute-start | bytes 393224 | tf_op jit(solution)/shard_map/ppermute | solution.py:388
  68.2 1.9 %collective-permute-start.12 = (bf16[8,64,128]{2,1,0:T(8,128)(2,1)S(1)}, bf16[8,64,128]{2,1,0:T(8,128)(2,1)S(1)}, u32[]{:S(2)}, u32[]{:S(2)}) collective-permute-start(bf16[8,64,128]{2,1,0:T(8,128)(2,1)S(1)} %get-tuple-element.58), channel_id=1, source_target_pairs={{1,0},{2,1},{3,2},{4,3},{5,4},{6,5},{7,6},{8,7},{9,8},{10,9},{11,1... | collective-permute-start | bytes 393224 | tf_op jit(solution)/shard_map/ppermute | solution.py:391
  70.1 4.1 %shard_map.73 = (f32[2,9,64,128]{3,2,1,0:T(8,128)S(1)}, bf16[2,9,64,128]{3,2,1,0:T(8,128)(2,1)S(1)}, bf16[2,9,64,128]{3,2,1,0:T(8,128)(2,1)S(1)}, bf16[2,9,64,12...) custom-call(s32[3]{0:T(128)S(1)} %pad_add_fusion.at, bf16[4,8,64,128]{3,2,1,0:T(8,128)(2,1)S(1)} %get-tuple-element.50.grad.after, ...), custom_call_target="tpu_custom_call" | custom-call | flops 1800000000 | bytes 8388608 | tf_op jit(solution)/shard_map/pallas_call | solution.py:471
  74.5 4.7 %shard_map.74 = (f32[4,9,64,128]{3,2,1,0:T(8,128)S(1)}, bf16[4,9,64,128]{3,2,1,0:T(8,128)(2,1)S(1)}, bf16[4,9,64,128]{3,2,1,0:T(8,128)(2,1)}, bf16[4,9,64,128]{3,2,1,0:T(8,128)(2,1)S(1)}) custom-call(s32[3]{0:T(128)S(1)} %pad_add_fusion.at, bf16[4,10,192,128]{3,2,1,0:T(8,128)(2,1)S(1)} %get-tuple-element.56.inner, ...), custom_call_target="tpu_custom_call" | custom-call | flops 1800000000 | bytes 8388608 | tf_op jit(solution)/shard_map/pallas_call | solution.py:474
  79.2 1.4 %shard_map.76 = bf16[2,448,256]{2,1,0:T(8,128)(2,1)} custom-call(s32[3]{0:T(128)S(1)} %pad_add_fusion.at, f32[2,448,256]{2,1,0:T(8,128)S(1)} %get-tuple-element.55.after.refs_4_.keep, f32[2,448,256]{2,1,0:T(8,128)S(1)} %collective-permute-done.17.got, bf16[4,9,64,128]{3,2,1,0:T(8,128)(2,1)S(1)} %get-tuple-element.64.first.second.third, ...), custom_call_target="tpu_custom_call" | custom-call | flops 1000000 | bytes 8388608 | tf_op jit(solution)/shard_map/pallas_call | solution.py:477
  80.6 7.2 %all-to-all-start = ((bf16[16,56,256]{2,1,0:T(8,128)(2,1)}), bf16[16,56,256]{2,1,0:T(8,128)(2,1)S(1)}, u32[]{:S(2)}, u32[]{:S(2)}) async-start(bf16[16,56,256]{2,1,0:T(8,128)(2,1)} %bitcast.3), calls=%async_computation | async-start | bytes 917504 | tf_op jit(solution)/shard_map/all_to_all | solution.py:480
  87.8 2.7 %collective-permute-start.14 = (bf16[4,9,64,128]{3,2,1,0:T(8,128)(2,1)}, bf16[4,9,64,128]{3,2,1,0:T(8,128)(2,1)S(1)}, u32[]{:S(2)}, u32[]{:S(2)}) collective-permute-start(bf16[4,9,64,128]{3,2,1,0:T(8,128)(2,1)} %get-tuple-element.65), channel_id=1, source_target_pairs={{0,64},{32,96},{64,0},{96,32},{1,65},{33,97},{65,1},{97,33},{2,66}... | collective-permute-start | bytes 1769480 | tf_op jit(solution)/shard_map/ppermute | solution.py:385
  92.0 5.1 %all-to-all-done.pieces = bf16[16,56,256]{2,1,0:T(8,128)(2,1)S(1)} async-done(((bf16[16,56,256]{2,1,0:T(8,128)(2,1)}), bf16[16,56,256]{2,1,0:T(8,128)(2,1)S(1)}, u32[]{:S(2)}, u32[]{:S(2)}) %all-to-all-start) | async-done | bytes 458784 | tf_op jit(solution)/shard_map/all_to_all | solution.py:480
  97.7 11.0 %all_to_all.10 = f32[8,56,256]{2,1,0:T(8,128)S(1)} all-to-all(f32[8,56,256]{2,1,0:T(8,128)S(1)} %shard_map.77), channel_id=1, replica_groups=mesh['y'=4,'xh'=2,'z'=4,'xl'=2,'core'=2] {'z','xl'}, dimensions={0} | all-to-all | bytes 917504 | tf_op jit(solution)/shard_map/all_to_all | solution.py:490
  108.7 2.6 %collective-permute-start.18 = (f32[448,256]{1,0:T(8,128)S(1)}, f32[448,256]{1,0:T(8,128)S(1)}, u32[]{:S(2)}, u32[]{:S(2)}) collective-permute-start(f32[448,256]{1,0:T(8,128)S(1)} %bitcast.5), channel_id=1, source_target_pairs={{0,1},{1,0},{2,3},{3,2},{4,5},{5,4},{6,7},{7,6},{8,9},{9,8},{10,11... | collective-permute-start | bytes 1376264 | tf_op jit(solution)/shard_map/ppermute | solution.py:382
  112.4 4.4 %collective-permute-done.15.back = bf16[4,9,64,128]{3,2,1,0:T(8,128)(2,1)S(1)} collective-permute-done((bf16[4,9,64,128]{3,2,1,0:T(8,128)(2,1)}, bf16[4,9,64,128]{3,2,1,0:T(8,128)(2,1)S(1)}, u32[]{:S(2)}, u32[]{:S(2)}) %collective-permute-start.15) | collective-permute-done | bytes 589856 | tf_op jit(solution)/shard_map/ppermute | solution.py:385
  117.6 1.4 %shard_map.75 = (bf16[4,8,32,128]{3,2,1,0:T(8,128)(2,1)S(1)}, f32[4,2,32,128]{3,2,1,0:T(8,128)S(1)}, bf16[4,9,32,128]{3,2,1,0:T(8,128)(2,1)S(1)}) custom-call(s32[3]{0:T(128)S(1)} %pad_add_fusion.at, f32[4,9,64,128]{3,2,1,0:T(8,128)S(1)} %get-tuple-element.63.own, bf16[4,9,64,128]{3,2,1,0:T(8,128)(2,1)} %collective-permute-done.13.near, ...), custom_call_target="tpu_custom_call" | custom-call | flops 1000000 | bytes 8388608 | tf_op jit(solution)/shard_map/pallas_call | solution.py:484
  119.0 2.9 %collective-permute-start.16 = (bf16[4,9,32,128]{3,2,1,0:T(8,128)(2,1)S(1)}, bf16[4,9,32,128]{3,2,1,0:T(8,128)(2,1)S(1)}, u32[]{:S(2)}, u32[]{:S(2)}) collective-permute-start(bf16[4,9,32,128]{3,2,1,0:T(8,128)(2,1)S(1)} %get-tuple-element.69), channel_id=1, source_target_pairs={{0,16},{16,0},{1,17},{17,1},{2,18},{18,2},{3,19},{19,3},{4,20},{20... | collective-permute-start | bytes 884744 | tf_op jit(solution)/shard_map/ppermute | solution.py:379
  122.7 1.5 %shard_map.78.after = f32[27,32,256]{2,1,0:T(8,128)} custom-call(s32[3]{0:T(128)S(1)} %pad_add_fusion.at, f32[448,256]{1,0:T(8,128)S(1)} %bitcast.6, f32[448,256]{1,0:T(8,128)S(1)} %collective-permute-done.18.other), custom_call_target="tpu_custom_call" | custom-call | flops 1000000 | bytes 8388608 | tf_op jit(solution)/shard_map/pallas_call | solution.py:491
  124.2 4.2 %collective-permute-done.16.got = bf16[4,9,32,128]{3,2,1,0:T(8,128)(2,1)S(1)} collective-permute-done((bf16[4,9,32,128]{3,2,1,0:T(8,128)(2,1)S(1)}, bf16[4,9,32,128]{3,2,1,0:T(8,128)(2,1)S(1)}, u32[]{:S(2)}, u32[]{:S(2)}) %collective-permute-start.16) | collective-permute-done | bytes 294944 | tf_op jit(solution)/shard_map/ppermute | solution.py:379
  129.6 1.4 %shard_map.79 = bf16[4,16,32,128]{3,2,1,0:T(8,128)(2,1)} custom-call(s32[3]{0:T(128)S(1)} %pad_add_fusion.at, bf16[4,8,32,128]{3,2,1,0:T(8,128)(2,1)S(1)} %get-tuple-element.67.kept, f32[4,2,32,128]{3,2,1,0:T(8,128)S(1)} %get-tuple-element.68.edges, bf16[4,9,32,128]{3,2,1,0:T(8,128)(2,1)S(1)} %collective-permute-done.16.got, f32[27,32,256]{2,1,0:T(8,128)S(1)} %copy-done), custom_call_target="tpu_custom_call" | custom-call | flops 1000000 | bytes 8388608 | tf_op jit(solution)/shard_map/pallas_call | solution.py:494
  (46 shorter events, 13.5 us)
Async XLA Ops:
  0.6 8.3 %copy-start.7 = (bf16[4,16,32,128]{3,2,1,0:T(8,128)(2,1)S(1)}, bf16[4,16,32,128]{3,2,1,0:T(8,128)(2,1)}, u32[]{:S(2)}) copy-start(bf16[4,16,32,128]{3,2,1,0:T(8,128)(2,1)} %param.4) | copy-start | bytes 1572868
  1.7 9.9 %collective-permute-start = (bf16[4,9,32,128]{3,2,1,0:T(8,128)(2,1)S(1)}, bf16[4,9,32,128]{3,2,1,0:T(8,128)(2,1)S(1)}, u32[]{:S(2)}, u32[]{:S(2)}) collective-permute-start(bf16[4,9,32,128]{3,2,1,0:T(8,128)(2,1)S(1)} %constant_dynamic-slice_fusion.1.after), channel_id=1, source_target_pairs={{0,16},{16,0},{1,17},{17,1},{2,18},{18,2},{3,19},{19,3},{4,20},{20... | collective-permute-start | bytes 884744 | tf_op jit(solution)/shard_map/ppermute | solution.py:379
  6.1 1.0 copy-start.1
  7.2 1.0 copy-start.2
  8.8 18.6 %collective-permute-start.7 = (bf16[45,32,256]{2,1,0:T(8,128)(2,1)S(1)}, bf16[45,32,256]{2,1,0:T(8,128)(2,1)S(1)}, u32[]{:S(2)}, u32[]{:S(2)}) collective-permute-start(bf16[45,32,256]{2,1,0:T(8,128)(2,1)S(1)} %get-tuple-element.37.kernel_own), channel_id=1, source_target_pairs={{0,16},{16,0},{1,17},{17,1},{2,18},{18,2},{3,19},{19,3},{4,20},{20... | collective-permute-start | bytes 2211848 | tf_op jit(solution)/shard_map/ppermute | solution.py:379
  11.8 8.6 %collective-permute-start.1 = (bf16[2,9,64,128]{3,2,1,0:T(8,128)(2,1)S(1)}, bf16[2,9,64,128]{3,2,1,0:T(8,128)(2,1)S(1)}, u32[]{:S(2)}, u32[]{:S(2)}) collective-permute-start(bf16[2,9,64,128]{3,2,1,0:T(8,128)(2,1)S(1)} %maximum_select_fusion.1.own_lo), channel_id=1, source_target_pairs={{0,32},{32,64},{64,96},{96,0},{1,33},{33,65},{65,97},{97,1},{2,34}... | collective-permute-start | bytes 884744 | tf_op jit(solution)/shard_map/ppermute | solution.py:385
  13.6 6.7 %collective-permute-start.4 = (bf16[2,9,64,128]{3,2,1,0:T(8,128)(2,1)S(1)}, bf16[2,9,64,128]{3,2,1,0:T(8,128)(2,1)S(1)}, u32[]{:S(2)}, u32[]{:S(2)}) collective-permute-start(bf16[2,9,64,128]{3,2,1,0:T(8,128)(2,1)S(1)} %maximum_select_fusion.2.own_hi), channel_id=1, source_target_pairs={{0,96},{32,0},{64,32},{96,64},{1,97},{33,1},{65,33},{97,65},{2,98}... | collective-permute-start | bytes 884744 | tf_op jit(solution)/shard_map/ppermute | solution.py:385
  15.1 11.4 %collective-permute-start.3 = (bf16[2,9,64,128]{3,2,1,0:T(8,128)(2,1)S(1)}, bf16[2,9,64,128]{3,2,1,0:T(8,128)(2,1)S(1)}, u32[]{:S(2)}, u32[]{:S(2)}) collective-permute-start(bf16[2,9,64,128]{3,2,1,0:T(8,128)(2,1)S(1)} %maximum_select_fusion.1.own_lo), channel_id=1, source_target_pairs={{0,96},{32,0},{64,32},{96,64},{1,97},{33,1},{65,33},{97,65},{2,98}... | collective-permute-start | bytes 884744 | tf_op jit(solution)/shard_map/ppermute | solution.py:385
  16.6 10.3 %collective-permute-start.2 = (bf16[2,9,64,128]{3,2,1,0:T(8,128)(2,1)S(1)}, bf16[2,9,64,128]{3,2,1,0:T(8,128)(2,1)S(1)}, u32[]{:S(2)}, u32[]{:S(2)}) collective-permute-start(bf16[2,9,64,128]{3,2,1,0:T(8,128)(2,1)S(1)} %maximum_select_fusion.2.own_hi), channel_id=1, source_target_pairs={{0,32},{32,64},{64,96},{96,0},{1,33},{33,65},{65,97},{97,1},{2,34}... | collective-permute-start | bytes 884744 | tf_op jit(solution)/shard_map/ppermute | solution.py:385
  20.3 12.9 %collective-permute-start.5 = (bf16[2,9,64,128]{3,2,1,0:T(8,128)(2,1)S(1)}, bf16[2,9,64,128]{3,2,1,0:T(8,128)(2,1)S(1)}, u32[]{:S(2)}, u32[]{:S(2)}) collective-permute-start(bf16[2,9,64,128]{3,2,1,0:T(8,128)(2,1)S(1)} %collective-permute-done.1.left_lo), channel_id=1, source_target_pairs={{0,32},{32,64},{64,96},{96,0},{1,33},{33,65},{65,97},{97,1},{2,34}... | collective-permute-start | bytes 884744 | tf_op jit(solution)/shard_map/ppermute | solution.py:385
  20.3 12.9 %collective-permute-start.6 = (bf16[2,9,64,128]{3,2,1,0:T(8,128)(2,1)S(1)}, bf16[2,9,64,128]{3,2,1,0:T(8,128)(2,1)S(1)}, u32[]{:S(2)}, u32[]{:S(2)}) collective-permute-start(bf16[2,9,64,128]{3,2,1,0:T(8,128)(2,1)S(1)} %collective-permute-done.4.right_hi), channel_id=1, source_target_pairs={{0,96},{32,0},{64,32},{96,64},{1,97},{33,1},{65,33},{97,65},{2,98}... | collective-permute-start | bytes 884744 | tf_op jit(solution)/shard_map/ppermute | solution.py:385
  33.8 18.3 %collective-permute-start.8 = (bf16[4,9,64,128]{3,2,1,0:T(8,128)(2,1)S(1)}, bf16[4,9,64,128]{3,2,1,0:T(8,128)(2,1)S(1)}, u32[]{:S(2)}, u32[]{:S(2)}) collective-permute-start(bf16[4,9,64,128]{3,2,1,0:T(8,128)(2,1)S(1)} %get-tuple-element.40), channel_id=1, source_target_pairs={{0,1},{1,2},{2,3},{3,4},{4,5},{5,6},{6,7},{7,8},{8,9},{9,10},{10,1... | collective-permute-start | bytes 1769480 | tf_op jit(solution)/shard_map/ppermute | solution.py:388
  39.4 15.2 %collective-permute-start.9 = (bf16[4,9,64,128]{3,2,1,0:T(8,128)(2,1)S(1)}, bf16[4,9,64,128]{3,2,1,0:T(8,128)(2,1)S(1)}, u32[]{:S(2)}, u32[]{:S(2)}) collective-permute-start(bf16[4,9,64,128]{3,2,1,0:T(8,128)(2,1)S(1)} %get-tuple-element.41), channel_id=1, source_target_pairs={{1,0},{2,1},{3,2},{4,3},{5,4},{6,5},{7,6},{8,7},{9,8},{10,9},{11,1... | collective-permute-start | bytes 1769480 | tf_op jit(solution)/shard_map/ppermute | solution.py:391
  58.4 0.7 copy-start.6
  59.1 5.5 %copy-start.3 = (bf16[4,8,32,128]{3,2,1,0:T(8,128)(2,1)}, bf16[4,8,32,128]{3,2,1,0:T(8,128)(2,1)S(1)}, u32[]{:S(2)}) copy-start(bf16[4,8,32,128]{3,2,1,0:T(8,128)(2,1)S(1)} %get-tuple-element.48) | copy-start | bytes 786436
  64.6 14.6 %collective-permute-start.17 = (f32[2,448,256]{2,1,0:T(8,128)S(1)}, f32[2,448,256]{2,1,0:T(8,128)S(1)}, u32[]{:S(2)}, u32[]{:S(2)}) collective-permute-start(f32[2,448,256]{2,1,0:T(8,128)S(1)} %get-tuple-element.70), channel_id=1, source_target_pairs={{0,1},{1,0},{2,3},{3,2},{4,5},{5,4},{6,7},{7,6},{8,9},{9,8},{10,11... | collective-permute-start | bytes 2752520 | tf_op jit(solution)/shard_map/ppermute | solution.py:382
  64.7 9.5 %collective-permute-start.11 = (bf16[8,64,128]{2,1,0:T(8,128)(2,1)S(1)}, bf16[8,64,128]{2,1,0:T(8,128)(2,1)S(1)}, u32[]{:S(2)}, u32[]{:S(2)}) collective-permute-start(bf16[8,64,128]{2,1,0:T(8,128)(2,1)S(1)} %get-tuple-element.57), channel_id=1, source_target_pairs={{0,1},{1,2},{2,3},{3,4},{4,5},{5,6},{6,7},{7,8},{8,9},{9,10},{10,1... | collective-permute-start | bytes 393224 | tf_op jit(solution)/shard_map/ppermute | solution.py:388
  68.2 6.3 %collective-permute-start.12 = (bf16[8,64,128]{2,1,0:T(8,128)(2,1)S(1)}, bf16[8,64,128]{2,1,0:T(8,128)(2,1)S(1)}, u32[]{:S(2)}, u32[]{:S(2)}) collective-permute-start(bf16[8,64,128]{2,1,0:T(8,128)(2,1)S(1)} %get-tuple-element.58), channel_id=1, source_target_pairs={{1,0},{2,1},{3,2},{4,3},{5,4},{6,5},{7,6},{8,7},{9,8},{10,9},{11,1... | collective-permute-start | bytes 393224 | tf_op jit(solution)/shard_map/ppermute | solution.py:391
  79.2 1.4 %copy-start.5 = (bf16[4,9,64,128]{3,2,1,0:T(8,128)(2,1)}, bf16[4,9,64,128]{3,2,1,0:T(8,128)(2,1)S(1)}, u32[]{:S(2)}) copy-start(bf16[4,9,64,128]{3,2,1,0:T(8,128)(2,1)S(1)} %get-tuple-element.66) | copy-start | bytes 1769476
  80.6 16.5 %all-to-all-start = ((bf16[16,56,256]{2,1,0:T(8,128)(2,1)}), bf16[16,56,256]{2,1,0:T(8,128)(2,1)S(1)}, u32[]{:S(2)}, u32[]{:S(2)}) async-start(bf16[16,56,256]{2,1,0:T(8,128)(2,1)} %bitcast.3), calls=%async_computation | async-start | bytes 917504 | tf_op jit(solution)/shard_map/all_to_all | solution.py:480
  87.8 24.6 %collective-permute-start.14 = (bf16[4,9,64,128]{3,2,1,0:T(8,128)(2,1)}, bf16[4,9,64,128]{3,2,1,0:T(8,128)(2,1)S(1)}, u32[]{:S(2)}, u32[]{:S(2)}) collective-permute-start(bf16[4,9,64,128]{3,2,1,0:T(8,128)(2,1)} %get-tuple-element.65), channel_id=1, source_target_pairs={{0,64},{32,96},{64,0},{96,32},{1,65},{33,97},{65,1},{97,33},{2,66}... | collective-permute-start | bytes 1769480 | tf_op jit(solution)/shard_map/ppermute | solution.py:385
  90.5 26.3 %collective-permute-start.15 = (bf16[4,9,64,128]{3,2,1,0:T(8,128)(2,1)}, bf16[4,9,64,128]{3,2,1,0:T(8,128)(2,1)S(1)}, u32[]{:S(2)}, u32[]{:S(2)}) collective-permute-start(bf16[4,9,64,128]{3,2,1,0:T(8,128)(2,1)} %copy-done.5), channel_id=1, source_target_pairs={{0,96},{32,0},{64,32},{96,64},{1,97},{33,1},{65,33},{97,65},{2,98}... | collective-permute-start | bytes 1769480 | tf_op jit(solution)/shard_map/ppermute | solution.py:385
  91.6 26.0 %collective-permute-start.13 = (bf16[4,9,64,128]{3,2,1,0:T(8,128)(2,1)S(1)}, bf16[4,9,64,128]{3,2,1,0:T(8,128)(2,1)}, u32[]{:S(2)}, u32[]{:S(2)}) collective-permute-start(bf16[4,9,64,128]{3,2,1,0:T(8,128)(2,1)S(1)} %get-tuple-element.64.first.second.third), channel_id=1, source_target_pairs={{0,32},{32,64},{64,96},{96,0},{1,33},{33,65},{65,97},{97,1},{2,34}... | collective-permute-start | bytes 1769480 | tf_op jit(solution)/shard_map/ppermute | solution.py:385
  97.7 24.1 %copy-start.4 = (bf16[4,8,32,128]{3,2,1,0:T(8,128)(2,1)S(1)}, bf16[4,8,32,128]{3,2,1,0:T(8,128)(2,1)}, u32[]{:S(2)}) copy-start(bf16[4,8,32,128]{3,2,1,0:T(8,128)(2,1)} %copy-done.3) | copy-start | bytes 786436
  108.7 14.0 %collective-permute-start.18 = (f32[448,256]{1,0:T(8,128)S(1)}, f32[448,256]{1,0:T(8,128)S(1)}, u32[]{:S(2)}, u32[]{:S(2)}) collective-permute-start(f32[448,256]{1,0:T(8,128)S(1)} %bitcast.5), channel_id=1, source_target_pairs={{0,1},{1,0},{2,3},{3,2},{4,5},{5,4},{6,7},{7,6},{8,9},{9,8},{10,11... | collective-permute-start | bytes 1376264 | tf_op jit(solution)/shard_map/ppermute | solution.py:382
  111.4 10.5 %collective-permute-start.10 = (bf16[4,8,32,128]{3,2,1,0:T(8,128)(2,1)}, bf16[4,8,32,128]{3,2,1,0:T(8,128)(2,1)S(1)}, u32[]{:S(2)}, u32[]{:S(2)}) collective-permute-start(bf16[4,8,32,128]{3,2,1,0:T(8,128)(2,1)} %copy-done.6), channel_id=1, source_target_pairs={{0,16},{16,0},{1,17},{17,1},{2,18},{18,2},{3,19},{19,3},{4,20},{20... | collective-permute-start | bytes 786440 | tf_op jit(solution)/shard_map/ppermute | solution.py:379
  119.0 9.4 %collective-permute-start.16 = (bf16[4,9,32,128]{3,2,1,0:T(8,128)(2,1)S(1)}, bf16[4,9,32,128]{3,2,1,0:T(8,128)(2,1)S(1)}, u32[]{:S(2)}, u32[]{:S(2)}) collective-permute-start(bf16[4,9,32,128]{3,2,1,0:T(8,128)(2,1)S(1)} %get-tuple-element.69), channel_id=1, source_target_pairs={{0,16},{16,0},{1,17},{17,1},{2,18},{18,2},{3,19},{19,3},{4,20},{20... | collective-permute-start | bytes 884744 | tf_op jit(solution)/shard_map/ppermute | solution.py:379
  128.4 1.2 copy-start
